TPU v7x, 512 devices: a whole 4x8x8 slice. The times are simulated.
512 devices in a mesh: site: 16 (over z, core), dev: 32 (over y, x).
Axes of the slice: x: 4, y: 8, z: 8, core: 2. Of those that a mesh axis runs over, the one named last changes fastest.
Arguments:
- tokens: bfloat16 [16, 4096, 8192], P('site', 'dev'), may hold values from -6 to 6
- cotangent: bfloat16 [16, 4096, 256], P('site', 'dev'), may hold values from -0.119628906 to 0.119628906
- weight: bfloat16 [256, 8192], P('dev'), may hold values from -0.0625 to 0.0625
- momentum: float32 [16, 256, 8192], P('site', 'dev'), may hold values from -6 to 6
- kept_index: int32 [16, 256, 128, 16], P(None, 'dev'), may hold values from 0 to 63, all different within a row
Outputs:
- scores: bfloat16 [16, 4096, 256], P('site', 'dev')
- momentum_out: float32 [16, 256, 8192], P('site', 'dev')
Inputs may be any that keep to these rules, and one draw needn't show every extreme that they name: `kept_index`: the 16 indices of one block and site are all different.
All inputs are finite; a program needn't handle non-finite values.
Results may differ from a plain program's by a relative error of at most 0.022.
Values may be sent and summed in bfloat16 or wider, within the bound.
No kernel may reach another device: no remote copies, remote signals or barrier semaphores. Data moves between devices by JAX's collectives and lax.ppermute only.
A program may use at most 64 MiB of HBM per device.

v0:
```python
import jax
import jax.numpy as jnp
from jax import lax
from jax.sharding import PartitionSpec as P

momentum_decay = 0.999
step_size = 0.01


def pair_table():
    lanes = jnp.arange(128)
    freq = (lanes % 64)[:, None].astype(jnp.float32)
    place = (lanes % 64)[None, :].astype(jnp.float32)
    factor = jnp.where(freq == 0.0, jnp.sqrt(1.0 / 64.0), jnp.sqrt(2.0 / 64.0)).astype(jnp.float32)
    same_half = ((lanes // 64)[:, None] == (lanes // 64)[None, :]).astype(jnp.float32)
    return factor * jnp.cos(jnp.pi * (2.0 * place + 1.0) * freq / 128.0) * same_half


def spread_index(block_index):
    row_count, block_count, kept = block_index.shape
    paired = block_index.reshape(row_count, block_count // 2, 2, kept)
    offsets = (jnp.arange(2) * 64)[None, None, :, None]
    return (paired + offsets).reshape(row_count, block_count // 2, 2 * kept)


def shards(tokens, cotangent, weight, momentum, kept_index):
    local_tokens = tokens[0]
    local_cotan = cotangent[0]
    row_total = weight.shape[0]
    grad = lax.psum_scatter(
        lax.dot_general(
            local_cotan, local_tokens, (((0,), (0,)), ((), ())), preferred_element_type=jnp.float32
        ).astype(jnp.bfloat16),
        "dev",
        scatter_dimension=0,
        tiled=True,
    ).astype(jnp.float32)
    width = grad.shape[1]
    table = pair_table()
    lane_iota = jnp.arange(128)
    raised = momentum_decay * momentum[0] + grad
    coefs = jnp.dot(raised.reshape(-1, 128), table.T, precision=lax.Precision.HIGHEST)
    coefs = coefs.reshape(row_total, width // 128, 128)
    site_number = lax.axis_index("site")
    own_index = lax.dynamic_index_in_dim(kept_index, site_number, 0, keepdims=False)
    own_lanes = spread_index(own_index)
    keep_mask = jnp.any(own_lanes[..., None] == lane_iota, axis=2).astype(jnp.float32)
    picked = coefs * keep_mask
    reverted = jnp.dot(picked.reshape(-1, 128), table, precision=lax.Precision.HIGHEST)
    momentum_new = raised - reverted.reshape(row_total, width)
    matches = own_lanes[..., None] == lane_iota
    kept_values = jnp.sum(jnp.where(matches, coefs[:, :, None, :], 0.0), axis=3).astype(
        jnp.bfloat16
    )
    gathered = lax.all_gather(kept_values.reshape(1, row_total, -1), "site", axis=0, tiled=True)
    site_total = gathered.shape[0]

    def add_site(site_step, running):
        lanes_here = spread_index(kept_index[site_step])
        values_here = gathered[site_step].reshape(lanes_here.shape).astype(jnp.float32)
        placed = jnp.where(lanes_here[..., None] == lane_iota, values_here[..., None], 0.0)
        return running + jnp.sum(placed, axis=2)

    total = lax.fori_loop(0, site_total, add_site, jnp.zeros(coefs.shape, jnp.float32))
    decoded = jnp.dot(total.reshape(-1, 128), table, precision=lax.Precision.HIGHEST)
    decoded = decoded.reshape(row_total, width)
    new_weight = (weight.astype(jnp.float32) - step_size * decoded).astype(jnp.bfloat16)
    scores = lax.dot_general(
        local_tokens,
        lax.all_gather(new_weight, "dev", axis=0, tiled=True),
        (((1,), (1,)), ((), ())),
        preferred_element_type=jnp.float32,
    ).astype(jnp.bfloat16)
    return (scores[None], momentum_new[None])


def solution(mesh):
    placed = (
        P("site", "dev", None),
        P("site", "dev", None),
        P("dev", None),
        P("site", "dev", None),
        P(None, "dev", None, None),
    )
    return jax.shard_map(
        shards,
        mesh=mesh,
        in_specs=placed,
        out_specs=(P("site", "dev", None), P("site", "dev", None)),
        check_vma=False,
    )
```

profile of v0, /device:TPU:1, one launch (start us, length us, event | category | flops | bytes accessed | tf_op | source)
XLA Modules:
  0.0 495.5 jit_solution(15137741454141894746)
XLA Ops:
  7.2 1.5 copy-done
  8.8 4.0 convolution_convert_fusion
  12.9 0.8 constant_dynamic-slice_fusion.1
  14.3 226.3 %reduce-scatter.2.cloned.1.call-done = bf16[8,8192]{1,0:T(8,128)(2,1)} async-done(((bf16[256,8192]{1,0:T(8,128)(2,1)}), bf16[8,8192]{1,0:T(8,128)(2,1)}) %reduce-scatter.2.cloned.1.call-update) | async-done | bytes 131088 | tf_op jit(solution)/shard_map/reduce_scatter | solution.py:30
  240.6 0.9 bitcast_add_fusion
  242.3 0.7 copy-done.2
  243.0 5.1 %select_reduce_fusion.1 = bf16[8,64,32]{2,1,0:T(8,128)(2,1)S(1)} fusion(f32[8,64,128]{2,1,0:T(8,128)S(1)} %bitcast.31, s32[8,64,32]{2,1,0:T(8,128)S(1)} %broadcast_add_fusion.1), kind=kLoop, calls=%fused_computation.9 | loop fusion | flops 6275072 | bytes 360448 | tf_op jit(solution)/shard_map/reduce_sum | solution.py:52
  248.3 25.8 %all_gather.6 = bf16[16,8,2048]{2,1,0:T(8,128)(2,1)} all-gather(bf16[1,8,2048]{2,1,0:T(8,128)(2,1)S(1)} %convert_element_type.73), channel_id=1, replica_groups=mesh['site'=16,'dev'=32] {'site'}, dimensions={0}, use_global_device_ids=true | all-gather | bytes 557056 | tf_op jit(solution)/shard_map/all_gather | solution.py:55
  274.0 129.3 %while.14 = (s32[]{:T(128)}, f32[8,64,128]{2,1,0:T(8,128)S(1)}, s32[16,8,128,16]{2,3,1,0:T(8,128)}, bf16[16,8,2048]{2,1,0:T(8,128)(2,1)}, s32[]{:T(128)}, /*index=5*/s32[]{:T(128)}) while((s32[]{:T(128)}, f32[8,64,128]{2,1,0:T(8,128)S(1)}, s32[16,8,128,16]{2,3,1,0:T(8,128)}, bf16[16,8,2048]{2,1,0:T(8,128)(2,1)}, s32[]{:T(128)}, ...), condition=%wide.region_4.5_spmd.clone, body=%wide.region_2.4_spmd.clone.sunk | while | flops 6389765 | bytes 1933927 | solution.py:64
  274.0 0.9 constant_dynamic-slice_fusion.3
  275.5 0.8 dynamic-slice_convert_fusion.2
  276.3 5.7 %select_reduce_fusion.3 = f32[8,64,128]{2,1,0:T(8,128)S(1)} fusion(f32[8,64,32]{2,1,0:T(8,128)S(1)} %reshape.142, s32[8,64,32]{2,1,0:T(8,128)S(1)} %broadcast_add_fusion.3), kind=kLoop, calls=%fused_computation.2.clone.1 | loop fusion | flops 6225920 | bytes 393216 | tf_op jit(solution)/shard_map/while/body/eval_jaxpr/reduce_sum | solution.py:62
  282.2 0.8 constant_dynamic-slice_fusion.3
  283.5 0.8 dynamic-slice_convert_fusion.2
  284.4 5.7 %select_reduce_fusion.3 = f32[8,64,128]{2,1,0:T(8,128)S(1)} fusion(f32[8,64,32]{2,1,0:T(8,128)S(1)} %reshape.142, s32[8,64,32]{2,1,0:T(8,128)S(1)} %broadcast_add_fusion.3), kind=kLoop, calls=%fused_computation.2.clone.1 | loop fusion | flops 6225920 | bytes 393216 | tf_op jit(solution)/shard_map/while/body/eval_jaxpr/reduce_sum | solution.py:62
  290.2 0.8 constant_dynamic-slice_fusion.3
  291.6 0.8 dynamic-slice_convert_fusion.2
  292.5 5.7 %select_reduce_fusion.3 = f32[8,64,128]{2,1,0:T(8,128)S(1)} fusion(f32[8,64,32]{2,1,0:T(8,128)S(1)} %reshape.142, s32[8,64,32]{2,1,0:T(8,128)S(1)} %broadcast_add_fusion.3), kind=kLoop, calls=%fused_computation.2.clone.1 | loop fusion | flops 6225920 | bytes 393216 | tf_op jit(solution)/shard_map/while/body/eval_jaxpr/reduce_sum | solution.py:62
  298.3 0.8 constant_dynamic-slice_fusion.3
  299.7 0.8 dynamic-slice_convert_fusion.2
  300.6 5.7 %select_reduce_fusion.3 = f32[8,64,128]{2,1,0:T(8,128)S(1)} fusion(f32[8,64,32]{2,1,0:T(8,128)S(1)} %reshape.142, s32[8,64,32]{2,1,0:T(8,128)S(1)} %broadcast_add_fusion.3), kind=kLoop, calls=%fused_computation.2.clone.1 | loop fusion | flops 6225920 | bytes 393216 | tf_op jit(solution)/shard_map/while/body/eval_jaxpr/reduce_sum | solution.py:62
  306.4 0.8 constant_dynamic-slice_fusion.3
  307.8 0.8 dynamic-slice_convert_fusion.2
  308.7 5.7 %select_reduce_fusion.3 = f32[8,64,128]{2,1,0:T(8,128)S(1)} fusion(f32[8,64,32]{2,1,0:T(8,128)S(1)} %reshape.142, s32[8,64,32]{2,1,0:T(8,128)S(1)} %broadcast_add_fusion.3), kind=kLoop, calls=%fused_computation.2.clone.1 | loop fusion | flops 6225920 | bytes 393216 | tf_op jit(solution)/shard_map/while/body/eval_jaxpr/reduce_sum | solution.py:62
  314.5 0.8 constant_dynamic-slice_fusion.3
  315.9 0.8 dynamic-slice_convert_fusion.2
  316.8 5.7 %select_reduce_fusion.3 = f32[8,64,128]{2,1,0:T(8,128)S(1)} fusion(f32[8,64,32]{2,1,0:T(8,128)S(1)} %reshape.142, s32[8,64,32]{2,1,0:T(8,128)S(1)} %broadcast_add_fusion.3), kind=kLoop, calls=%fused_computation.2.clone.1 | loop fusion | flops 6225920 | bytes 393216 | tf_op jit(solution)/shard_map/while/body/eval_jaxpr/reduce_sum | solution.py:62
  322.6 0.8 constant_dynamic-slice_fusion.3
  323.9 0.8 dynamic-slice_convert_fusion.2
  324.8 5.7 %select_reduce_fusion.3 = f32[8,64,128]{2,1,0:T(8,128)S(1)} fusion(f32[8,64,32]{2,1,0:T(8,128)S(1)} %reshape.142, s32[8,64,32]{2,1,0:T(8,128)S(1)} %broadcast_add_fusion.3), kind=kLoop, calls=%fused_computation.2.clone.1 | loop fusion | flops 6225920 | bytes 393216 | tf_op jit(solution)/shard_map/while/body/eval_jaxpr/reduce_sum | solution.py:62
  330.6 0.8 constant_dynamic-slice_fusion.3
  332.0 0.8 dynamic-slice_convert_fusion.2
  332.9 5.7 %select_reduce_fusion.3 = f32[8,64,128]{2,1,0:T(8,128)S(1)} fusion(f32[8,64,32]{2,1,0:T(8,128)S(1)} %reshape.142, s32[8,64,32]{2,1,0:T(8,128)S(1)} %broadcast_add_fusion.3), kind=kLoop, calls=%fused_computation.2.clone.1 | loop fusion | flops 6225920 | bytes 393216 | tf_op jit(solution)/shard_map/while/body/eval_jaxpr/reduce_sum | solution.py:62
  338.7 0.8 constant_dynamic-slice_fusion.3
  340.1 0.8 dynamic-slice_convert_fusion.2
  341.0 5.7 %select_reduce_fusion.3 = f32[8,64,128]{2,1,0:T(8,128)S(1)} fusion(f32[8,64,32]{2,1,0:T(8,128)S(1)} %reshape.142, s32[8,64,32]{2,1,0:T(8,128)S(1)} %broadcast_add_fusion.3), kind=kLoop, calls=%fused_computation.2.clone.1 | loop fusion | flops 6225920 | bytes 393216 | tf_op jit(solution)/shard_map/while/body/eval_jaxpr/reduce_sum | solution.py:62
  346.8 0.8 constant_dynamic-slice_fusion.3
  348.2 0.8 dynamic-slice_convert_fusion.2
  349.1 5.7 %select_reduce_fusion.3 = f32[8,64,128]{2,1,0:T(8,128)S(1)} fusion(f32[8,64,32]{2,1,0:T(8,128)S(1)} %reshape.142, s32[8,64,32]{2,1,0:T(8,128)S(1)} %broadcast_add_fusion.3), kind=kLoop, calls=%fused_computation.2.clone.1 | loop fusion | flops 6225920 | bytes 393216 | tf_op jit(solution)/shard_map/while/body/eval_jaxpr/reduce_sum | solution.py:62
  354.9 0.8 constant_dynamic-slice_fusion.3
  356.3 0.8 dynamic-slice_convert_fusion.2
  357.2 5.7 %select_reduce_fusion.3 = f32[8,64,128]{2,1,0:T(8,128)S(1)} fusion(f32[8,64,32]{2,1,0:T(8,128)S(1)} %reshape.142, s32[8,64,32]{2,1,0:T(8,128)S(1)} %broadcast_add_fusion.3), kind=kLoop, calls=%fused_computation.2.clone.1 | loop fusion | flops 6225920 | bytes 393216 | tf_op jit(solution)/shard_map/while/body/eval_jaxpr/reduce_sum | solution.py:62
  363.0 0.8 constant_dynamic-slice_fusion.3
  364.4 0.8 dynamic-slice_convert_fusion.2
  365.2 5.7 %select_reduce_fusion.3 = f32[8,64,128]{2,1,0:T(8,128)S(1)} fusion(f32[8,64,32]{2,1,0:T(8,128)S(1)} %reshape.142, s32[8,64,32]{2,1,0:T(8,128)S(1)} %broadcast_add_fusion.3), kind=kLoop, calls=%fused_computation.2.clone.1 | loop fusion | flops 6225920 | bytes 393216 | tf_op jit(solution)/shard_map/while/body/eval_jaxpr/reduce_sum | solution.py:62
  371.0 0.8 constant_dynamic-slice_fusion.3
  372.4 0.8 dynamic-slice_convert_fusion.2
  373.3 5.7 %select_reduce_fusion.3 = f32[8,64,128]{2,1,0:T(8,128)S(1)} fusion(f32[8,64,32]{2,1,0:T(8,128)S(1)} %reshape.142, s32[8,64,32]{2,1,0:T(8,128)S(1)} %broadcast_add_fusion.3), kind=kLoop, calls=%fused_computation.2.clone.1 | loop fusion | flops 6225920 | bytes 393216 | tf_op jit(solution)/shard_map/while/body/eval_jaxpr/reduce_sum | solution.py:62
  379.1 0.8 constant_dynamic-slice_fusion.3
  380.5 0.8 dynamic-slice_convert_fusion.2
  381.4 5.7 %select_reduce_fusion.3 = f32[8,64,128]{2,1,0:T(8,128)S(1)} fusion(f32[8,64,32]{2,1,0:T(8,128)S(1)} %reshape.142, s32[8,64,32]{2,1,0:T(8,128)S(1)} %broadcast_add_fusion.3), kind=kLoop, calls=%fused_computation.2.clone.1 | loop fusion | flops 6225920 | bytes 393216 | tf_op jit(solution)/shard_map/while/body/eval_jaxpr/reduce_sum | solution.py:62
  387.2 0.8 constant_dynamic-slice_fusion.3
  388.6 0.8 dynamic-slice_convert_fusion.2
  389.5 5.7 %select_reduce_fusion.3 = f32[8,64,128]{2,1,0:T(8,128)S(1)} fusion(f32[8,64,32]{2,1,0:T(8,128)S(1)} %reshape.142, s32[8,64,32]{2,1,0:T(8,128)S(1)} %broadcast_add_fusion.3), kind=kLoop, calls=%fused_computation.2.clone.1 | loop fusion | flops 6225920 | bytes 393216 | tf_op jit(solution)/shard_map/while/body/eval_jaxpr/reduce_sum | solution.py:62
  395.3 0.8 constant_dynamic-slice_fusion.3
  396.7 0.8 dynamic-slice_convert_fusion.2
  397.6 5.7 %select_reduce_fusion.3 = f32[8,64,128]{2,1,0:T(8,128)S(1)} fusion(f32[8,64,32]{2,1,0:T(8,128)S(1)} %reshape.142, s32[8,64,32]{2,1,0:T(8,128)S(1)} %broadcast_add_fusion.3), kind=kLoop, calls=%fused_computation.2.clone.1 | loop fusion | flops 6225920 | bytes 393216 | tf_op jit(solution)/shard_map/while/body/eval_jaxpr/reduce_sum | solution.py:62
  404.1 0.7 subtract_convert_fusion
  404.8 4.9 fusion.2
  409.7 1.6 fusion.12
  411.4 0.7 subtract_bitcast_fusion
  412.1 72.3 %all-gather.2.cloned.1.call-done = bf16[256,8192]{1,0:T(8,128)(2,1)} async-done(((bf16[8,8192]{1,0:T(8,128)(2,1)}), bf16[256,8192]{1,0:T(8,128)(2,1)}) %all-gather.2.cloned.1.call-update) | async-done | bytes 4194320 | tf_op jit(solution)/shard_map/all_gather | solution.py:70
  484.5 3.4 fusion.9
  487.9 0.7 copy.16
  (156 shorter events, 13.7 us)
Async XLA Ops:
  7.2 1.6 copy-start
  7.2 233.4 %reduce-scatter.2.cloned.1.call-start = ((), (), s32[]{:S(2)}) async-start(), calls=%async_computation.1 | async-start | bytes 4325376 | tf_op jit(solution)/shard_map/reduce_scatter | solution.py:30
  12.8 227.8 %copy-start.3 = (f32[1,8,8192]{2,1,0:T(8,128)S(1)}, f32[1,8,8192]{2,1,0:T(8,128)}, u32[]{:S(2)}) copy-start(f32[1,8,8192]{2,1,0:T(8,128)} %param.10) | copy-start | bytes 786436
  12.8 471.6 %all-gather.2.cloned.1.call-start = ((), (), s32[]{:S(2)}) async-start(), calls=%async_computation.2 | async-start | bytes 4325376 | tf_op jit(solution)/shard_map/all_gather | solution.py:70
  14.3 259.7 %copy-start.1 = (s32[8,64,32]{2,1,0:T(8,128)}, s32[8,64,32]{2,1,0:T(8,128)S(1)}, u32[]{:S(2)}) copy-start(s32[8,64,32]{2,1,0:T(8,128)S(1)} %broadcast_add_fusion.1) | copy-start | bytes 196612
  242.3 0.7 copy-start.2
  274.0 130.1 %copy-start.4 = (bf16[8,8192]{1,0:T(8,128)(2,1)S(1)}, bf16[8,8192]{1,0:T(8,128)(2,1)}, u32[]{:S(2)}) copy-start(bf16[8,8192]{1,0:T(8,128)(2,1)} %param.9) | copy-start | bytes 393220
Sparse Core Ops, SparseCore 0:
  13.0 227.5 reduce-scatter.1
  404.9 79.4 all-gather.1
where the time goes:
time: 500 us; the launch traced here: 495 us
  waiting for transfers between devices  299 us (60%)
  other arithmetic  118 us (24%)
  local copies, waits for them, and re-layouts  27.9 us (6%)
  blocking collectives  25.8 us (5%)
  between operations  14.2 us (3%)
  matrix products  10.4 us (2%)
    reduce_scatter x1, waiting for transfers between devices, shards(): lax.psum_scatter(lax.dot_general(local_cotan, local_tokens, (((0,), (0,))...  226 us
    reduce_sum x16, other arithmetic, add_site(): return running + jnp.sum(placed, axis=2)  91 us
    all_gather x1, waiting for transfers between devices, shards(): lax.all_gather(new_weight, 'dev', axis=0, tiled=True)  72.3 us
    all_gather x1, blocking collectives, shards(): lax.all_gather(kept_values.reshape(1, row_total, -1), 'site', axis=0, til...  25.8 us
    dynamic_slice x32, local copies, waits for them, and re-layouts, add_site(): lanes_here = spread_index(kept_index[site_step])  16.7 us
    convert_element_type x16, other arithmetic, add_site(): gathered[site_step].reshape(lanes_here.shape).astype(jnp.float32)  12.3 us
  transfers between devices with their start and end apart: 2, of which 2 were waited for; matrix products, arithmetic and copies ran while one was open for 2% of the time, Pallas kernels for 0%

commit v1 on v0

v1 whole, which is shorter than its diff:
```python
import numpy as np
import jax
import jax.numpy as jnp
from jax import lax
from jax.sharding import Mesh, PartitionSpec as P

momentum_decay = 0.999
step_size = 0.01
SITE = ("z", "core")
DEV = ("y", "x")


def pair_table():
    freq = np.arange(64)[:, None]
    place = np.arange(64)[None, :]
    factor = np.where(freq == 0, np.sqrt(1.0 / 64.0), np.sqrt(2.0 / 64.0))
    one = factor * np.cos(np.pi * (2.0 * place + 1.0) * freq / 128.0)
    return np.kron(np.eye(2), one).astype(np.float32)


def exact_dot(a, b):
    return jnp.dot(a, b, precision=lax.Precision.HIGHEST)


def shards(tokens, cotangent, weight, momentum, kept_index):
    nz, ncore, ny, nx = (lax.axis_size(name) for name in ("z", "core", "y", "x"))
    site = lax.axis_index(SITE)
    sites = nz * ncore
    _, tok, width = tokens.shape
    rows_all = cotangent.shape[2]
    rows = weight.shape[0]
    part = width // nx
    tiles = width // 128
    table = pair_table()

    sliced = tokens[0].reshape(tok, nx, part).transpose(1, 0, 2)
    cotans = jnp.broadcast_to(cotangent, (nx, tok, rows_all))
    joined = lax.all_to_all(jnp.concatenate([sliced, cotans], axis=2), "x", 0, 0, tiled=True)
    tok_x = joined[:, :, :part].reshape(nx * tok, part)
    cot_x = joined[:, :, part:].reshape(nx * tok, rows_all)

    own = lax.dynamic_index_in_dim(kept_index, site, 0, keepdims=False)
    own = own.reshape(rows, tiles, 2, -1) + jnp.array([0, 64], jnp.int32)[None, None, :, None]
    own = own.reshape(rows, tiles, -1).transpose(1, 0, 2)
    keep = jnp.any(own[..., None] == jnp.arange(128, dtype=jnp.int32), axis=2)
    keep = keep.astype(jnp.float32).reshape(tiles * rows, 128)

    partial = lax.dot_general(
        cot_x, tok_x, (((0,), (0,)), ((), ())), preferred_element_type=jnp.float32
    ).astype(jnp.bfloat16)
    terms = lax.all_to_all(partial.reshape(ny * nx, rows, part), DEV, 0, 0, tiled=True)
    grad = jnp.sum(terms.reshape(ny, nx, rows, part).astype(jnp.float32), axis=0)
    grad = grad.reshape(nx, rows, part // 128, 128).transpose(0, 2, 1, 3).reshape(tiles * rows, 128)
    moment = momentum[0].reshape(rows, tiles, 128).transpose(1, 0, 2).reshape(tiles * rows, 128)
    raised = momentum_decay * moment + grad
    picked = exact_dot(raised, table.T) * keep
    moment_new = raised - exact_dot(picked, table)
    moment_new = moment_new.reshape(tiles, rows, 128).transpose(1, 0, 2).reshape(1, rows, width)

    sent = picked.astype(jnp.bfloat16).reshape(nx, sites, rows, 128).transpose(1, 0, 2, 3)
    sent = lax.all_to_all(sent, SITE, 0, 0, tiled=True)
    total = jnp.sum(sent.astype(jnp.float32), axis=0).reshape(nx * rows, 128)
    decoded = exact_dot(total, table).reshape(nx, rows, 128)
    held = weight.reshape(rows, nx, sites, 128).transpose(2, 1, 0, 3)
    held = lax.dynamic_index_in_dim(held, site, 0, keepdims=False)
    fresh = (held.astype(jnp.float32) - step_size * decoded).astype(jnp.bfloat16)

    spread = jnp.broadcast_to(fresh[None], (nz, nx, rows, 128)).reshape(nz * nx, rows, 128)
    got = lax.all_to_all(spread, ("z", "x"), 0, 0, tiled=True)
    got = got.reshape(nz, nx * rows, 128).transpose(1, 0, 2).reshape(1, nx * rows, nz * 128)
    got = lax.all_to_all(jnp.broadcast_to(got, (ny, nx * rows, nz * 128)), "y", 0, 0, tiled=True)
    mine = got.reshape(rows_all, nz * 128)
    other = lax.ppermute(mine, "core", [(0, 1), (1, 0)])
    core = lax.axis_index("core")
    tok_pairs = tok_x.reshape(nx * tok, nz, ncore, 128)
    tok_mine = lax.dynamic_index_in_dim(tok_pairs, core, 2, keepdims=False).reshape(nx * tok, nz * 128)
    tok_other = lax.dynamic_index_in_dim(tok_pairs, 1 - core, 2, keepdims=False).reshape(nx * tok, nz * 128)
    across = (((1,), (1,)), ((), ()))
    scores = lax.dot_general(tok_mine, mine, across, preferred_element_type=jnp.float32)
    scores = scores + lax.dot_general(tok_other, other, across, preferred_element_type=jnp.float32)
    scores = lax.all_to_all(scores.reshape(nx, tok, rows_all), "x", 0, 0, tiled=True)
    scores = jnp.sum(scores, axis=0).astype(jnp.bfloat16)
    return (scores[None], moment_new)


def solution(mesh):
    grid = Mesh(mesh.devices.reshape(8, 2, 8, 4), ("z", "core", "y", "x"))
    placed = (
        P(SITE, DEV, None),
        P(SITE, DEV, None),
        P(DEV, None),
        P(SITE, DEV, None),
        P(None, DEV, None, None),
    )
    return jax.shard_map(
        shards,
        mesh=grid,
        in_specs=placed,
        out_specs=(P(SITE, DEV, None), P(SITE, DEV, None)),
        check_vma=False,
    )
```

time: 500 us -> 180 us (0.36)
  waiting for transfers between devices: 299 us -> 45.6 us
  other arithmetic: 118 us -> 6.21 us
  starting transfers between devices: 0.08 us -> 38 us
  blocking collectives: 25.8 us -> 42.8 us
  between operations: 14.2 us -> 0.9 us
  local copies, waits for them, and re-layouts: 27.9 us -> 34.9 us
    reduce_scatter x1 -> x0, waiting for transfers between devices: 226 us -> none  [shards(): lax.psum_scatter(lax.dot_general(local_cotan, local_tokens, (((0,), (0,))...]
    reduce_sum x17 -> x3, other arithmetic: 96.1 us -> 2.08 us  [the longest x1 1.39 us: shards(): jnp.sum(terms.reshape(ny, nx, rows, part).astype(jnp.float32), axis=0)]
    all_gather x1 -> x0, waiting for transfers between devices: 72.3 us -> none  [shards(): lax.all_gather(new_weight, 'dev', axis=0, tiled=True)]
    all_to_all x0 -> x4, waiting for transfers between devices: none -> 45.6 us  [the longest x1 17.8 us: shards(): lax.all_to_all(partial.reshape(ny * nx, rows, part), DEV, 0, 0, tiled=True)]
    all_to_all x0 -> x2, blocking collectives: none -> 42.8 us  [the longest x1 29.1 us: shards(): lax.all_to_all(jnp.concatenate([sliced, cotans], axis=2), 'x', 0, 0, tile...]
    all_to_all x0 -> x4, starting transfers between devices: none -> 33.6 us  [the longest x1 14.3 us: shards(): sent = lax.all_to_all(sent, SITE, 0, 0, tiled=True)]
    all_gather x1 -> x0, blocking collectives: 25.8 us -> none  [shards(): lax.all_gather(kept_values.reshape(1, row_total, -1), 'site', axis=0, til...]
    convert_element_type x18 -> x0, other arithmetic: 13 us -> none  [the longest x16 12.3 us: add_site(): gathered[site_step].reshape(lanes_here.shape).astype(jnp.float32)]
  transfers between devices with their start and end apart: 2 -> 5, of which waited for: 2 -> 4; matrix products, arithmetic and copies ran while one was open for 2% -> 18% of each run, Pallas kernels for 0% -> 0%
where the time goes in v1:
time: 180 us; the launch traced here: 179 us
  waiting for transfers between devices  45.6 us (25%)
  blocking collectives  42.8 us (24%)
  starting transfers between devices  38 us (21%)
  local copies, waits for them, and re-layouts  34.9 us (19%)
  matrix products  10.2 us (6%)
  other arithmetic  6.21 us (3%)
    all_to_all x1, blocking collectives, shards(): lax.all_to_all(jnp.concatenate([sliced, cotans], axis=2), 'x', 0, 0, tile...  29.1 us
    all_to_all x1, waiting for transfers between devices, shards(): lax.all_to_all(partial.reshape(ny * nx, rows, part), DEV, 0, 0, tiled=True)  17.8 us
    unnamed x24, local copies, waits for them, and re-layouts  16 us
    all_to_all x1, starting transfers between devices, shards(): sent = lax.all_to_all(sent, SITE, 0, 0, tiled=True)  14.3 us
    all_to_all x1, blocking collectives, shards(): got = lax.all_to_all(spread, ('z', 'x'), 0, 0, tiled=True)  13.7 us
    all_to_all x1, starting transfers between devices, shards(): lax.all_to_all(partial.reshape(ny * nx, rows, part), DEV, 0, 0, tiled=True)  11.7 us
    all_to_all x1, waiting for transfers between devices, shards(): lax.all_to_all(jnp.broadcast_to(got, (ny, nx * rows, nz * 128)), 'y', 0,...  11.1 us
    all_to_all x1, waiting for transfers between devices, shards(): lax.all_to_all(scores.reshape(nx, tok, rows_all), 'x', 0, 0, tiled=True)  8.5 us
  transfers between devices with their start and end apart: 5, of which 4 were waited for; matrix products, arithmetic and copies ran while one was open for 18% of the time, Pallas kernels for 0%

profile of v1, /device:TPU:1, one launch (start us, length us, event | category | flops | bytes accessed | tf_op | source)
XLA Modules:
  0.0 178.5 jit_solution(7248658891879326564)
XLA Ops:
  0.6 0.0 copy-start
  0.6 4.2 %copy.39 = bf16[1,128,8192]{1,2,0:T(8,128)(2,1)} copy(bf16[1,128,8192]{2,1,0:T(8,128)(2,1)} %param.8) | data formatting | bytes 4194304 | tf_op args[0]
  4.8 0.0 copy-start.7
  4.8 3.0 %copy.40 = bf16[128,4,2048]{2,0,1:T(8,128)(2,1)S(1)} copy(bf16[128,4,2048]{0,2,1:T(8,128)(2,1)} %bitcast.78) | data formatting | bytes 4194304 | tf_op jit(solution)/shard_map/reshape;squeeze | solution.py:36
  7.8 0.0 copy-done.7
  7.8 0.2 pad_maximum_fusion
  8.0 29.1 %all_to_all.30 = bf16[4,128,2304]{2,1,0:T(8,128)(2,1)S(1)} all-to-all(bf16[4,128,2304]{2,1,0:T(8,128)(2,1)S(1)} %pad_maximum_fusion), channel_id=1, replica_groups=mesh['z'=8,'core'=2,'y'=8,'x'=4] {'x'}, dimensions={0} | all-to-all | bytes 4718592 | tf_op jit(solution)/shard_map/all_to_all | solution.py:38
  37.1 1.8 fusion.2
  38.9 11.7 %all-to-all-start.1 = ((bf16[32,8,2048]{2,1,0:T(8,128)(2,1)}), bf16[32,8,2048]{2,1,0:T(8,128)(2,1)}, u32[]{:S(2)}, u32[]{:S(2)}) async-start(bf16[32,8,2048]{2,1,0:T(8,128)(2,1)} %fusion.2), calls=%async_computation.1 | async-start | bytes 2097152 | tf_op jit(solution)/shard_map/all_to_all | solution.py:51
  50.6 0.0 copy-done
  50.6 0.0 copy-start.9
  50.6 1.0 copy.43
  51.6 1.9 %reshape.85 = s32[8,64,32]{2,1,0:T(8,128)} reshape(s32[1,8,128,16]{3,2,1,0:T(8,128)} %copy.43) | data formatting | bytes 131072 | tf_op jit(solution)/shard_map/reshape | solution.py:43
  53.5 0.1 add.39
  53.6 0.1 add.40
  53.7 1.0 add_bitcast_fusion
  54.7 0.2 copy.44
  54.8 3.0 %fusion = pred[64,8,128]{2,1,0:T(8,128)(4,1)S(1)} fusion(s32[64,8,32]{2,1,0:T(8,128)S(1)} %copy.44), kind=kLoop, calls=%fused_computation.1 | loop fusion | flops 4128768 | bytes 131072 | tf_op jit(solution)/shard_map/reduce_or | solution.py:45
  57.8 17.8 %all-to-all-done.1 = bf16[32,8,2048]{2,1,0:T(8,128)(2,1)} async-done(((bf16[32,8,2048]{2,1,0:T(8,128)(2,1)}), bf16[32,8,2048]{2,1,0:T(8,128)(2,1)}, u32[]{:S(2)}, u32[]{:S(2)}) %all-to-all-start.1) | async-done | bytes 1048608 | tf_op jit(solution)/shard_map/all_to_all | solution.py:51
  75.6 1.4 convert_reduce_fusion
  77.0 0.0 copy-start.3
  77.0 0.7 copy-done.3
  77.7 0.0 copy-done.9
  77.7 2.0 %fusion.9 = (bf16[512,128]{1,0:T(8,128)(2,1)S(1)}, f32[512,128]{1,0:T(8,128)}) fusion(f32[128,128]{1,0:T(8,128)S(1)} %copy-done.9, f32[512,128]{1,0:T(8,128)S(1)} %bitcast.81, f32[1,8,8192]{2,1,0:T(8,128)} %param.11, pred[64,8,128]{2,1,0:T(8,128)(4,1)S(1)} %fusion), kind=kOutput, calls=%fused_computation.28 | convolution fusion | flops 100925440 | bytes 1048576 | tf_op jit(solution)/shard_map/dot_general | solution.py:22
  79.7 0.7 copy.58
  80.4 14.3 %all-to-all-start.2 = ((bf16[16,4,8,128]{3,2,1,0:T(8,128)(2,1)}), bf16[16,4,8,128]{3,2,1,0:T(8,128)(2,1)S(1)}, u32[]{:S(2)}, u32[]{:S(2)}) async-start(bf16[16,4,8,128]{3,2,1,0:T(8,128)(2,1)} %bitcast.83), calls=%async_computation.2 | async-start | bytes 262144 | tf_op jit(solution)/shard_map/all_to_all | solution.py:61
  94.7 0.9 copy.54
  95.6 8.2 %all-to-all-done.2 = bf16[16,4,8,128]{3,2,1,0:T(8,128)(2,1)S(1)} async-done(((bf16[16,4,8,128]{3,2,1,0:T(8,128)(2,1)}), bf16[16,4,8,128]{3,2,1,0:T(8,128)(2,1)S(1)}, u32[]{:S(2)}, u32[]{:S(2)}) %all-to-all-start.2) | async-done | bytes 131104 | tf_op jit(solution)/shard_map/all_to_all | solution.py:61
  103.9 1.0 fusion.5
  104.9 13.7 %all_to_all.31 = bf16[32,8,128]{2,1,0:T(8,128)(2,1)S(1)} all-to-all(bf16[32,8,128]{2,1,0:T(8,128)(2,1)S(1)} %bitcast.86), channel_id=1, replica_groups=mesh['z'=8,'core'=2,'y'=8,'x'=4] {'z','x'}, dimensions={0} | all-to-all | bytes 131072 | tf_op jit(solution)/shard_map/all_to_all | solution.py:69
  118.6 0.9 broadcast_in_dim.28
  119.5 4.1 %all-to-all-start.4 = ((bf16[8,32,1024]{2,1,0:T(8,128)(2,1)}), bf16[8,32,1024]{2,1,0:T(8,128)(2,1)}, u32[]{:S(2)}, u32[]{:S(2)}) async-start(bf16[8,32,1024]{2,1,0:T(8,128)(2,1)} %broadcast_in_dim.28), calls=%async_computation.4 | async-start | bytes 1048576 | tf_op jit(solution)/shard_map/all_to_all | solution.py:71
  123.6 1.6 slice.8
  125.3 3.2 %reshape_reshape.3 = bf16[512,8,2,128]{3,2,1,0:T(2,128)(2,1)S(1)} reshape(bf16[4,128,2048]{2,1,0:T(8,128)(2,1)} %slice.8) | data formatting | bytes 4194304 | tf_op jit(solution)/shard_map/reshape;reshape | solution.py:75
  128.5 11.1 %all-to-all-done.4 = bf16[8,32,1024]{2,1,0:T(8,128)(2,1)} async-done(((bf16[8,32,1024]{2,1,0:T(8,128)(2,1)}), bf16[8,32,1024]{2,1,0:T(8,128)(2,1)}, u32[]{:S(2)}, u32[]{:S(2)}) %all-to-all-start.4) | async-done | bytes 524320 | tf_op jit(solution)/shard_map/all_to_all | solution.py:71
  139.6 4.4 %collective-permute-start = (bf16[256,1024]{1,0:T(8,128)(2,1)}, bf16[256,1024]{1,0:T(8,128)(2,1)}, u32[]{:S(2)}, u32[]{:S(2)}) collective-permute-start(bf16[256,1024]{1,0:T(8,128)(2,1)} %bitcast.23), channel_id=1, source_target_pairs={{0,32},{32,0},{1,33},{33,1},{2,34},{34,2},{3,35},{35,3},{4,36},{36... | collective-permute-start | bytes 1572872 | tf_op jit(solution)/shard_map/ppermute | solution.py:73
  144.0 6.3 %constant_dynamic-slice_fusion = (bf16[512,8,1,128]{3,2,1,0:T(2,128)(2,1)}, bf16[512,8,1,128]{3,2,1,0:T(2,128)(2,1)}) fusion(bf16[512,8,2,128]{3,2,1,0:T(2,128)(2,1)S(1)} %reshape_reshape.3, s32[]{:T(128)S(6)} %select_n.15, s32[]{:T(128)S(6)} %select_n.13), kind=kLoop, calls=%fused_computation.21 | loop fusion | bytes 4194312 | tf_op jit(solution)/shard_map/jit(dynamic_index_in_dim)/dynamic_slice | solution.py:77
  150.3 0.0 copy-start.1
  150.3 5.9 %copy.50 = bf16[512,8,1,128]{0,3,1,2:T(8,128)(2,1)} copy(bf16[512,8,1,128]{3,2,1,0:T(2,128)(2,1)} %get-tuple-element.3) | data formatting | bytes 2097152
  156.2 0.0 copy-done.1
  156.2 4.2 %copy.52 = bf16[512,8,1,128]{0,3,1,2:T(8,128)(2,1)} copy(bf16[512,8,1,128]{3,2,1,0:T(2,128)(2,1)S(1)} %copy-done.1) | data formatting | bytes 2097152
  160.4 0.0 copy-start.2
  160.4 1.9 %fusion.10 = f32[512,256]{1,0:T(8,128)S(1)} fusion(bf16[512,1024]{0,1:T(8,128)(2,1)} %bitcast.80, bf16[256,1024]{1,0:T(8,128)(2,1)} %bitcast.23), kind=kOutput, calls=%fused_computation.29 | convolution fusion | flops 268435456 | bytes 2097152 | tf_op jit(solution)/shard_map/dot_general | solution.py:79
  162.3 0.0 copy-start.4
  162.3 0.0 copy-start.5
  162.3 0.0 copy-start.6
  162.4 0.0 copy-start.8
  162.4 0.0 collective-permute-done
  162.4 0.0 copy-done.2
  162.4 2.4 %convolution_add_fusion = f32[512,256]{1,0:T(8,128)} fusion(f32[512,256]{1,0:T(8,128)S(1)} %fusion.10, bf16[512,1024]{0,1:T(8,128)(2,1)S(1)} %bitcast.79, bf16[256,1024]{1,0:T(8,128)(2,1)} %collective-permute-done), kind=kOutput, calls=%fused_computation.7 | convolution fusion | flops 268566528 | bytes 2621440 | tf_op jit(solution)/shard_map/dot_general | solution.py:80
  164.8 3.5 %all-to-all-start.5 = ((f32[4,128,256]{2,1,0:T(8,128)}), f32[4,128,256]{2,1,0:T(8,128)S(1)}, u32[]{:S(2)}, u32[]{:S(2)}) async-start(f32[4,128,256]{2,1,0:T(8,128)} %bitcast.25), calls=%async_computation.5 | async-start | bytes 1048576 | tf_op jit(solution)/shard_map/all_to_all | solution.py:81
  168.3 0.0 copy-done.4
  168.3 0.0 copy-done.5
  168.3 0.0 copy-done.6
  168.3 0.0 copy-done.8
  168.3 1.1 fusion.3
  169.4 8.5 %all-to-all-done.5 = f32[4,128,256]{2,1,0:T(8,128)S(1)} async-done(((f32[4,128,256]{2,1,0:T(8,128)}), f32[4,128,256]{2,1,0:T(8,128)S(1)}, u32[]{:S(2)}, u32[]{:S(2)}) %all-to-all-start.5) | async-done | bytes 524320 | tf_op jit(solution)/shard_map/all_to_all | solution.py:81
  177.9 0.7 reduce_sum.29
  (7 shorter events, 0.1 us)
Async XLA Ops:
  0.6 50.0 %copy-start = (s32[16,8,128,16]{2,3,1,0:T(8,128)S(1)}, s32[16,8,128,16]{2,3,1,0:T(8,128)}, u32[]{:S(2)}) copy-start(s32[16,8,128,16]{2,3,1,0:T(8,128)} %param.12) | copy-start | bytes 3145732
  4.8 3.0 %copy-start.7 = (bf16[1,128,256]{2,1,0:T(8,128)(2,1)S(1)}, bf16[1,128,256]{2,1,0:T(8,128)(2,1)}, u32[]{:S(2)}) copy-start(bf16[1,128,256]{2,1,0:T(8,128)(2,1)} %param.9) | copy-start | bytes 196612
  38.9 36.8 %all-to-all-start.1 = ((bf16[32,8,2048]{2,1,0:T(8,128)(2,1)}), bf16[32,8,2048]{2,1,0:T(8,128)(2,1)}, u32[]{:S(2)}, u32[]{:S(2)}) async-start(bf16[32,8,2048]{2,1,0:T(8,128)(2,1)} %fusion.2), calls=%async_computation.1 | async-start | bytes 2097152 | tf_op jit(solution)/shard_map/all_to_all | solution.py:51
  50.6 27.1 %copy-start.9 = (f32[128,128]{1,0:T(8,128)S(1)}, f32[128,128]{1,0:T(8,128)}, u32[]{:S(2)}) copy-start(f32[128,128]{1,0:T(8,128)} %constant.51.clone) | copy-start | bytes 196612
  77.0 0.7 copy-start.3
  80.4 23.4 %all-to-all-start.2 = ((bf16[16,4,8,128]{3,2,1,0:T(8,128)(2,1)}), bf16[16,4,8,128]{3,2,1,0:T(8,128)(2,1)S(1)}, u32[]{:S(2)}, u32[]{:S(2)}) async-start(bf16[16,4,8,128]{3,2,1,0:T(8,128)(2,1)} %bitcast.83), calls=%async_computation.2 | async-start | bytes 262144 | tf_op jit(solution)/shard_map/all_to_all | solution.py:61
  119.5 20.1 %all-to-all-start.4 = ((bf16[8,32,1024]{2,1,0:T(8,128)(2,1)}), bf16[8,32,1024]{2,1,0:T(8,128)(2,1)}, u32[]{:S(2)}, u32[]{:S(2)}) async-start(bf16[8,32,1024]{2,1,0:T(8,128)(2,1)} %broadcast_in_dim.28), calls=%async_computation.4 | async-start | bytes 1048576 | tf_op jit(solution)/shard_map/all_to_all | solution.py:71
  139.6 22.8 %collective-permute-start = (bf16[256,1024]{1,0:T(8,128)(2,1)}, bf16[256,1024]{1,0:T(8,128)(2,1)}, u32[]{:S(2)}, u32[]{:S(2)}) collective-permute-start(bf16[256,1024]{1,0:T(8,128)(2,1)} %bitcast.23), channel_id=1, source_target_pairs={{0,32},{32,0},{1,33},{33,1},{2,34},{34,2},{3,35},{35,3},{4,36},{36... | collective-permute-start | bytes 1572872 | tf_op jit(solution)/shard_map/ppermute | solution.py:73
  150.3 6.0 %copy-start.1 = (bf16[512,8,1,128]{3,2,1,0:T(2,128)(2,1)S(1)}, bf16[512,8,1,128]{3,2,1,0:T(2,128)(2,1)}, u32[]{:S(2)}) copy-start(bf16[512,8,1,128]{3,2,1,0:T(2,128)(2,1)} %get-tuple-element.2) | copy-start | bytes 3145732
  160.4 2.0 %copy-start.2 = (bf16[512,8,1,128]{0,3,1,2:T(8,128)(2,1)S(1)}, bf16[512,8,1,128]{0,3,1,2:T(8,128)(2,1)}, u32[]{:S(2)}) copy-start(bf16[512,8,1,128]{0,3,1,2:T(8,128)(2,1)} %copy.52) | copy-start | bytes 3145732
  162.3 5.9 %copy-start.4 = (f32[4,8,2048]{2,1,0:T(8,128)S(1)}, f32[4,8,2048]{2,1,0:T(8,128)}, u32[]{:S(2)}) copy-start(f32[4,8,2048]{2,1,0:T(8,128)} %copy-done.3) | copy-start | bytes 786436
  162.3 5.9 %copy-start.5 = (f32[1,8,8192]{2,1,0:T(8,128)S(1)}, f32[1,8,8192]{2,1,0:T(8,128)}, u32[]{:S(2)}) copy-start(f32[1,8,8192]{2,1,0:T(8,128)} %param.11) | copy-start | bytes 786436
  162.3 5.9 %copy-start.6 = (f32[512,128]{1,0:T(8,128)S(1)}, f32[512,128]{1,0:T(8,128)}, u32[]{:S(2)}) copy-start(f32[512,128]{1,0:T(8,128)} %get-tuple-element.5) | copy-start | bytes 786436
  162.4 5.9 %copy-start.8 = (f32[128,128]{1,0:T(8,128)S(1)}, f32[128,128]{1,0:T(8,128)}, u32[]{:S(2)}) copy-start(f32[128,128]{1,0:T(8,128)} %constant.52.clone) | copy-start | bytes 196612
  164.8 13.1 %all-to-all-start.5 = ((f32[4,128,256]{2,1,0:T(8,128)}), f32[4,128,256]{2,1,0:T(8,128)S(1)}, u32[]{:S(2)}, u32[]{:S(2)}) async-start(f32[4,128,256]{2,1,0:T(8,128)} %bitcast.25), calls=%async_computation.5 | async-start | bytes 1048576 | tf_op jit(solution)/shard_map/all_to_all | solution.py:81

commit v2 on v1

v2 whole, which is shorter than its diff:
```python
import numpy as np
import jax
import jax.numpy as jnp
from jax import lax
from jax.experimental import pallas as pl
from jax.experimental.pallas import tpu as pltpu
from jax.sharding import Mesh, PartitionSpec as P

momentum_decay = 0.999
step_size = 0.01
SITE = ("z", "core")
GROUP = ("yl", "x")
DEV = ("yh", "yl", "x")
VMEM_LIMIT = 48 * 1024 * 1024


def pair_table():
    freq = np.arange(64)[:, None]
    place = np.arange(64)[None, :]
    factor = np.where(freq == 0, np.sqrt(1.0 / 64.0), np.sqrt(2.0 / 64.0))
    one = factor * np.cos(np.pi * (2.0 * place + 1.0) * freq / 128.0)
    return np.kron(np.eye(2), one).astype(np.float32)


def exact_dot(a, b):
    return jnp.dot(a, b, precision=lax.Precision.HIGHEST, preferred_element_type=jnp.float32)


def params():
    return pltpu.CompilerParams(vmem_limit_bytes=VMEM_LIMIT)


def pack(tokens, cotangent, groups):
    tok, width = tokens.shape
    part = width // groups
    rows_all = cotangent.shape[1]
    fold = part // rows_all
    extra = tok // fold

    def body(tok_ref, cot_ref, out_ref):
        out_ref[0, :tok, :] = tok_ref[...]
        for q in range(fold):
            out_ref[0, tok:, q * rows_all:(q + 1) * rows_all] = cot_ref[q * extra:(q + 1) * extra, :]

    return pl.pallas_call(
        body,
        grid=(groups,),
        in_specs=[
            pl.BlockSpec((tok, part), lambda g: (0, g)),
            pl.BlockSpec((tok, rows_all), lambda g: (0, 0)),
        ],
        out_specs=pl.BlockSpec((1, tok + extra, part), lambda g: (g, 0, 0)),
        out_shape=jax.ShapeDtypeStruct((groups, tok + extra, part), tokens.dtype),
        compiler_params=params(),
        name="pack",
    )(tokens, cotangent)


def gradient(joined, tok, rows_all):
    groups, high, part = joined.shape
    extra = high - tok
    fold = tok // extra
    cols = 256

    def body(tok_ref, cot_ref, out_ref):
        left = jnp.concatenate(
            [
                cot_ref[k, :, q * rows_all:(q + 1) * rows_all]
                for k in range(groups)
                for q in range(fold)
            ],
            axis=0,
        )
        right = tok_ref[...].reshape(groups * tok, cols)
        out_ref[...] = lax.dot_general(
            left, right, (((0,), (0,)), ((), ())), preferred_element_type=jnp.float32
        ).astype(out_ref.dtype)

    return pl.pallas_call(
        body,
        grid=(part // cols,),
        in_specs=[
            pl.BlockSpec((groups, tok, cols), lambda j: (0, 0, j)),
            pl.BlockSpec((groups, extra, part), lambda j: (0, tok // extra, 0)),
        ],
        out_specs=pl.BlockSpec((rows_all, cols), lambda j: (0, j)),
        out_shape=jax.ShapeDtypeStruct((rows_all, part), jnp.bfloat16),
        compiler_params=params(),
        name="gradient",
    )(joined, joined)


def raise_and_pick(terms, momentum, keep, table, groups, nz, ncore):
    rows, width = momentum.shape
    part = width // groups
    tiles = part // 128

    def body(terms_ref, mom_ref, keep_ref, table_ref, out_ref, sent_ref):
        pieces = []
        for g in range(groups):
            grad = terms_ref[g].astype(jnp.float32)
            for k in range(g + groups, terms_ref.shape[0], groups):
                grad = grad + terms_ref[k].astype(jnp.float32)
            raised = momentum_decay * mom_ref[:, g * part:(g + 1) * part] + grad
            pieces += [raised[:, t * 128:(t + 1) * 128] for t in range(tiles)]
        raised = jnp.concatenate(pieces, axis=0)
        both = table_ref[...]
        picked = exact_dot(raised, both.T) * keep_ref[...]
        moment_new = raised - exact_dot(picked, both)
        sent = picked.astype(jnp.bfloat16)
        for g in range(groups):
            for t in range(tiles):
                at = (g * tiles + t) * rows
                out_ref[:, g * part + t * 128:g * part + (t + 1) * 128] = moment_new[at:at + rows]
                for c in range(ncore):
                    sent_ref[t * ncore + c, g] = sent[at:at + rows]

    return pl.pallas_call(
        body,
        out_shape=(
            jax.ShapeDtypeStruct((rows, width), jnp.float32),
            jax.ShapeDtypeStruct((nz * ncore, groups, rows, 128), jnp.bfloat16),
        ),
        compiler_params=params(),
        name="raise_and_pick",
    )(terms, momentum, keep, table)


def update(sent, held, table, copies):
    sites, groups, rows, lanes = sent.shape

    def body(sent_ref, held_ref, table_ref, out_ref):
        total = sent_ref[0].astype(jnp.float32)
        for s in range(1, sites):
            total = total + sent_ref[s].astype(jnp.float32)
        decoded = exact_dot(total.reshape(groups * rows, lanes), table_ref[...])
        fresh = held_ref[...].astype(jnp.float32) - step_size * decoded.reshape(groups, rows, lanes)
        fresh = fresh.astype(jnp.bfloat16)
        for c in range(copies):
            out_ref[c] = fresh

    return pl.pallas_call(
        body,
        out_shape=jax.ShapeDtypeStruct((copies, groups, rows, lanes), jnp.bfloat16),
        compiler_params=params(),
        name="update",
    )(sent, held, table)


def project(joined, fresh, tok):
    groups, _, part = joined.shape
    tiles, rows_all, _ = fresh.shape

    def body(tok_ref, fresh_ref, out_ref):
        weight = jnp.concatenate([fresh_ref[t] for t in range(tiles)], axis=1)
        out_ref[0] = lax.dot_general(
            tok_ref[0], weight, (((1,), (1,)), ((), ())), preferred_element_type=jnp.float32
        ).astype(out_ref.dtype)

    return pl.pallas_call(
        body,
        grid=(groups,),
        in_specs=[
            pl.BlockSpec((1, tok, part), lambda g: (g, 0, 0)),
            pl.BlockSpec((tiles, rows_all, 128), lambda g: (0, 0, 0)),
        ],
        out_specs=pl.BlockSpec((1, tok, rows_all), lambda g: (g, 0, 0)),
        out_shape=jax.ShapeDtypeStruct((groups, tok, rows_all), jnp.bfloat16),
        compiler_params=params(),
        name="project",
    )(joined, fresh)


def exchange(value, axes):
    return lax.all_to_all(value, axes, 0, 0, tiled=True)


def shards(tokens, cotangent, weight, momentum, kept_index):
    nz, ncore, nyh, nyl, nx = (lax.axis_size(name) for name in ("z", "core", "yh", "yl", "x"))
    groups = nyl * nx
    site = lax.axis_index(SITE)
    _, tok, width = tokens.shape
    rows_all = cotangent.shape[2]
    rows = weight.shape[0]
    part = width // groups
    table = jnp.asarray(pair_table())

    joined = exchange(pack(tokens[0], cotangent[0], groups), GROUP)

    tiles = width // 128
    own = lax.dynamic_index_in_dim(kept_index, site, 0, keepdims=False)
    own = own.reshape(rows, tiles, 2, -1) + jnp.array([0, 64], jnp.int32)[None, None, :, None]
    own = own.reshape(rows, tiles, -1).transpose(1, 0, 2)
    keep = jnp.any(own[..., None] == jnp.arange(128, dtype=jnp.int32), axis=2)
    keep = keep.astype(jnp.float32).reshape(tiles * rows, 128)
    held = weight.reshape(rows, groups, part // 128, 128)
    held = lax.dynamic_index_in_dim(held, lax.axis_index("z"), 2, keepdims=False).transpose(1, 0, 2)

    partial = gradient(joined, tok, rows_all)
    terms = exchange(partial.reshape(nyh * groups, rows, part), DEV)
    moment_new, sent = raise_and_pick(terms, momentum[0], keep, table, groups, nz, ncore)

    fresh = update(exchange(sent, SITE), held, table, nz * nyh)
    fresh = exchange(fresh.reshape(nz * nyh * groups, rows, 128), ("z",) + DEV)
    scores = project(joined, fresh.reshape(nz, rows_all, 128), tok)
    scores = exchange(scores, GROUP)
    scores = jnp.sum(scores.astype(jnp.float32), axis=0).astype(jnp.bfloat16)
    return (scores[None], moment_new[None])


def solution(mesh):
    grid = Mesh(mesh.devices.reshape(8, 2, 4, 2, 4), ("z", "core", "yh", "yl", "x"))
    placed = (
        P(SITE, DEV, None),
        P(SITE, DEV, None),
        P(DEV, None),
        P(SITE, DEV, None),
        P(None, DEV, None, None),
    )
    return jax.shard_map(
        shards,
        mesh=grid,
        in_specs=placed,
        out_specs=(P(SITE, DEV, None), P(SITE, DEV, None)),
        check_vma=False,
    )
```

time: 180 us -> 139 us (0.77)
  blocking collectives: 42.8 us -> 73.3 us
  local copies, waits for them, and re-layouts: 34.9 us -> 5.65 us
  waiting for transfers between devices: 45.6 us -> 22 us
  starting transfers between devices: 38 us -> 24.6 us
  matrix products: 10.2 us -> 0 us
  Pallas kernels: 0 us -> 8 us
  other arithmetic: 6.21 us -> 3.73 us
    all_to_all x2 -> x3, blocking collectives: 42.8 us -> 73.3 us  [exchange(): return lax.all_to_all(value, axes, 0, 0, tiled=True)]
    all_to_all x4 -> x2, waiting for transfers between devices: 45.6 us -> 22 us  [exchange(): return lax.all_to_all(value, axes, 0, 0, tiled=True)]
    unnamed x24 -> x14, local copies, waits for them, and re-layouts: 16 us -> 4.27 us
    dot_general x6 -> x0, matrix products: 10.2 us -> none  [the longest x3 4.1 us: exact_dot(): return jnp.dot(a, b, precision=lax.Precision.HIGHEST)]
    all_to_all x4 -> x2, starting transfers between devices: 33.6 us -> 24.6 us  [exchange(): return lax.all_to_all(value, axes, 0, 0, tiled=True)]
    pallas_call x0 -> x5, Pallas kernels: none -> 8 us  [the longest x1 3 us: gradient(): pl.pallas_call(body, grid=(part // cols,), in_specs=[pl.BlockSpec((groups...]
    dynamic_slice x2 -> x0, local copies, waits for them, and re-layouts: 6.3 us -> none  [the longest x1 6.27 us: shards(): lax.dynamic_index_in_dim(tok_pairs, 1 - core, 2, keepdims=False)]
    another operation x2 -> x0, local copies, waits for them, and re-layouts: 6.19 us -> none  [the longest x1 3.22 us: shards(): tok_pairs = tok_x.reshape(nx * tok, nz, ncore, 128)]
  transfers between devices with their start and end apart: 5 -> 2, of which waited for: 4 -> 2; matrix products, arithmetic and copies ran while one was open for 18% -> 3% of each run, Pallas kernels for 0% -> 0%
where the time goes in v2:
time: 139 us; the launch traced here: 138 us
  blocking collectives  73.3 us (53%)
  starting transfers between devices  24.6 us (18%)
  waiting for transfers between devices  22 us (16%)
  Pallas kernels  8 us (6%)
  local copies, waits for them, and re-layouts  5.65 us (4%)
  other arithmetic  3.73 us (3%)
    all_to_all x3, blocking collectives, exchange(): return lax.all_to_all(value, axes, 0, 0, tiled=True)  73.3 us
    all_to_all x2, starting transfers between devices, exchange(): return lax.all_to_all(value, axes, 0, 0, tiled=True)  24.6 us
    all_to_all x2, waiting for transfers between devices, exchange(): return lax.all_to_all(value, axes, 0, 0, tiled=True)  22 us
    unnamed x14, local copies, waits for them, and re-layouts  4.27 us
    pallas_call x1, Pallas kernels, gradient(): pl.pallas_call(body, grid=(part // cols,), in_specs=[pl.BlockSpec((groups...  3 us
    reduce_or x1, other arithmetic, shards(): keep = jnp.any(own[..., None] == jnp.arange(128, dtype=jnp.int32), axis=2)  2.98 us
  transfers between devices with their start and end apart: 2, of which 2 were waited for; matrix products, arithmetic and copies ran while one was open for 3% of the time, Pallas kernels for 0%

profile of v2, /device:TPU:1, one launch (start us, length us, event | category | flops | bytes accessed | tf_op | source)
XLA Modules:
  0.0 137.9 jit_solution(3151026650454230621)
XLA Ops:
  0.6 0.0 copy-start
  0.6 0.0 copy-start.3
  0.7 1.7 %copy-done.3 = bf16[1,128,8192]{2,1,0:T(8,128)(2,1)S(1)} copy-done((bf16[1,128,8192]{2,1,0:T(8,128)(2,1)S(1)}, bf16[1,128,8192]{2,1,0:T(8,128)(2,1)}, u32[]{:S(2)}) %copy-start.3) | copy-done | bytes 2097176
  2.3 0.0 copy-start.6
  2.3 0.8 copy-done.6
  3.2 0.5 pack.1
  3.6 34.3 %all_to_all.25.tok_ref.cot_ref = bf16[8,160,1024]{2,1,0:T(8,128)(2,1)S(1)} all-to-all(bf16[8,160,1024]{2,1,0:T(8,128)(2,1)S(1)} %pack.1), channel_id=1, replica_groups=mesh['z'=8,'core'=2,'yh'=4,'yl'=2,'x'=4] {'yl','x'}, dimensions={0} | all-to-all | bytes 5242880 | tf_op jit(solution)/shard_map/all_to_all | solution.py:175
  37.9 0.0 copy-start.1
  37.9 3.0 %gradient.1 = bf16[256,1024]{1,0:T(8,128)(2,1)} custom-call(bf16[8,160,1024]{2,1,0:T(8,128)(2,1)S(1)} %all_to_all.25.tok_ref.cot_ref, bf16[8,160,1024]{2,1,0:T(8,128)(2,1)S(1)} %all_to_all.25.tok_ref.cot_ref), custom_call_target="tpu_custom_call" | custom-call | tf_op jit(solution)/shard_map/gradient/pallas_call | solution.py:79
  40.9 0.0 copy-done.1
  40.9 0.0 copy-start.4
  40.9 0.0 copy-start.5
  40.9 10.2 %all-to-all-start.1 = ((bf16[32,8,1024]{2,1,0:T(8,128)(2,1)}), bf16[32,8,1024]{2,1,0:T(8,128)(2,1)S(1)}, u32[]{:S(2)}, u32[]{:S(2)}) async-start(bf16[32,8,1024]{2,1,0:T(8,128)(2,1)} %bitcast.2), calls=%async_computation.1 | async-start | bytes 1048576 | tf_op jit(solution)/shard_map/all_to_all | solution.py:175
  51.1 0.0 copy-done
  51.1 0.2 copy.14
  51.3 0.1 reshape.30
  51.5 0.1 add.26
  51.6 0.1 add.27
  51.7 0.2 copy.15
  51.8 3.0 %fusion = pred[64,8,128]{2,1,0:T(8,128)(4,1)S(1)} fusion(s32[64,8,32]{2,1,0:T(8,128)S(1)} %copy.15), kind=kLoop, calls=%fused_computation.1 | loop fusion | flops 4128768 | bytes 131072 | tf_op jit(solution)/shard_map/reduce_or | solution.py:194
  54.9 11.0 %all-to-all-done.1.terms_ref = bf16[32,8,1024]{2,1,0:T(8,128)(2,1)S(1)} async-done(((bf16[32,8,1024]{2,1,0:T(8,128)(2,1)}), bf16[32,8,1024]{2,1,0:T(8,128)(2,1)S(1)}, u32[]{:S(2)}, u32[]{:S(2)}) %all-to-all-start.1) | async-done | bytes 524320 | tf_op jit(solution)/shard_map/all_to_all | solution.py:175
  65.8 0.0 copy-done.4
  65.8 0.0 copy-done.5
  65.8 1.8 %raise_and_pick.1 = (f32[8,8192]{1,0:T(8,128)}, bf16[16,8,8,128]{3,2,1,0:T(8,128)(2,1)}) custom-call(bf16[32,8,1024]{2,1,0:T(8,128)(2,1)S(1)} %all-to-all-done.1.terms_ref, f32[8,8192]{1,0:T(8,128)S(1)} %bitcast.24, f32[512,128]{1,0:T(8,128)S(1)} %convert_bitcast_fusion.keep_ref, f32[128,128]{1,0:T(8,128)S(1)} %copy-done.5), custom_call_target="tpu_custom_call" | custom-call | tf_op jit(solution)/shard_map/raise_and_pick/pallas_call | solution.py:118
  67.6 14.4 %all-to-all-start.2 = ((bf16[16,8,8,128]{3,2,1,0:T(8,128)(2,1)}), bf16[16,8,8,128]{3,2,1,0:T(8,128)(2,1)S(1)}, u32[]{:S(2)}, u32[]{:S(2)}) async-start(bf16[16,8,8,128]{3,2,1,0:T(8,128)(2,1)} %get-tuple-element.4), calls=%async_computation.2 | async-start | bytes 524288 | tf_op jit(solution)/shard_map/all_to_all | solution.py:175
  82.0 0.7 dynamic-slice_bitcast_fusion.held_ref
  82.7 11.0 %all-to-all-done.2.sent_ref = bf16[16,8,8,128]{3,2,1,0:T(8,128)(2,1)S(1)} async-done(((bf16[16,8,8,128]{3,2,1,0:T(8,128)(2,1)}), bf16[16,8,8,128]{3,2,1,0:T(8,128)(2,1)S(1)}, u32[]{:S(2)}, u32[]{:S(2)}) %all-to-all-start.2) | async-done | bytes 262176 | tf_op jit(solution)/shard_map/all_to_all | solution.py:175
  93.7 0.3 update.1
  94.0 27.1 %all_to_all.26 = bf16[256,8,128]{2,1,0:T(8,128)(2,1)S(1)} all-to-all(bf16[256,8,128]{2,1,0:T(8,128)(2,1)S(1)} %bitcast.23), channel_id=1, replica_groups=mesh['z'=8,'core'=2,'yh'=4,'yl'=2,'x'=4] {'z','yh','yl','x'}, dimensions={0} | all-to-all | bytes 1048576 | tf_op jit(solution)/shard_map/all_to_all | solution.py:175
  121.1 0.0 copy-start.2
  121.1 1.7 %copy-done.2 = bf16[8,160,1024]{2,1,0:T(8,128)(2,1)S(1)} copy-done((bf16[8,160,1024]{2,1,0:T(8,128)(2,1)S(1)}, bf16[8,160,1024]{2,1,0:T(8,128)(2,1)}, u32[]{:S(2)}) %copy-start.2) | copy-done | bytes 2621464
  122.8 2.5 %project.1 = bf16[8,128,256]{2,1,0:T(8,128)(2,1)S(1)} custom-call(bf16[8,160,1024]{2,1,0:T(8,128)(2,1)S(1)} %copy-done.2, bf16[8,256,128]{2,1,0:T(8,128)(2,1)S(1)} %bitcast.22), custom_call_target="tpu_custom_call" | custom-call | tf_op jit(solution)/shard_map/project/pallas_call | solution.py:160
  125.3 11.9 %all_to_all.27 = bf16[8,128,256]{2,1,0:T(8,128)(2,1)S(1)} all-to-all(bf16[8,128,256]{2,1,0:T(8,128)(2,1)S(1)} %project.1), channel_id=1, replica_groups=mesh['z'=8,'core'=2,'yh'=4,'yl'=2,'x'=4] {'yl','x'}, dimensions={0} | all-to-all | bytes 1048576 | tf_op jit(solution)/shard_map/all_to_all | solution.py:175
  137.2 0.7 reduce_sum.12
  (4 shorter events, 0.1 us)
Async XLA Ops:
  0.6 50.5 %copy-start = (s32[16,8,128,16]{2,3,1,0:T(8,128)S(1)}, s32[16,8,128,16]{2,3,1,0:T(8,128)}, u32[]{:S(2)}) copy-start(s32[16,8,128,16]{2,3,1,0:T(8,128)} %param.11) | copy-start | bytes 3145732
  0.6 1.7 %copy-start.3 = (bf16[1,128,8192]{2,1,0:T(8,128)(2,1)S(1)}, bf16[1,128,8192]{2,1,0:T(8,128)(2,1)}, u32[]{:S(2)}) copy-start(bf16[1,128,8192]{2,1,0:T(8,128)(2,1)} %param.7) | copy-start | bytes 6291460
  2.3 0.8 copy-start.6
  37.9 3.0 %copy-start.1 = (bf16[8,160,1024]{2,1,0:T(8,128)(2,1)}, bf16[8,160,1024]{2,1,0:T(8,128)(2,1)S(1)}, u32[]{:S(2)}) copy-start(bf16[8,160,1024]{2,1,0:T(8,128)(2,1)S(1)} %all_to_all.25.tok_ref.cot_ref) | copy-start | bytes 7864324
  40.9 24.9 %copy-start.4 = (f32[1,8,8192]{2,1,0:T(8,128)S(1)}, f32[1,8,8192]{2,1,0:T(8,128)}, u32[]{:S(2)}) copy-start(f32[1,8,8192]{2,1,0:T(8,128)} %param.10) | copy-start | bytes 786436
  40.9 24.9 %copy-start.5 = (f32[128,128]{1,0:T(8,128)S(1)}, f32[128,128]{1,0:T(8,128)}, u32[]{:S(2)}) copy-start(f32[128,128]{1,0:T(8,128)} %constant.35.clone.table_ref) | copy-start | bytes 196612
  40.9 24.9 %all-to-all-start.1 = ((bf16[32,8,1024]{2,1,0:T(8,128)(2,1)}), bf16[32,8,1024]{2,1,0:T(8,128)(2,1)S(1)}, u32[]{:S(2)}, u32[]{:S(2)}) async-start(bf16[32,8,1024]{2,1,0:T(8,128)(2,1)} %bitcast.2), calls=%async_computation.1 | async-start | bytes 1048576 | tf_op jit(solution)/shard_map/all_to_all | solution.py:175
  67.6 26.1 %all-to-all-start.2 = ((bf16[16,8,8,128]{3,2,1,0:T(8,128)(2,1)}), bf16[16,8,8,128]{3,2,1,0:T(8,128)(2,1)S(1)}, u32[]{:S(2)}, u32[]{:S(2)}) async-start(bf16[16,8,8,128]{3,2,1,0:T(8,128)(2,1)} %get-tuple-element.4), calls=%async_computation.2 | async-start | bytes 524288 | tf_op jit(solution)/shard_map/all_to_all | solution.py:175
  121.1 1.7 %copy-start.2 = (bf16[8,160,1024]{2,1,0:T(8,128)(2,1)S(1)}, bf16[8,160,1024]{2,1,0:T(8,128)(2,1)}, u32[]{:S(2)}) copy-start(bf16[8,160,1024]{2,1,0:T(8,128)(2,1)} %copy-done.1) | copy-start | bytes 7864324

commit v3 on v2

v3 whole, which is shorter than its diff:
```python
import numpy as np
import jax
import jax.numpy as jnp
from jax import lax
from jax.experimental import pallas as pl
from jax.experimental.pallas import tpu as pltpu
from jax.sharding import Mesh, PartitionSpec as P

momentum_decay = 0.999
step_size = 0.01
SITE = ("z", "core")
GROUP = ("yl", "x")
DEV = ("yh", "yl", "x")
MIB = 1024 * 1024
ACROSS = (((1,), (1,)), ((), ()))


def pair_table():
    freq = np.arange(64)[:, None]
    place = np.arange(64)[None, :]
    factor = np.where(freq == 0, np.sqrt(1.0 / 64.0), np.sqrt(2.0 / 64.0))
    one = factor * np.cos(np.pi * (2.0 * place + 1.0) * freq / 128.0)
    return np.kron(np.eye(2), one).astype(np.float32)


def exact_dot(a, b):
    return jnp.dot(a, b, precision=lax.Precision.HIGHEST, preferred_element_type=jnp.float32)


def params(mib=16):
    return pltpu.CompilerParams(vmem_limit_bytes=mib * MIB)


def pack(tokens, cotangent, groups):
    tok, width = tokens.shape
    part = width // groups
    rows_all = cotangent.shape[1]
    fold = part // rows_all
    extra = tok // fold

    def body(tok_ref, cot_ref, out_ref, sem):
        moves = [
            pltpu.make_async_copy(tok_ref.at[:, g * part:(g + 1) * part], out_ref.at[g, :tok, :], sem.at[g])
            for g in range(groups)
        ]
        for move in moves:
            move.start()
        for g in range(groups):
            for q in range(fold):
                out_ref[g, tok:, q * rows_all:(q + 1) * rows_all] = cot_ref[q * extra:(q + 1) * extra, :]
        for move in moves:
            move.wait()

    return pl.pallas_call(
        body,
        in_specs=[pl.BlockSpec(memory_space=pltpu.HBM), pl.BlockSpec(memory_space=pltpu.VMEM)],
        out_specs=pl.BlockSpec(memory_space=pltpu.VMEM),
        out_shape=jax.ShapeDtypeStruct((groups, tok + extra, part), tokens.dtype),
        scratch_shapes=[pltpu.SemaphoreType.DMA((groups,))],
        compiler_params=params(),
        name="pack",
    )(tokens, cotangent)


def gradient(joined, tok, rows_all):
    groups, high, part = joined.shape
    extra = high - tok
    fold = tok // extra
    cols = 256

    def body(joined_ref, out_ref):
        left = jnp.concatenate(
            [
                joined_ref[k, tok:, q * rows_all:(q + 1) * rows_all]
                for k in range(groups)
                for q in range(fold)
            ],
            axis=0,
        ).T
        for j in range(0, part, cols):
            right = jnp.concatenate([joined_ref[k, :tok, j:j + cols] for k in range(groups)], axis=0)
            out_ref[:, j:j + cols] = jnp.dot(
                left, right, preferred_element_type=jnp.float32
            ).astype(out_ref.dtype)

    return pl.pallas_call(
        body,
        out_shape=jax.ShapeDtypeStruct((rows_all, part), jnp.bfloat16),
        compiler_params=params(),
        name="gradient",
    )(joined)


def raise_and_pick(terms, momentum, keep, table, groups, nz, ncore):
    rows, width = momentum.shape
    part = width // groups
    tiles = part // 128
    share = rows // ncore

    def body(terms_ref, mom_ref, keep_ref, table_ref, out_ref, sent_ref):
        pieces = []
        for g in range(groups):
            grad = terms_ref[g].astype(jnp.float32)
            for k in range(g + groups, terms_ref.shape[0], groups):
                grad = grad + terms_ref[k].astype(jnp.float32)
            raised = momentum_decay * mom_ref[:, g * part:(g + 1) * part] + grad
            pieces += [raised[:, t * 128:(t + 1) * 128] for t in range(tiles)]
        raised = jnp.concatenate(pieces, axis=0)
        both = table_ref[...]
        picked = exact_dot(raised, both.T) * keep_ref[...]
        moment_new = raised - exact_dot(picked, both)
        for j in range(width // 128):
            out_ref[:, j * 128:(j + 1) * 128] = moment_new[j * rows:(j + 1) * rows]
        for t in range(tiles):
            for c in range(ncore):
                starts = [(g * tiles + t) * rows + c * share for g in range(groups)]
                mine = jnp.concatenate([picked[at:at + share] for at in starts], axis=0)
                sent_ref[t * ncore + c] = mine.astype(jnp.bfloat16)

    return pl.pallas_call(
        body,
        out_shape=(
            jax.ShapeDtypeStruct((rows, width), jnp.float32),
            jax.ShapeDtypeStruct((nz * ncore, groups * share, 128), jnp.bfloat16),
        ),
        compiler_params=params(),
        name="raise_and_pick",
    )(terms, momentum, keep, table)


def update(sent, weight, table, groups, copies):
    sites, high, lanes = sent.shape
    rows, width = weight.shape
    part = width // groups
    share = high // groups

    def body(sent_ref, weight_ref, table_ref, out_ref):
        z, first = lax.axis_index("z"), lax.axis_index("core") == 0
        total = sent_ref[0].astype(jnp.float32)
        for s in range(1, sites):
            total = total + sent_ref[s].astype(jnp.float32)
        decoded = exact_dot(total, table_ref[...])
        held = []
        for g in range(groups):
            at = pl.multiple_of(g * part + z * 128, 128)
            tile = weight_ref[:, pl.ds(at, 128)].astype(jnp.float32)
            held.append(jnp.where(first, tile[:share], tile[share:]))
        fresh = (jnp.concatenate(held, axis=0) - step_size * decoded).astype(jnp.bfloat16)
        for c in range(copies):
            out_ref[c] = fresh

    return pl.pallas_call(
        body,
        out_shape=jax.ShapeDtypeStruct((copies, high, lanes), jnp.bfloat16),
        compiler_params=params(),
        name="update",
    )(sent, weight, table)


def project(joined, mine, other, tok):
    groups, _, part = joined.shape
    tiles, half, _ = mine.shape

    def body(tok_ref, mine_ref, other_ref, out_ref, weight_ref):
        @pl.when(pl.program_id(0) == 0)
        def _():
            first = lax.axis_index("core") == 0
            for t in range(tiles):
                a, b = mine_ref[t], other_ref[t]
                weight_ref[:half, t * 128:(t + 1) * 128] = jnp.where(first, a, b)
                weight_ref[half:, t * 128:(t + 1) * 128] = jnp.where(first, b, a)

        for k in range(2):
            out_ref[k] = lax.dot_general(
                tok_ref[k], weight_ref[...], ACROSS, preferred_element_type=jnp.float32
            ).astype(out_ref.dtype)

    whole = pl.BlockSpec((tiles, half, 128), lambda g: (0, 0, 0))
    return pl.pallas_call(
        body,
        grid=(groups // 2,),
        in_specs=[pl.BlockSpec((2, tok, part), lambda g: (g, 0, 0)), whole, whole],
        out_specs=pl.BlockSpec((2, tok, 2 * half), lambda g: (g, 0, 0)),
        out_shape=jax.ShapeDtypeStruct((groups, tok, 2 * half), jnp.bfloat16),
        scratch_shapes=[pltpu.VMEM((2 * half, part), jnp.bfloat16)],
        compiler_params=params(),
        name="project",
    )(joined, mine, other)


def finish(parts, rows, ncore):
    count, tok, rows_all = parts.shape
    share = rows // ncore

    def body(parts_ref, out_ref):
        scores = parts_ref[0].astype(jnp.float32)
        for k in range(1, count):
            scores = scores + parts_ref[k].astype(jnp.float32)
        there = lax.broadcasted_iota(jnp.int32, (rows_all, rows_all), 1)
        here = lax.broadcasted_iota(jnp.int32, (rows_all, rows_all), 0)
        source = there % rows // share * (rows_all // ncore) + there // rows * share + there % share
        order = jnp.where(here == source, 1.0, 0.0).astype(jnp.bfloat16)
        out_ref[...] = jnp.dot(
            scores.astype(jnp.bfloat16), order, preferred_element_type=jnp.float32
        ).astype(jnp.bfloat16)

    return pl.pallas_call(
        body,
        out_shape=jax.ShapeDtypeStruct((tok, rows_all), jnp.bfloat16),
        compiler_params=params(),
        name="finish",
    )(parts)


def exchange(value, axes):
    return lax.all_to_all(value, axes, 0, 0, tiled=True)


def shards(tokens, cotangent, weight, momentum, kept_index):
    nz, ncore, nyh, nyl, nx = (lax.axis_size(name) for name in ("z", "core", "yh", "yl", "x"))
    groups = nyl * nx
    site = lax.axis_index(SITE)
    _, tok, width = tokens.shape
    rows_all = cotangent.shape[2]
    rows = weight.shape[0]
    part = width // groups
    table = jnp.asarray(pair_table())

    joined = exchange(pack(tokens[0], cotangent[0], groups), GROUP)

    tiles = width // 128
    own = lax.dynamic_index_in_dim(kept_index, site, 0, keepdims=False)
    own = own.reshape(rows, tiles, 2, -1) + jnp.array([0, 64], jnp.int32)[None, None, :, None]
    own = own.reshape(rows, tiles, -1).transpose(1, 0, 2)
    keep = jnp.any(own[..., None] == jnp.arange(128, dtype=jnp.int32), axis=2)
    keep = keep.astype(jnp.float32).reshape(tiles * rows, 128)

    partial = gradient(joined, tok, rows_all)
    terms = exchange(partial.reshape(nyh * groups, rows, part), DEV)
    moment_new, sent = raise_and_pick(terms, momentum[0], keep, table, groups, nz, ncore)

    fresh = update(exchange(sent, SITE), weight, table, groups, nz * nyh)
    fresh = exchange(fresh.reshape(nz * nyh * groups, rows // ncore, 128), ("z",) + DEV)
    mine = fresh.reshape(nz, rows_all // ncore, 128)
    other = lax.ppermute(mine, "core", [(0, 1), (1, 0)])
    scores = exchange(project(joined, mine, other, tok), GROUP)
    return (finish(scores, rows, ncore)[None], moment_new[None])


def solution(mesh):
    grid = Mesh(mesh.devices.reshape(8, 2, 4, 2, 4), ("z", "core", "yh", "yl", "x"))
    placed = (
        P(SITE, DEV, None),
        P(SITE, DEV, None),
        P(DEV, None),
        P(SITE, DEV, None),
        P(None, DEV, None, None),
    )
    return jax.shard_map(
        shards,
        mesh=grid,
        in_specs=placed,
        out_specs=(P(SITE, DEV, None), P(SITE, DEV, None)),
        check_vma=False,
    )
```

time: 139 us -> 136 us (0.978)
  blocking collectives: 73.3 us -> 91.3 us
  starting transfers between devices: 24.6 us -> 14.6 us
  waiting for transfers between devices: 22 us -> 12.1 us
    all_to_all x3 -> x4, blocking collectives: 73.3 us -> 91.3 us  [exchange(): return lax.all_to_all(value, axes, 0, 0, tiled=True)]
    all_to_all x2 -> x1, starting transfers between devices: 24.6 us -> 10.2 us  [exchange(): return lax.all_to_all(value, axes, 0, 0, tiled=True)]
    all_to_all x2 -> x1, waiting for transfers between devices: 22 us -> 10.9 us  [exchange(): return lax.all_to_all(value, axes, 0, 0, tiled=True)]
    ppermute x0 -> x1, starting transfers between devices: none -> 4.41 us  [shards(): other = lax.ppermute(mine, 'core', [(0, 1), (1, 0)])]
    unnamed x14 -> x16, local copies, waits for them, and re-layouts: 4.27 us -> 5.78 us
    pallas_call x4 -> x5, Pallas kernels: 6.23 us -> 5.13 us  [the longest x1 2.26 us: project(): pl.pallas_call(body, grid=(groups // 2,), in_specs=[pl.BlockSpec((2, tok,...]
where the time goes in v3:
time: 136 us; the launch traced here: 135 us
  blocking collectives  91.3 us (67%)
  starting transfers between devices  14.6 us (11%)
  waiting for transfers between devices  12.1 us (9%)
  Pallas kernels  6.89 us (5%)
  local copies, waits for them, and re-layouts  6.43 us (5%)
  other arithmetic  3.02 us (2%)
    all_to_all x4, blocking collectives, exchange(): return lax.all_to_all(value, axes, 0, 0, tiled=True)  91.3 us
    all_to_all x1, waiting for transfers between devices, exchange(): return lax.all_to_all(value, axes, 0, 0, tiled=True)  10.9 us
    all_to_all x1, starting transfers between devices, exchange(): return lax.all_to_all(value, axes, 0, 0, tiled=True)  10.2 us
    unnamed x16, local copies, waits for them, and re-layouts  5.78 us
    ppermute x1, starting transfers between devices, shards(): other = lax.ppermute(mine, 'core', [(0, 1), (1, 0)])  4.41 us
    reduce_or x1, other arithmetic, shards(): keep = jnp.any(own[..., None] == jnp.arange(128, dtype=jnp.int32), axis=2)  2.98 us
  transfers between devices with their start and end apart: 2, of which 2 were waited for; matrix products, arithmetic and copies ran while one was open for 3% of the time, Pallas kernels for 0%

profile of v3, /device:TPU:1, one launch (start us, length us, event | category | flops | bytes accessed | tf_op | source)
XLA Modules:
  0.0 135.1 jit_solution(3767336739069541545)
XLA Ops:
  0.6 0.0 copy-start
  0.6 0.0 copy-start.3
  0.7 1.7 %copy-done.3 = bf16[1,128,8192]{2,1,0:T(8,128)(2,1)S(1)} copy-done((bf16[1,128,8192]{2,1,0:T(8,128)(2,1)S(1)}, bf16[1,128,8192]{2,1,0:T(8,128)(2,1)}, u32[]{:S(2)}) %copy-start.3) | copy-done | bytes 2097176
  2.3 0.0 copy-start.7
  2.3 0.8 copy-done.7
  3.2 0.3 pack.1
  3.5 34.3 %all_to_all.25.joined_ref.tok_ref = bf16[8,160,1024]{2,1,0:T(8,128)(2,1)S(1)} all-to-all(bf16[8,160,1024]{2,1,0:T(8,128)(2,1)S(1)} %pack.1), channel_id=1, replica_groups=mesh['z'=8,'core'=2,'yh'=4,'yl'=2,'x'=4] {'yl','x'}, dimensions={0} | all-to-all | bytes 5242880 | tf_op jit(solution)/shard_map/all_to_all | solution.py:216
  37.7 1.5 %gradient.1 = bf16[256,1024]{1,0:T(8,128)(2,1)} custom-call(bf16[8,160,1024]{2,1,0:T(8,128)(2,1)S(1)} %all_to_all.25.joined_ref.tok_ref), custom_call_target="tpu_custom_call" | custom-call | tf_op jit(solution)/shard_map/gradient/pallas_call | solution.py:86
  39.3 0.0 copy-start.1
  39.3 1.5 %copy-done.1 = bf16[8,160,1024]{2,1,0:T(8,128)(2,1)} copy-done((bf16[8,160,1024]{2,1,0:T(8,128)(2,1)}, bf16[8,160,1024]{2,1,0:T(8,128)(2,1)S(1)}, u32[]{:S(2)}) %copy-start.1) | copy-done | bytes 2621464
  40.8 0.0 copy-start.4
  40.8 0.0 copy-start.5
  40.8 0.0 copy-start.6
  40.8 10.2 %all-to-all-start.1 = ((bf16[32,8,1024]{2,1,0:T(8,128)(2,1)}), bf16[32,8,1024]{2,1,0:T(8,128)(2,1)S(1)}, u32[]{:S(2)}, u32[]{:S(2)}) async-start(bf16[32,8,1024]{2,1,0:T(8,128)(2,1)} %bitcast.2), calls=%async_computation.1 | async-start | bytes 1048576 | tf_op jit(solution)/shard_map/all_to_all | solution.py:216
  51.0 0.0 copy-done
  51.0 0.2 copy.12
  51.2 0.1 reshape.27
  51.4 0.1 add.22
  51.4 0.1 add.23
  51.5 0.2 copy.13
  51.7 3.0 %fusion = pred[64,8,128]{2,1,0:T(8,128)(4,1)S(1)} fusion(s32[64,8,32]{2,1,0:T(8,128)S(1)} %copy.13), kind=kLoop, calls=%fused_computation.1 | loop fusion | flops 4128768 | bytes 131072 | tf_op jit(solution)/shard_map/reduce_or | solution.py:235
  54.7 10.9 %all-to-all-done.1.terms_ref = bf16[32,8,1024]{2,1,0:T(8,128)(2,1)S(1)} async-done(((bf16[32,8,1024]{2,1,0:T(8,128)(2,1)}), bf16[32,8,1024]{2,1,0:T(8,128)(2,1)S(1)}, u32[]{:S(2)}, u32[]{:S(2)}) %all-to-all-start.1) | async-done | bytes 524320 | tf_op jit(solution)/shard_map/all_to_all | solution.py:216
  65.7 0.0 copy-done.4
  65.7 0.0 copy-done.5
  65.7 1.8 %raise_and_pick.1 = (f32[8,8192]{1,0:T(8,128)}, bf16[16,32,128]{2,1,0:T(8,128)(2,1)S(1)}) custom-call(bf16[32,8,1024]{2,1,0:T(8,128)(2,1)S(1)} %all-to-all-done.1.terms_ref, f32[8,8192]{1,0:T(8,128)S(1)} %bitcast.18, f32[512,128]{1,0:T(8,128)S(1)} %convert_bitcast_fusion.keep_ref, f32[128,128]{1,0:T(8,128)S(1)} %copy-done.5), custom_call_target="tpu_custom_call" | custom-call | tf_op jit(solution)/shard_map/raise_and_pick/pallas_call | solution.py:120
  67.4 23.4 %all_to_all.26.sent_ref = bf16[16,32,128]{2,1,0:T(8,128)(2,1)S(1)} all-to-all(bf16[16,32,128]{2,1,0:T(8,128)(2,1)S(1)} %get-tuple-element.4), channel_id=1, replica_groups=mesh['z'=8,'core'=2,'yh'=4,'yl'=2,'x'=4] {'z','core'}, dimensions={0} | all-to-all | bytes 262144 | tf_op jit(solution)/shard_map/all_to_all | solution.py:216
  90.8 0.0 copy-done.6
  90.8 0.2 update.1
  91.0 22.3 %all_to_all.27 = bf16[256,4,128]{2,1,0:T(4,128)(2,1)S(1)} all-to-all(bf16[256,4,128]{2,1,0:T(4,128)(2,1)S(1)} %bitcast.17), channel_id=1, replica_groups=mesh['z'=8,'core'=2,'yh'=4,'yl'=2,'x'=4] {'z','yh','yl','x'}, dimensions={0} | all-to-all | bytes 524288 | tf_op jit(solution)/shard_map/all_to_all | solution.py:216
  113.4 4.4 %collective-permute-start = (bf16[8,128,128]{2,1,0:T(8,128)(2,1)S(1)}, bf16[8,128,128]{2,1,0:T(8,128)(2,1)S(1)}, u32[]{:S(2)}, u32[]{:S(2)}) collective-permute-start(bf16[8,128,128]{2,1,0:T(8,128)(2,1)S(1)} %bitcast.15), channel_id=1, source_target_pairs={{0,32},{32,0},{1,33},{33,1},{2,34},{34,2},{3,35},{35,3},{4,36},{36... | collective-permute-start | bytes 786440 | tf_op jit(solution)/shard_map/ppermute | solution.py:245
  117.8 1.1 collective-permute-done.other_ref
  118.9 0.0 copy-start.2
  118.9 1.7 %copy-done.2 = bf16[8,160,1024]{2,1,0:T(8,128)(2,1)S(1)} copy-done((bf16[8,160,1024]{2,1,0:T(8,128)(2,1)S(1)}, bf16[8,160,1024]{2,1,0:T(8,128)(2,1)}, u32[]{:S(2)}) %copy-start.2) | copy-done | bytes 2621464
  120.7 2.3 %project.1 = bf16[8,128,256]{2,1,0:T(8,128)(2,1)S(1)} custom-call(bf16[8,160,1024]{2,1,0:T(8,128)(2,1)S(1)} %copy-done.2, bf16[8,128,128]{2,1,0:T(8,128)(2,1)S(1)} %bitcast.16, bf16[8,128,128]{2,1,0:T(8,128)(2,1)S(1)} %collective-permute-done.other_ref), custom_call_target="tpu_custom_call" | custom-call | tf_op jit(solution)/shard_map/project/pallas_call | solution.py:179
  122.9 11.3 %all_to_all.28.parts_ref = bf16[8,128,256]{2,1,0:T(8,128)(2,1)S(1)} all-to-all(bf16[8,128,256]{2,1,0:T(8,128)(2,1)S(1)} %project.1), channel_id=1, replica_groups=mesh['z'=8,'core'=2,'yh'=4,'yl'=2,'x'=4] {'yl','x'}, dimensions={0} | all-to-all | bytes 1048576 | tf_op jit(solution)/shard_map/all_to_all | solution.py:216
  134.3 0.8 finish.1
  (4 shorter events, 0.1 us)
Async XLA Ops:
  0.6 50.3 %copy-start = (s32[16,8,128,16]{2,3,1,0:T(8,128)S(1)}, s32[16,8,128,16]{2,3,1,0:T(8,128)}, u32[]{:S(2)}) copy-start(s32[16,8,128,16]{2,3,1,0:T(8,128)} %param.11) | copy-start | bytes 3145732
  0.6 1.7 %copy-start.3 = (bf16[1,128,8192]{2,1,0:T(8,128)(2,1)S(1)}, bf16[1,128,8192]{2,1,0:T(8,128)(2,1)}, u32[]{:S(2)}) copy-start(bf16[1,128,8192]{2,1,0:T(8,128)(2,1)} %param.7) | copy-start | bytes 6291460
  2.3 0.8 copy-start.7
  39.3 1.5 %copy-start.1 = (bf16[8,160,1024]{2,1,0:T(8,128)(2,1)}, bf16[8,160,1024]{2,1,0:T(8,128)(2,1)S(1)}, u32[]{:S(2)}) copy-start(bf16[8,160,1024]{2,1,0:T(8,128)(2,1)S(1)} %all_to_all.25.joined_ref.tok_ref) | copy-start | bytes 7864324
  40.8 24.9 %copy-start.4 = (f32[1,8,8192]{2,1,0:T(8,128)S(1)}, f32[1,8,8192]{2,1,0:T(8,128)}, u32[]{:S(2)}) copy-start(f32[1,8,8192]{2,1,0:T(8,128)} %param.10) | copy-start | bytes 786436
  40.8 24.9 %copy-start.5 = (f32[128,128]{1,0:T(8,128)S(1)}, f32[128,128]{1,0:T(8,128)}, u32[]{:S(2)}) copy-start(f32[128,128]{1,0:T(8,128)} %constant.27.clone.table_ref) | copy-start | bytes 196612
  40.8 50.0 %copy-start.6 = (bf16[8,8192]{1,0:T(8,128)(2,1)S(1)}, bf16[8,8192]{1,0:T(8,128)(2,1)}, u32[]{:S(2)}) copy-start(bf16[8,8192]{1,0:T(8,128)(2,1)} %weight_ref.1) | copy-start | bytes 393220
  40.8 24.9 %all-to-all-start.1 = ((bf16[32,8,1024]{2,1,0:T(8,128)(2,1)}), bf16[32,8,1024]{2,1,0:T(8,128)(2,1)S(1)}, u32[]{:S(2)}, u32[]{:S(2)}) async-start(bf16[32,8,1024]{2,1,0:T(8,128)(2,1)} %bitcast.2), calls=%async_computation.1 | async-start | bytes 1048576 | tf_op jit(solution)/shard_map/all_to_all | solution.py:216
  113.4 5.6 %collective-permute-start = (bf16[8,128,128]{2,1,0:T(8,128)(2,1)S(1)}, bf16[8,128,128]{2,1,0:T(8,128)(2,1)S(1)}, u32[]{:S(2)}, u32[]{:S(2)}) collective-permute-start(bf16[8,128,128]{2,1,0:T(8,128)(2,1)S(1)} %bitcast.15), channel_id=1, source_target_pairs={{0,32},{32,0},{1,33},{33,1},{2,34},{34,2},{3,35},{35,3},{4,36},{36... | collective-permute-start | bytes 786440 | tf_op jit(solution)/shard_map/ppermute | solution.py:245
  118.9 1.7 %copy-start.2 = (bf16[8,160,1024]{2,1,0:T(8,128)(2,1)S(1)}, bf16[8,160,1024]{2,1,0:T(8,128)(2,1)}, u32[]{:S(2)}) copy-start(bf16[8,160,1024]{2,1,0:T(8,128)(2,1)} %copy-done.1) | copy-start | bytes 7864324

commit v4 on v2

v4 whole, which is shorter than its diff:
```python
import numpy as np
import jax
import jax.numpy as jnp
from jax import lax
from jax.experimental import pallas as pl
from jax.experimental.pallas import tpu as pltpu
from jax.sharding import Mesh, PartitionSpec as P

momentum_decay = 0.999
step_size = 0.01
SITE = ("z", "core")
GROUP = ("yl", "x")
DEV = ("yh", "yl", "x")
MIB = 1024 * 1024
ACROSS = (((1,), (1,)), ((), ()))
SIDE = 16


def pair_table():
    freq = np.arange(64)[:, None]
    place = np.arange(64)[None, :]
    factor = np.where(freq == 0, np.sqrt(1.0 / 64.0), np.sqrt(2.0 / 64.0))
    one = factor * np.cos(np.pi * (2.0 * place + 1.0) * freq / 128.0)
    return np.kron(np.eye(2), one).astype(np.float32)


def exact_dot(a, b):
    return jnp.dot(a, b, precision=lax.Precision.HIGHEST, preferred_element_type=jnp.float32)


def iota(shape, axis):
    return lax.broadcasted_iota(jnp.int32, shape, axis)


def params(mib=16):
    return pltpu.CompilerParams(vmem_limit_bytes=mib * MIB)


def pack(tokens, cotangent, momentum, weight, kept, groups):
    tok, width = tokens.shape
    part = width // groups
    rows_all = cotangent.shape[1]
    rows = weight.shape[0]
    fold = part // rows_all
    extra = tok // fold
    _, entries, blocks = kept.shape
    below = extra + SIDE

    def body(tok_ref, cot_ref, mom_ref, weight_ref, kept_ref, out_ref, held_ref, cot_vmem, mom_vmem, weight_vmem,
             spots_ref, in_sem, part_sem, out_sem):
        fetches = [
            pltpu.make_async_copy(tok_ref.at[:, g * part:(g + 1) * part], held_ref.at[g, :tok, :], in_sem.at[g])
            for g in range(groups)
        ]
        sends = [pltpu.make_async_copy(held_ref.at[g], out_ref.at[g], out_sem.at[g]) for g in range(groups)]
        parts = [
            pltpu.make_async_copy(kept_ref.at[lax.axis_index(SITE)], spots_ref, part_sem.at[0]),
            pltpu.make_async_copy(cot_ref, cot_vmem, part_sem.at[1]),
            pltpu.make_async_copy(mom_ref, mom_vmem, part_sem.at[2]),
            pltpu.make_async_copy(weight_ref, weight_vmem, part_sem.at[3]),
        ]
        for fetch in parts + fetches:
            fetch.start()
        for fetch in parts:
            fetch.wait()
        z = lax.axis_index("z")
        spots = spots_ref[...].astype(jnp.float32).T
        unused = jnp.zeros((rows, part - 3 * 128), jnp.float32)
        span = part // 64
        for g in range(groups):
            for q in range(fold):
                held_ref[g, tok:tok + extra, q * rows_all:(q + 1) * rows_all] = cot_vmem[q * extra:(q + 1) * extra, :]
            tile = weight_vmem[:, pl.ds(pl.multiple_of(g * part + z * 128, 128), 128)].astype(jnp.float32)
            low = [spots[g * span + h * rows:g * span + (h + 1) * rows] for h in range(span // rows)]
            low = jnp.concatenate(low + [tile, unused], axis=1)
            side = jnp.concatenate([mom_vmem[:, g * part:(g + 1) * part], low], axis=0)
            held_ref[g, tok + extra:, :] = side.astype(jnp.bfloat16)
        for fetch, send in zip(fetches, sends):
            fetch.wait()
            send.start()
        for send in sends:
            send.wait()

    anywhere = pl.BlockSpec(memory_space=pl.ANY)
    return pl.pallas_call(
        body,
        in_specs=[anywhere] * 5,
        out_specs=anywhere,
        out_shape=jax.ShapeDtypeStruct((groups, tok + below, part), tokens.dtype),
        scratch_shapes=[
            pltpu.VMEM((groups, tok + below, part), tokens.dtype),
            pltpu.VMEM((tok, rows_all), cotangent.dtype),
            pltpu.VMEM((rows, width), jnp.float32),
            pltpu.VMEM((rows, width), weight.dtype),
            pltpu.VMEM((entries, blocks), jnp.int32),
            pltpu.SemaphoreType.DMA((groups,)),
            pltpu.SemaphoreType.DMA((4,)),
            pltpu.SemaphoreType.DMA((groups,)),
        ],
        compiler_params=params(62),
        name="pack",
    )(tokens, cotangent, momentum, weight, kept)


def gradient(joined, tok, rows_all):
    groups, high, part = joined.shape
    extra = high - tok - SIDE
    fold = tok // extra
    cols = 256

    def body(joined_ref, out_ref):
        left = jnp.concatenate(
            [
                joined_ref[k, tok:tok + extra, q * rows_all:(q + 1) * rows_all]
                for k in range(groups)
                for q in range(fold)
            ],
            axis=0,
        ).T
        for j in range(0, part, cols):
            right = jnp.concatenate([joined_ref[k, :tok, j:j + cols] for k in range(groups)], axis=0)
            out_ref[:, j:j + cols] = jnp.dot(
                left, right, preferred_element_type=jnp.float32
            ).astype(out_ref.dtype)

    return pl.pallas_call(
        body,
        out_shape=jax.ShapeDtypeStruct((rows_all, part), jnp.bfloat16),
        compiler_params=params(),
        name="gradient",
    )(joined)


def raise_and_pick(terms, joined, table, sites, rows_all, nx):
    nyh, band, part = terms.shape
    groups, high, _ = joined.shape
    tiles = part // 128
    rows = band // groups
    fold = part // rows_all
    span = part // 64

    def body(terms_ref, side_ref, table_ref, sent_ref, change_ref, held_ref, keep_ref, moment_ref):
        core = lax.axis_index("core")
        freq = iota((64, 128), 0).astype(jnp.float32)
        gather = iota((rows, 128), 0) == iota((rows, 128), 1) // (128 // rows)
        gather = jnp.where(gather, 1.0, 0.0).astype(jnp.bfloat16)
        for g in range(groups):
            side = side_ref[g].astype(jnp.float32)
            marks = []
            for b in range(span):
                line = side[rows + b % rows:rows + b % rows + 1, b // rows * 128:(b // rows + 1) * 128]
                marks.append(jnp.where(line == freq, 1.0, 0.0).astype(jnp.bfloat16))
            keep = lax.dot_general(
                gather, jnp.concatenate(marks, axis=0), ACROSS, preferred_element_type=jnp.float32
            )
            for t in range(tiles):
                at = t * band + g * rows
                keep_ref[at:at + rows, :] = keep[:, t * 128:(t + 1) * 128]
                moment_ref[at:at + rows, :] = momentum_decay * side[:rows, t * 128:(t + 1) * 128]
        for x in range(nx):
            side = side_ref[core * nx + x].astype(jnp.float32)
            held_ref[x * rows:(x + 1) * rows, :] = side[rows:2 * rows, span // rows * 128:(span // rows + 1) * 128]

        grad = terms_ref[0].astype(jnp.float32)
        for k in range(1, nyh):
            grad = grad + terms_ref[k].astype(jnp.float32)
        grad = jnp.concatenate([grad[:, t * 128:(t + 1) * 128] for t in range(tiles)], axis=0)
        both = table_ref[...]
        picked = exact_dot(moment_ref[...] + grad, both.T) * keep_ref[...]
        sent_ref[...] = picked.astype(jnp.bfloat16).reshape(sent_ref.shape)
        change = grad - exact_dot(picked, both)
        for g in range(groups):
            pieces = []
            for q in range(fold):
                across = []
                for t in range(q * tiles // fold, (q + 1) * tiles // fold):
                    at = t * band + g * rows
                    across.append(change[at:at + rows])
                pieces.append(jnp.concatenate(across, axis=1))
            change_ref[g] = jnp.concatenate(pieces, axis=0).astype(jnp.bfloat16)

    def whole(*shape):
        return pl.BlockSpec(shape, lambda i: (0,) * len(shape))

    share = tiles * band // sites
    return pl.pallas_call(
        body,
        grid=(1,),
        in_specs=[
            whole(nyh, band, part),
            pl.BlockSpec((groups, SIDE, part), lambda i: (0, high // SIDE - 1, 0)),
            whole(128, 128),
        ],
        out_specs=(whole(sites, share, 128), whole(groups, fold * rows, rows_all), whole(nx * rows, 128)),
        out_shape=(
            jax.ShapeDtypeStruct((sites, share, 128), jnp.bfloat16),
            jax.ShapeDtypeStruct((groups, fold * rows, rows_all), jnp.bfloat16),
            jax.ShapeDtypeStruct((nx * rows, 128), jnp.float32),
        ),
        scratch_shapes=[pltpu.VMEM((tiles * band, 128), jnp.float32)] * 2,
        compiler_params=params(),
        name="raise_and_pick",
    )(terms, joined, table)


def update(sent, held, table, copies):
    sites, high, lanes = sent.shape

    def body(sent_ref, held_ref, table_ref, out_ref):
        total = sent_ref[0].astype(jnp.float32)
        for s in range(1, sites):
            total = total + sent_ref[s].astype(jnp.float32)
        fresh = (held_ref[...] - step_size * exact_dot(total, table_ref[...])).astype(jnp.bfloat16)
        for c in range(copies):
            out_ref[c] = fresh

    return pl.pallas_call(
        body,
        out_shape=jax.ShapeDtypeStruct((copies, high, lanes), jnp.bfloat16),
        compiler_params=params(),
        name="update",
    )(sent, held, table)


def project(joined, mine, other, change, tok):
    groups, _, part = joined.shape
    tiles, nyh, share, _ = mine.shape
    rows_all = 2 * nyh * share
    extra = change.shape[1]

    def body(joined_ref, mine_ref, other_ref, change_ref, out_ref):
        first = lax.axis_index("core") == 0
        weight = []
        for t in range(tiles):
            bands = []
            for y in range(nyh):
                a, b = mine_ref[t, y], other_ref[t, y]
                bands += [jnp.where(first, a, b), jnp.where(first, b, a)]
            weight.append(jnp.concatenate(bands, axis=0))
        weight = jnp.concatenate(weight, axis=1)
        for k in range(groups):
            out_ref[k, :tok, :] = lax.dot_general(
                joined_ref[k, :tok, :], weight, ACROSS, preferred_element_type=jnp.float32
            ).astype(out_ref.dtype)
            out_ref[k, tok:, :] = change_ref[k]

    return pl.pallas_call(
        body,
        out_shape=jax.ShapeDtypeStruct((groups, tok + extra, rows_all), jnp.bfloat16),
        compiler_params=params(),
        name="project",
    )(joined, mine, other, change)


def finish(parts, momentum, tok):
    groups, high, rows_all = parts.shape
    rows, width = momentum.shape
    part = width // groups

    def body(parts_ref, mom_ref, scores_ref, out_ref):
        scores = parts_ref[0, :tok, :].astype(jnp.float32)
        for k in range(1, groups):
            scores = scores + parts_ref[k, :tok, :].astype(jnp.float32)
        scores_ref[...] = scores.astype(jnp.bfloat16)
        for g in range(groups):
            change = parts_ref[g, tok:, :].astype(jnp.float32)
            for q in range(part // rows_all):
                at = g * part + q * rows_all
                out_ref[:, at:at + rows_all] = (
                    momentum_decay * mom_ref[:, at:at + rows_all] + change[q * rows:(q + 1) * rows]
                )

    return pl.pallas_call(
        body,
        out_shape=(
            jax.ShapeDtypeStruct((tok, rows_all), jnp.bfloat16),
            jax.ShapeDtypeStruct((rows, width), jnp.float32),
        ),
        compiler_params=params(),
        name="finish",
    )(parts, momentum)


def exchange(value, axes):
    return lax.all_to_all(value, axes, 0, 0, tiled=True)


def shards(tokens, cotangent, weight, momentum, kept_index):
    nz, ncore, nyh, nyl, nx = (lax.axis_size(name) for name in ("z", "core", "yh", "yl", "x"))
    groups = nyl * nx
    sites = nz * ncore
    _, tok, width = tokens.shape
    rows_all = cotangent.shape[2]
    rows = weight.shape[0]
    part = width // groups
    band = rows_all // nyh
    table = jnp.asarray(pair_table())

    kept = kept_index.transpose(0, 1, 3, 2).reshape(sites, -1, width // 64)
    joined = exchange(pack(tokens[0], cotangent[0], momentum[0], weight, kept, groups), GROUP)

    partial = gradient(joined, tok, rows_all)
    terms = exchange(partial.reshape(nyh, band, part), "yh")
    sent, change, held = raise_and_pick(terms, joined, table, sites, rows_all, nx)

    fresh = update(exchange(sent, SITE), held, table, nz * nyh)
    mine = exchange(fresh, ("z", "yh")).reshape(nz, nyh, band // ncore, 128)
    other = lax.ppermute(mine, "core", [(0, 1), (1, 0)])
    scores, moment_new = finish(exchange(project(joined, mine, other, change, tok), GROUP), momentum[0], tok)
    return (scores[None], moment_new[None])


def solution(mesh):
    grid = Mesh(mesh.devices.reshape(8, 2, 4, 2, 4), ("z", "core", "yh", "yl", "x"))
    placed = (
        P(SITE, DEV, None),
        P(SITE, DEV, None),
        P(DEV, None),
        P(SITE, DEV, None),
        P(None, DEV, None, None),
    )
    return jax.shard_map(
        shards,
        mesh=grid,
        in_specs=placed,
        out_specs=(P(SITE, DEV, None), P(SITE, DEV, None)),
        check_vma=False,
    )
```

time: 139 us -> 127 us (0.914)
  blocking collectives: 73.3 us -> 111 us
  waiting for transfers between devices: 22 us -> 1.14 us
  starting transfers between devices: 24.6 us -> 4.8 us
  local copies, waits for them, and re-layouts: 5.65 us -> 0.01 us
  other arithmetic: 3.73 us -> 0 us
    all_to_all x3 -> x5, blocking collectives: 73.3 us -> 111 us  [exchange(): return lax.all_to_all(value, axes, 0, 0, tiled=True)]
    all_to_all x2 -> x0, starting transfers between devices: 24.6 us -> none  [exchange(): return lax.all_to_all(value, axes, 0, 0, tiled=True)]
    all_to_all x2 -> x0, waiting for transfers between devices: 22 us -> none  [exchange(): return lax.all_to_all(value, axes, 0, 0, tiled=True)]
    ppermute x0 -> x1, starting transfers between devices: none -> 4.8 us  [shards(): other = lax.ppermute(mine, 'core', [(0, 1), (1, 0)])]
    unnamed x14 -> x4, local copies, waits for them, and re-layouts: 4.27 us -> 0.01 us
    reduce_or x1 -> x0, other arithmetic: 2.98 us -> none  [shards(): keep = jnp.any(own[..., None] == jnp.arange(128, dtype=jnp.int32), axis=2)]
    pallas_call x5 -> x6, Pallas kernels: 8 us -> 8.28 us  [the longest x1 3.5 us: pack(): pl.pallas_call(body, in_specs=[anywhere] * 5, out_specs=anywhere, out_sha...]
  transfers between devices with their start and end apart: 2 -> 1, of which waited for: 2 -> 1; matrix products, arithmetic and copies ran while one was open for 3% -> 0% of each run, Pallas kernels for 0% -> 0%
where the time goes in v4:
time: 127 us; the launch traced here: 126 us
  blocking collectives  111 us (87%)
  Pallas kernels  8.28 us (7%)
  starting transfers between devices  4.8 us (4%)
    all_to_all x5, blocking collectives, exchange(): return lax.all_to_all(value, axes, 0, 0, tiled=True)  111 us
    ppermute x1, starting transfers between devices, shards(): other = lax.ppermute(mine, 'core', [(0, 1), (1, 0)])  4.8 us
    pallas_call x1, Pallas kernels, pack(): pl.pallas_call(body, in_specs=[anywhere] * 5, out_specs=anywhere, out_sha...  3.5 us
  transfers between devices with their start and end apart: 1, of which 1 were waited for; matrix products, arithmetic and copies ran while one was open for 0% of the time, Pallas kernels for 0%

profile of v4, /device:TPU:1, one launch (start us, length us, event | category | flops | bytes accessed | tf_op | source)
XLA Modules:
  0.0 126.2 jit_solution(6564594962542773267)
XLA Ops:
  0.6 3.5 %pack.1 = bf16[8,176,1024]{2,1,0:T(8,128)(2,1)} custom-call(bf16[128,8192]{1,0:T(8,128)(2,1)} %bitcast.15, bf16[128,256]{1,0:T(8,128)(2,1)} %bitcast.17, f32[8,8192]{1,0:T(8,128)} %bitcast.11, bf16[8,8192]{1,0:T(8,128)(2,1)} %weight_ref.1, s32[16,128,128]{2,1,0:T(8,128)} %bitcast.16), custom_call_target="tpu_custom_call" | custom-call | tf_op jit(solution)/shard_map/pack/pallas_call | solution.py:85
  4.1 35.7 %all_to_all.25.joined_ref.side_ref = bf16[8,176,1024]{2,1,0:T(8,128)(2,1)S(1)} all-to-all(bf16[8,176,1024]{2,1,0:T(8,128)(2,1)} %pack.1), channel_id=1, replica_groups=mesh['z'=8,'core'=2,'yh'=4,'yl'=2,'x'=4] {'yl','x'}, dimensions={0} | all-to-all | bytes 5767168 | tf_op jit(solution)/shard_map/all_to_all | solution.py:285
  39.8 0.0 copy-start.1
  39.8 0.7 gradient.1
  40.6 24.0 %all_to_all.26.terms_ref = bf16[4,64,1024]{2,1,0:T(8,128)(2,1)S(1)} all-to-all(bf16[4,64,1024]{2,1,0:T(8,128)(2,1)S(1)} %bitcast.10), channel_id=1, replica_groups=mesh['z'=8,'core'=2,'yh'=4,'yl'=2,'x'=4] {'yh'}, dimensions={0} | all-to-all | bytes 1048576 | tf_op jit(solution)/shard_map/all_to_all | solution.py:285
  64.6 0.0 copy-done.1
  64.6 1.6 %raise_and_pick.1 = (bf16[16,32,128]{2,1,0:T(8,128)(2,1)S(1)}, bf16[8,32,256]{2,1,0:T(8,128)(2,1)S(1)}, f32[32,128]{1,0:T(8,128)S(1)}) custom-call(bf16[4,64,1024]{2,1,0:T(8,128)(2,1)S(1)} %all_to_all.26.terms_ref, bf16[8,176,1024]{2,1,0:T(8,128)(2,1)S(1)} %all_to_all.25.joined_ref.side_ref, f32[128,128]{1,0:T(8,128)S(1)} %copy-done.1), custom_call_target="tpu_custom_call" | custom-call | tf_op jit(solution)/shard_map/raise_and_pick/pallas_call | solution.py:186
  66.2 22.6 %all_to_all.27.sent_ref = bf16[16,32,128]{2,1,0:T(8,128)(2,1)S(1)} all-to-all(bf16[16,32,128]{2,1,0:T(8,128)(2,1)S(1)} %get-tuple-element.7), channel_id=1, replica_groups=mesh['z'=8,'core'=2,'yh'=4,'yl'=2,'x'=4] {'z','core'}, dimensions={0} | all-to-all | bytes 262144 | tf_op jit(solution)/shard_map/all_to_all | solution.py:285
  88.8 0.2 update.1
  89.0 15.3 %all_to_all.28 = bf16[32,32,128]{2,1,0:T(8,128)(2,1)S(1)} all-to-all(bf16[32,32,128]{2,1,0:T(8,128)(2,1)S(1)} %update.1), channel_id=1, replica_groups=mesh['z'=8,'core'=2,'yh'=4,'yl'=2,'x'=4] {'z','yh'}, dimensions={0} | all-to-all | bytes 524288 | tf_op jit(solution)/shard_map/all_to_all | solution.py:285
  104.3 0.0 copy-start
  104.3 4.8 %collective-permute-start = (bf16[8,4,32,128]{3,2,1,0:T(8,128)(2,1)S(1)}, bf16[8,4,32,128]{3,2,1,0:T(8,128)(2,1)S(1)}, u32[]{:S(2)}, u32[]{:S(2)}) collective-permute-start(bf16[8,4,32,128]{3,2,1,0:T(8,128)(2,1)S(1)} %bitcast.13), channel_id=1, source_target_pairs={{0,32},{32,0},{1,33},{33,1},{2,34},{34,2},{3,35},{35,3},{4,36},{36... | collective-permute-start | bytes 786440 | tf_op jit(solution)/shard_map/ppermute | solution.py:308
  109.1 1.1 collective-permute-done.other_ref
  110.3 1.5 %project.1 = bf16[8,160,256]{2,1,0:T(8,128)(2,1)S(1)} custom-call(bf16[8,176,1024]{2,1,0:T(8,128)(2,1)S(1)} %all_to_all.25.joined_ref.side_ref, bf16[8,4,32,128]{3,2,1,0:T(8,128)(2,1)S(1)} %bitcast.14, bf16[8,4,32,128]{3,2,1,0:T(8,128)(2,1)S(1)} %collective-permute-done.other_ref, bf16[8,32,256]{2,1,0:T(8,128)(2,1)S(1)} %get-tuple-element.9.change_ref), custom_call_target="tpu_custom_call" | custom-call | tf_op jit(solution)/shard_map/project/pallas_call | solution.py:247
  111.8 13.6 %all_to_all.29.parts_ref = bf16[8,160,256]{2,1,0:T(8,128)(2,1)S(1)} all-to-all(bf16[8,160,256]{2,1,0:T(8,128)(2,1)S(1)} %project.1), channel_id=1, replica_groups=mesh['z'=8,'core'=2,'yh'=4,'yl'=2,'x'=4] {'yl','x'}, dimensions={0} | all-to-all | bytes 1310720 | tf_op jit(solution)/shard_map/all_to_all | solution.py:285
  125.4 0.0 copy-done
  125.4 0.8 finish.1
Async XLA Ops:
  39.8 24.8 %copy-start.1 = (f32[128,128]{1,0:T(8,128)S(1)}, f32[128,128]{1,0:T(8,128)}, u32[]{:S(2)}) copy-start(f32[128,128]{1,0:T(8,128)} %constant.2.clone.table_ref) | copy-start | bytes 196612
  104.3 21.0 %copy-start = (f32[1,8,8192]{2,1,0:T(8,128)S(1)}, f32[1,8,8192]{2,1,0:T(8,128)}, u32[]{:S(2)}) copy-start(f32[1,8,8192]{2,1,0:T(8,128)} %param.9) | copy-start | bytes 786436
  104.3 5.9 %collective-permute-start = (bf16[8,4,32,128]{3,2,1,0:T(8,128)(2,1)S(1)}, bf16[8,4,32,128]{3,2,1,0:T(8,128)(2,1)S(1)}, u32[]{:S(2)}, u32[]{:S(2)}) collective-permute-start(bf16[8,4,32,128]{3,2,1,0:T(8,128)(2,1)S(1)} %bitcast.13), channel_id=1, source_target_pairs={{0,32},{32,0},{1,33},{33,1},{2,34},{34,2},{3,35},{35,3},{4,36},{36... | collective-permute-start | bytes 786440 | tf_op jit(solution)/shard_map/ppermute | solution.py:308

commit v5 on v4

--- a/solution.py
+++ b/solution.py
@@ -30,6 +30,20 @@
 
 def iota(shape, axis):
     return lax.broadcasted_iota(jnp.int32, shape, axis)
+
+
+def halves(a):
+    high = a.astype(jnp.bfloat16)
+    return high, (a - high.astype(jnp.float32)).astype(jnp.bfloat16)
+
+
+def close_dot(a, b):
+    (a_high, a_low), (b_high, b_low) = halves(a), halves(b)
+
+    def dot(p, q):
+        return jnp.dot(p, q, preferred_element_type=jnp.float32)
+
+    return dot(a_high, b_high) + (dot(a_high, b_low) + dot(a_low, b_high))
 
 
 def params(mib=16):
@@ -75,9 +89,8 @@
             low = jnp.concatenate(low + [tile, unused], axis=1)
             side = jnp.concatenate([mom_vmem[:, g * part:(g + 1) * part], low], axis=0)
             held_ref[g, tok + extra:, :] = side.astype(jnp.bfloat16)
-        for fetch, send in zip(fetches, sends):
-            fetch.wait()
-            send.start()
+            fetches[g].wait()
+            sends[g].start()
         for send in sends:
             send.wait()
 
@@ -166,9 +179,9 @@
             grad = grad + terms_ref[k].astype(jnp.float32)
         grad = jnp.concatenate([grad[:, t * 128:(t + 1) * 128] for t in range(tiles)], axis=0)
         both = table_ref[...]
-        picked = exact_dot(moment_ref[...] + grad, both.T) * keep_ref[...]
+        picked = close_dot(moment_ref[...] + grad, both.T) * keep_ref[...]
         sent_ref[...] = picked.astype(jnp.bfloat16).reshape(sent_ref.shape)
-        change = grad - exact_dot(picked, both)
+        change = grad - close_dot(picked, both)
         for g in range(groups):
             pieces = []
             for q in range(fold):
@@ -238,10 +251,13 @@
                 bands += [jnp.where(first, a, b), jnp.where(first, b, a)]
             weight.append(jnp.concatenate(bands, axis=0))
         weight = jnp.concatenate(weight, axis=1)
+        weight = weight.T
+        for k in range(0, groups, 2):
+            both = jnp.concatenate([joined_ref[k, :tok, :], joined_ref[k + 1, :tok, :]], axis=0)
+            both = jnp.dot(both, weight, preferred_element_type=jnp.float32).astype(out_ref.dtype)
+            out_ref[k, :tok, :] = both[:tok]
+            out_ref[k + 1, :tok, :] = both[tok:]
         for k in range(groups):
-            out_ref[k, :tok, :] = lax.dot_general(
-                joined_ref[k, :tok, :], weight, ACROSS, preferred_element_type=jnp.float32
-            ).astype(out_ref.dtype)
             out_ref[k, tok:, :] = change_ref[k]
 
     return pl.pallas_call(

time: 127 us -> 125 us (0.984)
  no operation moved by 1% of the time
where the time goes in v5:
time: 125 us
  blocking collectives  111 us (89%)
  Pallas kernels  7.07 us (6%)
  starting transfers between devices  4.8 us (4%)
    all_to_all x5, blocking collectives, exchange(): return lax.all_to_all(value, axes, 0, 0, tiled=True)  111 us
    ppermute x1, starting transfers between devices, shards(): other = lax.ppermute(mine, 'core', [(0, 1), (1, 0)])  4.8 us
    pallas_call x1, Pallas kernels, pack(): pl.pallas_call(body, in_specs=[anywhere] * 5, out_specs=anywhere, out_sha...  3.44 us
  transfers between devices with their start and end apart: 1, of which 1 were waited for; matrix products, arithmetic and copies ran while one was open for 0% of the time, Pallas kernels for 0%

profile of v5, /device:TPU:1, one launch (start us, length us, event | category | flops | bytes accessed | tf_op | source)
XLA Modules:
  0.0 124.9 jit_solution(8410158026790315616)
XLA Ops:
  0.6 3.4 %pack.1 = bf16[8,176,1024]{2,1,0:T(8,128)(2,1)} custom-call(bf16[128,8192]{1,0:T(8,128)(2,1)} %bitcast.15, bf16[128,256]{1,0:T(8,128)(2,1)} %bitcast.17, f32[8,8192]{1,0:T(8,128)} %bitcast.11, bf16[8,8192]{1,0:T(8,128)(2,1)} %weight_ref.1, s32[16,128,128]{2,1,0:T(8,128)} %bitcast.16), custom_call_target="tpu_custom_call" | custom-call | tf_op jit(solution)/shard_map/pack/pallas_call | solution.py:98
  4.1 35.7 %all_to_all.25.joined_ref.side_ref = bf16[8,176,1024]{2,1,0:T(8,128)(2,1)S(1)} all-to-all(bf16[8,176,1024]{2,1,0:T(8,128)(2,1)} %pack.1), channel_id=1, replica_groups=mesh['z'=8,'core'=2,'yh'=4,'yl'=2,'x'=4] {'yl','x'}, dimensions={0} | all-to-all | bytes 5767168 | tf_op jit(solution)/shard_map/all_to_all | solution.py:301
  39.8 0.0 copy-start.1
  39.8 0.7 gradient.1
  40.5 24.0 %all_to_all.26.terms_ref = bf16[4,64,1024]{2,1,0:T(8,128)(2,1)S(1)} all-to-all(bf16[4,64,1024]{2,1,0:T(8,128)(2,1)S(1)} %bitcast.10), channel_id=1, replica_groups=mesh['z'=8,'core'=2,'yh'=4,'yl'=2,'x'=4] {'yh'}, dimensions={0} | all-to-all | bytes 1048576 | tf_op jit(solution)/shard_map/all_to_all | solution.py:301
  64.6 0.0 copy-done.1
  64.6 1.1 raise_and_pick.1
  65.7 22.6 %all_to_all.27.sent_ref = bf16[16,32,128]{2,1,0:T(8,128)(2,1)S(1)} all-to-all(bf16[16,32,128]{2,1,0:T(8,128)(2,1)S(1)} %get-tuple-element.7), channel_id=1, replica_groups=mesh['z'=8,'core'=2,'yh'=4,'yl'=2,'x'=4] {'z','core'}, dimensions={0} | all-to-all | bytes 262144 | tf_op jit(solution)/shard_map/all_to_all | solution.py:301
  88.3 0.2 update.1
  88.5 15.3 %all_to_all.28 = bf16[32,32,128]{2,1,0:T(8,128)(2,1)S(1)} all-to-all(bf16[32,32,128]{2,1,0:T(8,128)(2,1)S(1)} %update.1), channel_id=1, replica_groups=mesh['z'=8,'core'=2,'yh'=4,'yl'=2,'x'=4] {'z','yh'}, dimensions={0} | all-to-all | bytes 524288 | tf_op jit(solution)/shard_map/all_to_all | solution.py:301
  103.8 0.0 copy-start
  103.9 4.8 %collective-permute-start = (bf16[8,4,32,128]{3,2,1,0:T(8,128)(2,1)S(1)}, bf16[8,4,32,128]{3,2,1,0:T(8,128)(2,1)S(1)}, u32[]{:S(2)}, u32[]{:S(2)}) collective-permute-start(bf16[8,4,32,128]{3,2,1,0:T(8,128)(2,1)S(1)} %bitcast.13), channel_id=1, source_target_pairs={{0,32},{32,0},{1,33},{33,1},{2,34},{34,2},{3,35},{35,3},{4,36},{36... | collective-permute-start | bytes 786440 | tf_op jit(solution)/shard_map/ppermute | solution.py:324
  108.7 1.1 collective-permute-done.other_ref
  109.8 0.8 project.1
  110.6 13.6 %all_to_all.29.parts_ref = bf16[8,160,256]{2,1,0:T(8,128)(2,1)S(1)} all-to-all(bf16[8,160,256]{2,1,0:T(8,128)(2,1)S(1)} %project.1), channel_id=1, replica_groups=mesh['z'=8,'core'=2,'yh'=4,'yl'=2,'x'=4] {'yl','x'}, dimensions={0} | all-to-all | bytes 1310720 | tf_op jit(solution)/shard_map/all_to_all | solution.py:301
  124.1 0.0 copy-done
  124.1 0.8 finish.1
Async XLA Ops:
  39.8 24.8 %copy-start.1 = (f32[128,128]{1,0:T(8,128)S(1)}, f32[128,128]{1,0:T(8,128)}, u32[]{:S(2)}) copy-start(f32[128,128]{1,0:T(8,128)} %constant.2.clone.table_ref) | copy-start | bytes 196612
  103.8 20.3 %copy-start = (f32[1,8,8192]{2,1,0:T(8,128)S(1)}, f32[1,8,8192]{2,1,0:T(8,128)}, u32[]{:S(2)}) copy-start(f32[1,8,8192]{2,1,0:T(8,128)} %param.9) | copy-start | bytes 786436
  103.9 5.9 %collective-permute-start = (bf16[8,4,32,128]{3,2,1,0:T(8,128)(2,1)S(1)}, bf16[8,4,32,128]{3,2,1,0:T(8,128)(2,1)S(1)}, u32[]{:S(2)}, u32[]{:S(2)}) collective-permute-start(bf16[8,4,32,128]{3,2,1,0:T(8,128)(2,1)S(1)} %bitcast.13), channel_id=1, source_target_pairs={{0,32},{32,0},{1,33},{33,1},{2,34},{34,2},{3,35},{35,3},{4,36},{36... | collective-permute-start | bytes 786440 | tf_op jit(solution)/shard_map/ppermute | solution.py:324

commit v6 on v5

--- a/solution.py
+++ b/solution.py
@@ -50,7 +50,7 @@
     return pltpu.CompilerParams(vmem_limit_bytes=mib * MIB)
 
 
-def pack(tokens, cotangent, momentum, weight, kept, groups):
+def pack_all(tokens, cotangent, momentum, weight, kept, groups):
     tok, width = tokens.shape
     part = width // groups
     rows_all = cotangent.shape[1]
@@ -111,49 +111,169 @@
             pltpu.SemaphoreType.DMA((groups,)),
         ],
         compiler_params=params(62),
-        name="pack",
+        name="pack_all",
     )(tokens, cotangent, momentum, weight, kept)
 
 
-def gradient(joined, tok, rows_all):
-    groups, high, part = joined.shape
-    extra = high - tok - SIDE
-    fold = tok // extra
+def split_tokens(tokens, groups):
+    tok, width = tokens.shape
+    part = width // groups
+
+    def body(tok_ref, out_ref, sem):
+        moves = [
+            pltpu.make_async_copy(tok_ref.at[:, g * part:(g + 1) * part], out_ref.at[g], sem.at[g])
+            for g in range(groups)
+        ]
+        for move in moves:
+            move.start()
+        for move in moves:
+            move.wait()
+
+    return pl.pallas_call(
+        body,
+        in_specs=[pl.BlockSpec(memory_space=pl.ANY)],
+        out_specs=pl.BlockSpec(memory_space=pltpu.VMEM),
+        out_shape=jax.ShapeDtypeStruct((groups, tok, part), tokens.dtype),
+        scratch_shapes=[pltpu.SemaphoreType.DMA((groups,))],
+        compiler_params=params(),
+        name="split_tokens",
+    )(tokens)
+
+
+def pack_rest(cotangent, momentum, weight, kept, groups):
+    rows, width = momentum.shape
+    part = width // groups
+    tok, rows_all = cotangent.shape
+    fold = part // rows_all
+    extra = tok // fold
+    _, entries, blocks = kept.shape
+
+    def body(cot_ref, mom_ref, weight_ref, kept_ref, out_ref, cot_vmem, mom_vmem, weight_vmem, spots_ref, sem):
+        parts = [
+            pltpu.make_async_copy(kept_ref.at[lax.axis_index(SITE)], spots_ref, sem.at[0]),
+            pltpu.make_async_copy(mom_ref, mom_vmem, sem.at[1]),
+            pltpu.make_async_copy(weight_ref, weight_vmem, sem.at[2]),
+            pltpu.make_async_copy(cot_ref, cot_vmem, sem.at[3]),
+        ]
+        for fetch in parts:
+            fetch.start()
+        for fetch in parts:
+            fetch.wait()
+        z = lax.axis_index("z")
+        spots = spots_ref[...].astype(jnp.float32).T
+        unused = jnp.zeros((rows, part - 3 * 128), jnp.float32)
+        span = part // 64
+        for g in range(groups):
+            tile = weight_vmem[:, pl.ds(pl.multiple_of(g * part + z * 128, 128), 128)].astype(jnp.float32)
+            low = [spots[g * span + h * rows:g * span + (h + 1) * rows] for h in range(span // rows)]
+            low = jnp.concatenate(low + [tile, unused], axis=1)
+            side = jnp.concatenate([mom_vmem[:, g * part:(g + 1) * part], low], axis=0)
+            for q in range(fold):
+                out_ref[g, :extra, q * rows_all:(q + 1) * rows_all] = cot_vmem[q * extra:(q + 1) * extra, :]
+            out_ref[g, extra:, :] = side.astype(jnp.bfloat16)
+
+    anywhere = pl.BlockSpec(memory_space=pl.ANY)
+    return pl.pallas_call(
+        body,
+        in_specs=[anywhere] * 4,
+        out_specs=pl.BlockSpec(memory_space=pltpu.VMEM),
+        out_shape=jax.ShapeDtypeStruct((groups, extra + SIDE, part), jnp.bfloat16),
+        scratch_shapes=[
+            pltpu.VMEM((tok, rows_all), cotangent.dtype),
+            pltpu.VMEM((rows, width), jnp.float32),
+            pltpu.VMEM((rows, width), weight.dtype),
+            pltpu.VMEM((entries, blocks), jnp.int32),
+            pltpu.SemaphoreType.DMA((4,)),
+        ],
+        compiler_params=params(),
+        name="pack_rest",
+    )(cotangent, momentum, weight, kept)
+
+
+def follow(value, before):
+    def body(value_ref, before_ref, out_ref):
+        pass
+
+    anywhere = pl.BlockSpec(memory_space=pl.ANY)
+    return pl.pallas_call(
+        body,
+        in_specs=[anywhere] * 2,
+        out_specs=anywhere,
+        out_shape=jax.ShapeDtypeStruct(value.shape, value.dtype),
+        input_output_aliases={0: 0},
+        compiler_params=params(),
+        name="follow",
+    )(value, before)
+
+
+def gradient(arrays, tok, rows_all):
+    groups, _, part = arrays[0].shape
+    fold = part // rows_all
+    extra = tok // fold
     cols = 256
-
-    def body(joined_ref, out_ref):
+    start = tok if len(arrays) == 1 else 0
+
+    def body(*refs):
+        tok_ref, rest_ref = refs[0], refs[len(arrays) - 1]
+        out_ref, tok_out, side_out, sem = refs[len(arrays):]
+        moves = [
+            pltpu.make_async_copy(tok_ref.at[:, :tok, :], tok_out, sem.at[0]),
+            pltpu.make_async_copy(rest_ref.at[:, start + extra:, :], side_out, sem.at[1]),
+        ]
+        for move in moves:
+            move.start()
         left = jnp.concatenate(
             [
-                joined_ref[k, tok:tok + extra, q * rows_all:(q + 1) * rows_all]
+                rest_ref[k, start:start + extra, q * rows_all:(q + 1) * rows_all]
                 for k in range(groups)
                 for q in range(fold)
             ],
             axis=0,
         ).T
         for j in range(0, part, cols):
-            right = jnp.concatenate([joined_ref[k, :tok, j:j + cols] for k in range(groups)], axis=0)
+            right = jnp.concatenate([tok_ref[k, :tok, j:j + cols] for k in range(groups)], axis=0)
             out_ref[:, j:j + cols] = jnp.dot(
                 left, right, preferred_element_type=jnp.float32
             ).astype(out_ref.dtype)
-
-    return pl.pallas_call(
-        body,
-        out_shape=jax.ShapeDtypeStruct((rows_all, part), jnp.bfloat16),
+        for move in moves:
+            move.wait()
+
+    whole = pl.BlockSpec(memory_space=pltpu.VMEM)
+    anywhere = pl.BlockSpec(memory_space=pl.ANY)
+    return pl.pallas_call(
+        body,
+        in_specs=[whole] * len(arrays),
+        out_specs=(whole, anywhere, anywhere),
+        out_shape=(
+            jax.ShapeDtypeStruct((rows_all, part), jnp.bfloat16),
+            jax.ShapeDtypeStruct((groups, tok, part), jnp.bfloat16),
+            jax.ShapeDtypeStruct((groups, SIDE, part), jnp.bfloat16),
+        ),
+        scratch_shapes=[pltpu.SemaphoreType.DMA((2,))],
         compiler_params=params(),
         name="gradient",
-    )(joined)
-
-
-def raise_and_pick(terms, joined, table, sites, rows_all, nx):
+    )(*arrays)
+
+
+def raise_and_pick(terms, side, held_tokens, table, sites, rows_all, nx):
     nyh, band, part = terms.shape
-    groups, high, _ = joined.shape
+    groups = side.shape[0]
     tiles = part // 128
     rows = band // groups
     fold = part // rows_all
     span = part // 64
 
-    def body(terms_ref, side_ref, table_ref, sent_ref, change_ref, held_ref, keep_ref, moment_ref):
+    def body(terms_hbm, side_hbm, tok_hbm, table_ref, sent_ref, change_ref, held_ref, tok_ref, keep_ref, moment_ref,
+             terms_ref, side_ref, sem):
+        fetches = [
+            pltpu.make_async_copy(side_hbm, side_ref, sem.at[0]),
+            pltpu.make_async_copy(terms_hbm, terms_ref, sem.at[1]),
+            pltpu.make_async_copy(tok_hbm, tok_ref, sem.at[2]),
+        ]
+        for fetch in fetches:
+            fetch.start()
         core = lax.axis_index("core")
+        fetches[0].wait()
         freq = iota((64, 128), 0).astype(jnp.float32)
         gather = iota((rows, 128), 0) == iota((rows, 128), 1) // (128 // rows)
         gather = jnp.where(gather, 1.0, 0.0).astype(jnp.bfloat16)
@@ -174,6 +294,7 @@
             side = side_ref[core * nx + x].astype(jnp.float32)
             held_ref[x * rows:(x + 1) * rows, :] = side[rows:2 * rows, span // rows * 128:(span // rows + 1) * 128]
 
+        fetches[1].wait()
         grad = terms_ref[0].astype(jnp.float32)
         for k in range(1, nyh):
             grad = grad + terms_ref[k].astype(jnp.float32)
@@ -191,29 +312,25 @@
                     across.append(change[at:at + rows])
                 pieces.append(jnp.concatenate(across, axis=1))
             change_ref[g] = jnp.concatenate(pieces, axis=0).astype(jnp.bfloat16)
-
-    def whole(*shape):
-        return pl.BlockSpec(shape, lambda i: (0,) * len(shape))
-
+        fetches[2].wait()
+
+    whole = pl.BlockSpec(memory_space=pltpu.VMEM)
     share = tiles * band // sites
     return pl.pallas_call(
         body,
-        grid=(1,),
-        in_specs=[
-            whole(nyh, band, part),
-            pl.BlockSpec((groups, SIDE, part), lambda i: (0, high // SIDE - 1, 0)),
-            whole(128, 128),
-        ],
-        out_specs=(whole(sites, share, 128), whole(groups, fold * rows, rows_all), whole(nx * rows, 128)),
+        in_specs=[pl.BlockSpec(memory_space=pl.ANY)] * 3 + [whole],
+        out_specs=(whole,) * 4,
         out_shape=(
             jax.ShapeDtypeStruct((sites, share, 128), jnp.bfloat16),
             jax.ShapeDtypeStruct((groups, fold * rows, rows_all), jnp.bfloat16),
             jax.ShapeDtypeStruct((nx * rows, 128), jnp.float32),
+            jax.ShapeDtypeStruct(held_tokens.shape, jnp.bfloat16),
         ),
-        scratch_shapes=[pltpu.VMEM((tiles * band, 128), jnp.float32)] * 2,
+        scratch_shapes=[pltpu.VMEM((tiles * band, 128), jnp.float32)] * 2
+        + [pltpu.VMEM(terms.shape, terms.dtype), pltpu.VMEM(side.shape, side.dtype), pltpu.SemaphoreType.DMA((3,))],
         compiler_params=params(),
         name="raise_and_pick",
-    )(terms, joined, table)
+    )(terms, side, held_tokens, table)
 
 
 def update(sent, held, table, copies):
@@ -235,13 +352,13 @@
     )(sent, held, table)
 
 
-def project(joined, mine, other, change, tok):
-    groups, _, part = joined.shape
+def project(tokens, mine, other, change):
+    groups, tok, part = tokens.shape
     tiles, nyh, share, _ = mine.shape
     rows_all = 2 * nyh * share
     extra = change.shape[1]
 
-    def body(joined_ref, mine_ref, other_ref, change_ref, out_ref):
+    def body(tok_ref, mine_ref, other_ref, change_ref, out_ref):
         first = lax.axis_index("core") == 0
         weight = []
         for t in range(tiles):
@@ -253,7 +370,7 @@
         weight = jnp.concatenate(weight, axis=1)
         weight = weight.T
         for k in range(0, groups, 2):
-            both = jnp.concatenate([joined_ref[k, :tok, :], joined_ref[k + 1, :tok, :]], axis=0)
+            both = jnp.concatenate([tok_ref[k], tok_ref[k + 1]], axis=0)
             both = jnp.dot(both, weight, preferred_element_type=jnp.float32).astype(out_ref.dtype)
             out_ref[k, :tok, :] = both[:tok]
             out_ref[k + 1, :tok, :] = both[tok:]
@@ -265,7 +382,7 @@
         out_shape=jax.ShapeDtypeStruct((groups, tok + extra, rows_all), jnp.bfloat16),
         compiler_params=params(),
         name="project",
-    )(joined, mine, other, change)
+    )(tokens, mine, other, change)
 
 
 def finish(parts, momentum, tok):
@@ -313,16 +430,27 @@
     table = jnp.asarray(pair_table())
 
     kept = kept_index.transpose(0, 1, 3, 2).reshape(sites, -1, width // 64)
-    joined = exchange(pack(tokens[0], cotangent[0], momentum[0], weight, kept, groups), GROUP)
-
-    partial = gradient(joined, tok, rows_all)
-    terms = exchange(partial.reshape(nyh, band, part), "yh")
-    sent, change, held = raise_and_pick(terms, joined, table, sites, rows_all, nx)
+
+    def reduce_rows(arrays):
+        partial, held_tokens, side = gradient(arrays, tok, rows_all)
+        return held_tokens, exchange(partial.reshape(nyh, band, part), "yh"), side
+
+    def in_one(tokens, cotangent, momentum, weight, kept):
+        return reduce_rows([exchange(pack_all(tokens, cotangent, momentum, weight, kept, groups), GROUP)])
+
+    def in_two(tokens, cotangent, momentum, weight, kept):
+        rest = exchange(pack_rest(cotangent, momentum, weight, kept, groups), GROUP)
+        return reduce_rows([exchange(follow(split_tokens(tokens, groups), rest), GROUP), rest])
+
+    held_tokens, terms, side = lax.cond(
+        lax.axis_index("core") == 0, in_one, in_two, tokens[0], cotangent[0], momentum[0], weight, kept
+    )
+    sent, change, held, held_tokens = raise_and_pick(terms, side, held_tokens, table, sites, rows_all, nx)
 
     fresh = update(exchange(sent, SITE), held, table, nz * nyh)
     mine = exchange(fresh, ("z", "yh")).reshape(nz, nyh, band // ncore, 128)
     other = lax.ppermute(mine, "core", [(0, 1), (1, 0)])
-    scores, moment_new = finish(exchange(project(joined, mine, other, change, tok), GROUP), momentum[0], tok)
+    scores, moment_new = finish(exchange(project(held_tokens, mine, other, change), GROUP), momentum[0], tok)
     return (scores[None], moment_new[None])
 
 

time: 125 us -> 122 us (0.976)
  blocking collectives: 111 us -> 93.7 us
  waiting for transfers between devices: 1.14 us -> 7.89 us
  starting transfers between devices: 4.8 us -> 10.7 us
  Pallas kernels: 7.07 us -> 8.43 us
    all_to_all x5, blocking collectives: 111 us -> 93.7 us  [exchange(): return lax.all_to_all(value, axes, 0, 0, tiled=True)]
    all_to_all x0 -> x1, waiting for transfers between devices: none -> 6.75 us  [exchange(): return lax.all_to_all(value, axes, 0, 0, tiled=True)]
    all_to_all x0 -> x1, starting transfers between devices: none -> 5.87 us  [exchange(): return lax.all_to_all(value, axes, 0, 0, tiled=True)]
    pallas_call x3 -> x5, Pallas kernels: 5.33 us -> 6.67 us  [the longest x1 2.08 us: pack_rest(): pl.pallas_call(body, in_specs=[anywhere] * 4, out_specs=pl.BlockSpec(memo...]
  transfers between devices with their start and end apart: 1 -> 2, of which waited for: 1 -> 2; matrix products, arithmetic and copies ran while one was open for 0% -> 0% of each run, Pallas kernels for 0% -> 1%
where the time goes in v6:
time: 122 us; the launch traced here: 121 us
  blocking collectives  93.7 us (77%)
  starting transfers between devices  10.7 us (9%)
  Pallas kernels  8.43 us (7%)
  waiting for transfers between devices  7.89 us (6%)
    all_to_all x5, blocking collectives, exchange(): return lax.all_to_all(value, axes, 0, 0, tiled=True)  93.7 us
    all_to_all x1, waiting for transfers between devices, exchange(): return lax.all_to_all(value, axes, 0, 0, tiled=True)  6.75 us
    all_to_all x1, starting transfers between devices, exchange(): return lax.all_to_all(value, axes, 0, 0, tiled=True)  5.87 us
    ppermute x1, starting transfers between devices, shards(): other = lax.ppermute(mine, 'core', [(0, 1), (1, 0)])  4.84 us
  transfers between devices with their start and end apart: 2, of which 2 were waited for; matrix products, arithmetic and copies ran while one was open for 0% of the time, Pallas kernels for 1%

profile of v6, /device:TPU:1, one launch (start us, length us, event | category | flops | bytes accessed | tf_op | source)
XLA Modules:
  0.0 121.4 jit_solution(4864998983723650421)
XLA Ops:
  0.6 0.0 copy-start
  0.6 66.3 %conditional.1 = (bf16[8,128,1024]{2,1,0:T(8,128)(2,1)}, bf16[4,64,1024]{2,1,0:T(8,128)(2,1)S(1)}, bf16[8,16,1024]{2,1,0:T(8,128)(2,1)S(1)}) conditional(s32[]{:T(128)} %convert_element_type.3, (bf16[128,8192]{1,0:T(8,128)(2,1)}, bf16[128,256]{1,0:T(8,128)(2,1)}, f32[8,8192]{1,0:T(8,128)}, bf16[8,8192]{1,0:T(8,128)(2,1)}, ...), branch_computations={%region_0.0_spmd, %region_1.0_spmd} | conditional | bytes 7602232 | solution.py:445
  0.7 2.1 %pack_rest.1 = bf16[8,48,1024]{2,1,0:T(8,128)(2,1)} custom-call(bf16[128,256]{1,0:T(8,128)(2,1)} %get-tuple-element.21.cot_ref, f32[8,8192]{1,0:T(8,128)} %get-tuple-element.22.mom_ref, bf16[8,8192]{1,0:T(8,128)(2,1)} %get-tuple-element.23.weight_ref, s32[16,128,128]{2,1,0:T(8,128)} %get-tuple-element.24.kept_ref), custom_call_target="tpu_custom_call" | custom-call | tf_op jit(solution)/shard_map/cond/branch_0_fun/pack_rest/pallas_call | solution.py:176
  2.7 5.9 %all-to-all-start = ((bf16[8,48,1024]{2,1,0:T(8,128)(2,1)}), bf16[8,48,1024]{2,1,0:T(8,128)(2,1)S(1)}, u32[]{:S(2)}, u32[]{:S(2)}) async-start(bf16[8,48,1024]{2,1,0:T(8,128)(2,1)} %pack_rest.1), calls=%async_computation | async-start | bytes 1572864 | tf_op jit(solution)/shard_map/cond/branch_0_fun/all_to_all | solution.py:418
  8.6 1.6 %split_tokens.1.value_ref = bf16[8,128,1024]{2,1,0:T(8,128)(2,1)S(1)} custom-call(bf16[128,8192]{1,0:T(8,128)(2,1)} %get-tuple-element.20.tok_ref), custom_call_target="tpu_custom_call" | custom-call | tf_op jit(solution)/shard_map/cond/branch_0_fun/split_tokens/pallas_call | solution.py:132
  10.2 6.7 %all-to-all-done.before_ref.refs_1_ = bf16[8,48,1024]{2,1,0:T(8,128)(2,1)S(1)} async-done(((bf16[8,48,1024]{2,1,0:T(8,128)(2,1)}), bf16[8,48,1024]{2,1,0:T(8,128)(2,1)S(1)}, u32[]{:S(2)}, u32[]{:S(2)}) %all-to-all-start) | async-done | bytes 786464 | tf_op jit(solution)/shard_map/cond/branch_0_fun/all_to_all | solution.py:418
  17.0 29.2 %all_to_all.35.refs_0_ = bf16[8,128,1024]{2,1,0:T(8,128)(2,1)S(1)} all-to-all(bf16[8,128,1024]{2,1,0:T(8,128)(2,1)S(1)} %follow.1), channel_id=1, replica_groups=mesh['z'=8,'core'=2,'yh'=4,'yl'=2,'x'=4] {'yl','x'}, dimensions={0} | all-to-all | bytes 4194304 | tf_op jit(solution)/shard_map/cond/branch_0_fun/all_to_all | solution.py:418
  46.2 1.3 %gradient.2 = (bf16[256,1024]{1,0:T(8,128)(2,1)S(1)}, bf16[8,128,1024]{2,1,0:T(8,128)(2,1)}, bf16[8,16,1024]{2,1,0:T(8,128)(2,1)S(1)}) custom-call(bf16[8,128,1024]{2,1,0:T(8,128)(2,1)S(1)} %all_to_all.35.refs_0_, bf16[8,48,1024]{2,1,0:T(8,128)(2,1)S(1)} %all-to-all-done.before_ref.refs_1_), custom_call_target="tpu_custom_call" | custom-call | tf_op jit(solution)/shard_map/cond/branch_0_fun/gradient/pallas_call | solution.py:243
  47.5 19.4 %all_to_all.36 = bf16[4,64,1024]{2,1,0:T(8,128)(2,1)S(1)} all-to-all(bf16[4,64,1024]{2,1,0:T(8,128)(2,1)S(1)} %bitcast.13), channel_id=1, replica_groups=mesh['z'=8,'core'=2,'yh'=4,'yl'=2,'x'=4] {'yh'}, dimensions={0} | all-to-all | bytes 1048576 | tf_op jit(solution)/shard_map/cond/branch_0_fun/all_to_all | solution.py:418
  66.9 0.0 copy-done
  66.9 1.7 %raise_and_pick.1 = (bf16[16,32,128]{2,1,0:T(8,128)(2,1)S(1)}, bf16[8,32,256]{2,1,0:T(8,128)(2,1)S(1)}, f32[32,128]{1,0:T(8,128)S(1)}, bf16[8,128,1024]{2,1,0:T(8,128)(2,1)S(1)}) custom-call(bf16[4,64,1024]{2,1,0:T(8,128)(2,1)S(1)} %get-tuple-element.47.terms_hbm, bf16[8,16,1024]{2,1,0:T(8,128)(2,1)S(1)} %get-tuple-element.48.side_hbm, ...), custom_call_target="tpu_custom_call" | custom-call | tf_op jit(solution)/shard_map/raise_and_pick/pallas_call | solution.py:319
  68.6 16.2 %all_to_all.39.sent_ref = bf16[16,32,128]{2,1,0:T(8,128)(2,1)S(1)} all-to-all(bf16[16,32,128]{2,1,0:T(8,128)(2,1)S(1)} %get-tuple-element.51), channel_id=1, replica_groups=mesh['z'=8,'core'=2,'yh'=4,'yl'=2,'x'=4] {'z','core'}, dimensions={0} | all-to-all | bytes 262144 | tf_op jit(solution)/shard_map/all_to_all | solution.py:418
  84.8 0.2 update.1
  85.0 15.1 %all_to_all.40 = bf16[32,32,128]{2,1,0:T(8,128)(2,1)S(1)} all-to-all(bf16[32,32,128]{2,1,0:T(8,128)(2,1)S(1)} %update.1), channel_id=1, replica_groups=mesh['z'=8,'core'=2,'yh'=4,'yl'=2,'x'=4] {'z','yh'}, dimensions={0} | all-to-all | bytes 524288 | tf_op jit(solution)/shard_map/all_to_all | solution.py:418
  100.1 4.8 %collective-permute-start = (bf16[8,4,32,128]{3,2,1,0:T(8,128)(2,1)S(1)}, bf16[8,4,32,128]{3,2,1,0:T(8,128)(2,1)S(1)}, u32[]{:S(2)}, u32[]{:S(2)}) collective-permute-start(bf16[8,4,32,128]{3,2,1,0:T(8,128)(2,1)S(1)} %bitcast.11), channel_id=1, source_target_pairs={{0,32},{32,0},{1,33},{33,1},{2,34},{34,2},{3,35},{35,3},{4,36},{36... | collective-permute-start | bytes 786440 | tf_op jit(solution)/shard_map/ppermute | solution.py:452
  104.9 1.1 collective-permute-done.other_ref
  106.1 0.0 copy-start.1
  106.1 0.8 project.1
  106.8 13.8 %all_to_all.41.parts_ref = bf16[8,160,256]{2,1,0:T(8,128)(2,1)S(1)} all-to-all(bf16[8,160,256]{2,1,0:T(8,128)(2,1)S(1)} %project.1), channel_id=1, replica_groups=mesh['z'=8,'core'=2,'yh'=4,'yl'=2,'x'=4] {'yl','x'}, dimensions={0} | all-to-all | bytes 1310720 | tf_op jit(solution)/shard_map/all_to_all | solution.py:418
  120.6 0.0 copy-done.1
  120.6 0.8 finish.1
  (1 shorter events, 0.0 us)
Async XLA Ops:
  0.6 66.3 %copy-start = (f32[128,128]{1,0:T(8,128)S(1)}, f32[128,128]{1,0:T(8,128)}, u32[]{:S(2)}) copy-start(f32[128,128]{1,0:T(8,128)} %constant.10.clone.table_ref) | copy-start | bytes 196612
  2.7 14.2 %all-to-all-start = ((bf16[8,48,1024]{2,1,0:T(8,128)(2,1)}), bf16[8,48,1024]{2,1,0:T(8,128)(2,1)S(1)}, u32[]{:S(2)}, u32[]{:S(2)}) async-start(bf16[8,48,1024]{2,1,0:T(8,128)(2,1)} %pack_rest.1), calls=%async_computation | async-start | bytes 1572864 | tf_op jit(solution)/shard_map/cond/branch_0_fun/all_to_all | solution.py:418
  100.1 6.0 %collective-permute-start = (bf16[8,4,32,128]{3,2,1,0:T(8,128)(2,1)S(1)}, bf16[8,4,32,128]{3,2,1,0:T(8,128)(2,1)S(1)}, u32[]{:S(2)}, u32[]{:S(2)}) collective-permute-start(bf16[8,4,32,128]{3,2,1,0:T(8,128)(2,1)S(1)} %bitcast.11), channel_id=1, source_target_pairs={{0,32},{32,0},{1,33},{33,1},{2,34},{34,2},{3,35},{35,3},{4,36},{36... | collective-permute-start | bytes 786440 | tf_op jit(solution)/shard_map/ppermute | solution.py:452
  106.1 14.6 %copy-start.1 = (f32[1,8,8192]{2,1,0:T(8,128)S(1)}, f32[1,8,8192]{2,1,0:T(8,128)}, u32[]{:S(2)}) copy-start(f32[1,8,8192]{2,1,0:T(8,128)} %param.11) | copy-start | bytes 786436

commit v7 on v6

--- a/solution.py
+++ b/solution.py
@@ -13,6 +13,7 @@
 DEV = ("yh", "yl", "x")
 MIB = 1024 * 1024
 ACROSS = (((1,), (1,)), ((), ()))
+LEAD = 32
 SIDE = 16
 
 
@@ -121,7 +122,7 @@
 
     def body(tok_ref, out_ref, sem):
         moves = [
-            pltpu.make_async_copy(tok_ref.at[:, g * part:(g + 1) * part], out_ref.at[g], sem.at[g])
+            pltpu.make_async_copy(tok_ref.at[LEAD:, g * part:(g + 1) * part], out_ref.at[g], sem.at[g])
             for g in range(groups)
         ]
         for move in moves:
@@ -133,14 +134,14 @@
         body,
         in_specs=[pl.BlockSpec(memory_space=pl.ANY)],
         out_specs=pl.BlockSpec(memory_space=pltpu.VMEM),
-        out_shape=jax.ShapeDtypeStruct((groups, tok, part), tokens.dtype),
+        out_shape=jax.ShapeDtypeStruct((groups, tok - LEAD, part), tokens.dtype),
         scratch_shapes=[pltpu.SemaphoreType.DMA((groups,))],
         compiler_params=params(),
         name="split_tokens",
     )(tokens)
 
 
-def pack_rest(cotangent, momentum, weight, kept, groups):
+def pack_rest(tokens, cotangent, momentum, weight, kept, groups):
     rows, width = momentum.shape
     part = width // groups
     tok, rows_all = cotangent.shape
@@ -148,14 +149,20 @@
     extra = tok // fold
     _, entries, blocks = kept.shape
 
-    def body(cot_ref, mom_ref, weight_ref, kept_ref, out_ref, cot_vmem, mom_vmem, weight_vmem, spots_ref, sem):
+    def body(tok_ref, cot_ref, mom_ref, weight_ref, kept_ref, out_ref, cot_vmem, mom_vmem, weight_vmem, spots_ref, sem):
         parts = [
             pltpu.make_async_copy(kept_ref.at[lax.axis_index(SITE)], spots_ref, sem.at[0]),
             pltpu.make_async_copy(mom_ref, mom_vmem, sem.at[1]),
             pltpu.make_async_copy(weight_ref, weight_vmem, sem.at[2]),
             pltpu.make_async_copy(cot_ref, cot_vmem, sem.at[3]),
         ]
-        for fetch in parts:
+        leads = [
+            pltpu.make_async_copy(
+                tok_ref.at[:LEAD, g * part:(g + 1) * part], out_ref.at[g, :LEAD, :], sem.at[4 + g]
+            )
+            for g in range(groups)
+        ]
+        for fetch in parts + leads:
             fetch.start()
         for fetch in parts:
             fetch.wait()
@@ -169,25 +176,27 @@
             low = jnp.concatenate(low + [tile, unused], axis=1)
             side = jnp.concatenate([mom_vmem[:, g * part:(g + 1) * part], low], axis=0)
             for q in range(fold):
-                out_ref[g, :extra, q * rows_all:(q + 1) * rows_all] = cot_vmem[q * extra:(q + 1) * extra, :]
-            out_ref[g, extra:, :] = side.astype(jnp.bfloat16)
+                out_ref[g, LEAD:LEAD + extra, q * rows_all:(q + 1) * rows_all] = cot_vmem[q * extra:(q + 1) * extra, :]
+            out_ref[g, LEAD + extra:, :] = side.astype(jnp.bfloat16)
+        for lead in leads:
+            lead.wait()
 
     anywhere = pl.BlockSpec(memory_space=pl.ANY)
     return pl.pallas_call(
         body,
-        in_specs=[anywhere] * 4,
+        in_specs=[anywhere] * 5,
         out_specs=pl.BlockSpec(memory_space=pltpu.VMEM),
-        out_shape=jax.ShapeDtypeStruct((groups, extra + SIDE, part), jnp.bfloat16),
+        out_shape=jax.ShapeDtypeStruct((groups, LEAD + extra + SIDE, part), jnp.bfloat16),
         scratch_shapes=[
             pltpu.VMEM((tok, rows_all), cotangent.dtype),
             pltpu.VMEM((rows, width), jnp.float32),
             pltpu.VMEM((rows, width), weight.dtype),
             pltpu.VMEM((entries, blocks), jnp.int32),
-            pltpu.SemaphoreType.DMA((4,)),
+            pltpu.SemaphoreType.DMA((4 + groups,)),
         ],
         compiler_params=params(),
         name="pack_rest",
-    )(cotangent, momentum, weight, kept)
+    )(tokens, cotangent, momentum, weight, kept)
 
 
 def follow(value, before):
@@ -211,15 +220,18 @@
     fold = part // rows_all
     extra = tok // fold
     cols = 256
-    start = tok if len(arrays) == 1 else 0
+    lead = 0 if len(arrays) == 1 else LEAD
+    start = lead or tok
 
     def body(*refs):
         tok_ref, rest_ref = refs[0], refs[len(arrays) - 1]
         out_ref, tok_out, side_out, sem = refs[len(arrays):]
         moves = [
-            pltpu.make_async_copy(tok_ref.at[:, :tok, :], tok_out, sem.at[0]),
+            pltpu.make_async_copy(tok_ref.at[:, :tok - lead, :], tok_out.at[:, lead:, :], sem.at[0]),
             pltpu.make_async_copy(rest_ref.at[:, start + extra:, :], side_out, sem.at[1]),
         ]
+        if lead:
+            moves.append(pltpu.make_async_copy(rest_ref.at[:, :lead, :], tok_out.at[:, :lead, :], sem.at[2]))
         for move in moves:
             move.start()
         left = jnp.concatenate(
@@ -231,9 +243,11 @@
             axis=0,
         ).T
         for j in range(0, part, cols):
-            right = jnp.concatenate([tok_ref[k, :tok, j:j + cols] for k in range(groups)], axis=0)
+            right = []
+            for k in range(groups):
+                right += [rest_ref[k, :lead, j:j + cols]] * (lead > 0) + [tok_ref[k, :tok - lead, j:j + cols]]
             out_ref[:, j:j + cols] = jnp.dot(
-                left, right, preferred_element_type=jnp.float32
+                left, jnp.concatenate(right, axis=0), preferred_element_type=jnp.float32
             ).astype(out_ref.dtype)
         for move in moves:
             move.wait()
@@ -249,7 +263,7 @@
             jax.ShapeDtypeStruct((groups, tok, part), jnp.bfloat16),
             jax.ShapeDtypeStruct((groups, SIDE, part), jnp.bfloat16),
         ),
-        scratch_shapes=[pltpu.SemaphoreType.DMA((2,))],
+        scratch_shapes=[pltpu.SemaphoreType.DMA((3,))],
         compiler_params=params(),
         name="gradient",
     )(*arrays)
@@ -439,7 +453,7 @@
         return reduce_rows([exchange(pack_all(tokens, cotangent, momentum, weight, kept, groups), GROUP)])
 
     def in_two(tokens, cotangent, momentum, weight, kept):
-        rest = exchange(pack_rest(cotangent, momentum, weight, kept, groups), GROUP)
+        rest = exchange(pack_rest(tokens, cotangent, momentum, weight, kept, groups), GROUP)
         return reduce_rows([exchange(follow(split_tokens(tokens, groups), rest), GROUP), rest])
 
     held_tokens, terms, side = lax.cond(

time: 122 us -> 121 us (level)
  blocking collectives: 93.7 us -> 88.9 us
  waiting for transfers between devices: 7.89 us -> 11.4 us
    all_to_all x5, blocking collectives: 93.7 us -> 88.9 us  [exchange(): return lax.all_to_all(value, axes, 0, 0, tiled=True)]
    all_to_all x1, waiting for transfers between devices: 6.75 us -> 10.3 us  [exchange(): return lax.all_to_all(value, axes, 0, 0, tiled=True)]
where the time goes in v7:
time: 121 us; the launch traced here: 120 us
  blocking collectives  88.9 us (73%)
  waiting for transfers between devices  11.4 us (9%)
  starting transfers between devices  10.6 us (9%)
  Pallas kernels  8.71 us (7%)
    all_to_all x5, blocking collectives, exchange(): return lax.all_to_all(value, axes, 0, 0, tiled=True)  88.9 us
    all_to_all x1, waiting for transfers between devices, exchange(): return lax.all_to_all(value, axes, 0, 0, tiled=True)  10.3 us
    all_to_all x1, starting transfers between devices, exchange(): return lax.all_to_all(value, axes, 0, 0, tiled=True)  5.87 us
    ppermute x1, starting transfers between devices, shards(): other = lax.ppermute(mine, 'core', [(0, 1), (1, 0)])  4.76 us
  transfers between devices with their start and end apart: 2, of which 2 were waited for; matrix products, arithmetic and copies ran while one was open for 0% of the time, Pallas kernels for 1%

profile of v7, /device:TPU:1, one launch (start us, length us, event | category | flops | bytes accessed | tf_op | source)
XLA Modules:
  0.0 120.4 jit_solution(13616593020297701767)
XLA Ops:
  0.6 0.0 copy-start
  0.6 63.0 %conditional.1 = (bf16[8,128,1024]{2,1,0:T(8,128)(2,1)}, bf16[4,64,1024]{2,1,0:T(8,128)(2,1)S(1)}, bf16[8,16,1024]{2,1,0:T(8,128)(2,1)S(1)}) conditional(s32[]{:T(128)} %convert_element_type.3, (bf16[128,8192]{1,0:T(8,128)(2,1)}, bf16[128,256]{1,0:T(8,128)(2,1)}, f32[8,8192]{1,0:T(8,128)}, bf16[8,8192]{1,0:T(8,128)(2,1)}, ...), branch_computations={%region_0.0_spmd, %region_1.0_spmd} | conditional | bytes 8126520 | solution.py:459
  0.7 2.4 %pack_rest.1 = bf16[8,80,1024]{2,1,0:T(8,128)(2,1)} custom-call(bf16[128,8192]{1,0:T(8,128)(2,1)} %get-tuple-element.20.tok_ref, bf16[128,256]{1,0:T(8,128)(2,1)} %get-tuple-element.21.cot_ref, f32[8,8192]{1,0:T(8,128)} %get-tuple-element.22.mom_ref, bf16[8,8192]{1,0:T(8,128)(2,1)} %get-tuple-element.23.weight_ref, s32[16,128,128]{2,1,0:T(8,128)} %get-tuple-element.24.kept_ref), custom_call_target="tpu_custom_call" | custom-call | tf_op jit(solution)/shard_map/cond/branch_0_fun/pack_rest/pallas_call | solution.py:185
  3.1 5.9 %all-to-all-start = ((bf16[8,80,1024]{2,1,0:T(8,128)(2,1)}), bf16[8,80,1024]{2,1,0:T(8,128)(2,1)S(1)}, u32[]{:S(2)}, u32[]{:S(2)}) async-start(bf16[8,80,1024]{2,1,0:T(8,128)(2,1)} %pack_rest.1), calls=%async_computation | async-start | bytes 2621440 | tf_op jit(solution)/shard_map/cond/branch_0_fun/all_to_all | solution.py:432
  9.0 1.5 %split_tokens.1.value_ref = bf16[8,96,1024]{2,1,0:T(8,128)(2,1)S(1)} custom-call(bf16[128,8192]{1,0:T(8,128)(2,1)} %get-tuple-element.20.tok_ref), custom_call_target="tpu_custom_call" | custom-call | tf_op jit(solution)/shard_map/cond/branch_0_fun/split_tokens/pallas_call | solution.py:133
  10.5 10.3 %all-to-all-done.before_ref.refs_1_ = bf16[8,80,1024]{2,1,0:T(8,128)(2,1)S(1)} async-done(((bf16[8,80,1024]{2,1,0:T(8,128)(2,1)}), bf16[8,80,1024]{2,1,0:T(8,128)(2,1)S(1)}, u32[]{:S(2)}, u32[]{:S(2)}) %all-to-all-start) | async-done | bytes 1310752 | tf_op jit(solution)/shard_map/cond/branch_0_fun/all_to_all | solution.py:432
  20.7 24.1 %all_to_all.35.refs_0_ = bf16[8,96,1024]{2,1,0:T(8,128)(2,1)S(1)} all-to-all(bf16[8,96,1024]{2,1,0:T(8,128)(2,1)S(1)} %follow.1), channel_id=1, replica_groups=mesh['z'=8,'core'=2,'yh'=4,'yl'=2,'x'=4] {'yl','x'}, dimensions={0} | all-to-all | bytes 3145728 | tf_op jit(solution)/shard_map/cond/branch_0_fun/all_to_all | solution.py:432
  44.8 1.3 %gradient.2 = (bf16[256,1024]{1,0:T(8,128)(2,1)S(1)}, bf16[8,128,1024]{2,1,0:T(8,128)(2,1)}, bf16[8,16,1024]{2,1,0:T(8,128)(2,1)S(1)}) custom-call(bf16[8,96,1024]{2,1,0:T(8,128)(2,1)S(1)} %all_to_all.35.refs_0_, bf16[8,80,1024]{2,1,0:T(8,128)(2,1)S(1)} %all-to-all-done.before_ref.refs_1_), custom_call_target="tpu_custom_call" | custom-call | tf_op jit(solution)/shard_map/cond/branch_0_fun/gradient/pallas_call | solution.py:257
  46.2 17.5 %all_to_all.36 = bf16[4,64,1024]{2,1,0:T(8,128)(2,1)S(1)} all-to-all(bf16[4,64,1024]{2,1,0:T(8,128)(2,1)S(1)} %bitcast.13), channel_id=1, replica_groups=mesh['z'=8,'core'=2,'yh'=4,'yl'=2,'x'=4] {'yh'}, dimensions={0} | all-to-all | bytes 1048576 | tf_op jit(solution)/shard_map/cond/branch_0_fun/all_to_all | solution.py:432
  63.7 0.0 copy-done
  63.7 1.7 %raise_and_pick.1 = (bf16[16,32,128]{2,1,0:T(8,128)(2,1)S(1)}, bf16[8,32,256]{2,1,0:T(8,128)(2,1)S(1)}, f32[32,128]{1,0:T(8,128)S(1)}, bf16[8,128,1024]{2,1,0:T(8,128)(2,1)S(1)}) custom-call(bf16[4,64,1024]{2,1,0:T(8,128)(2,1)S(1)} %get-tuple-element.47.terms_hbm, bf16[8,16,1024]{2,1,0:T(8,128)(2,1)S(1)} %get-tuple-element.48.side_hbm, ...), custom_call_target="tpu_custom_call" | custom-call | tf_op jit(solution)/shard_map/raise_and_pick/pallas_call | solution.py:333
  65.3 18.4 %all_to_all.39.sent_ref = bf16[16,32,128]{2,1,0:T(8,128)(2,1)S(1)} all-to-all(bf16[16,32,128]{2,1,0:T(8,128)(2,1)S(1)} %get-tuple-element.51), channel_id=1, replica_groups=mesh['z'=8,'core'=2,'yh'=4,'yl'=2,'x'=4] {'z','core'}, dimensions={0} | all-to-all | bytes 262144 | tf_op jit(solution)/shard_map/all_to_all | solution.py:432
  83.7 0.2 update.1
  83.9 15.5 %all_to_all.40 = bf16[32,32,128]{2,1,0:T(8,128)(2,1)S(1)} all-to-all(bf16[32,32,128]{2,1,0:T(8,128)(2,1)S(1)} %update.1), channel_id=1, replica_groups=mesh['z'=8,'core'=2,'yh'=4,'yl'=2,'x'=4] {'z','yh'}, dimensions={0} | all-to-all | bytes 524288 | tf_op jit(solution)/shard_map/all_to_all | solution.py:432
  99.4 4.8 %collective-permute-start = (bf16[8,4,32,128]{3,2,1,0:T(8,128)(2,1)S(1)}, bf16[8,4,32,128]{3,2,1,0:T(8,128)(2,1)S(1)}, u32[]{:S(2)}, u32[]{:S(2)}) collective-permute-start(bf16[8,4,32,128]{3,2,1,0:T(8,128)(2,1)S(1)} %bitcast.11), channel_id=1, source_target_pairs={{0,32},{32,0},{1,33},{33,1},{2,34},{34,2},{3,35},{35,3},{4,36},{36... | collective-permute-start | bytes 786440 | tf_op jit(solution)/shard_map/ppermute | solution.py:466
  104.2 1.1 collective-permute-done.other_ref
  105.3 0.0 copy-start.1
  105.3 0.8 project.1
  106.1 13.5 %all_to_all.41.parts_ref = bf16[8,160,256]{2,1,0:T(8,128)(2,1)S(1)} all-to-all(bf16[8,160,256]{2,1,0:T(8,128)(2,1)S(1)} %project.1), channel_id=1, replica_groups=mesh['z'=8,'core'=2,'yh'=4,'yl'=2,'x'=4] {'yl','x'}, dimensions={0} | all-to-all | bytes 1310720 | tf_op jit(solution)/shard_map/all_to_all | solution.py:432
  119.6 0.0 copy-done.1
  119.6 0.8 finish.1
  (1 shorter events, 0.0 us)
Async XLA Ops:
  0.6 63.0 %copy-start = (f32[128,128]{1,0:T(8,128)S(1)}, f32[128,128]{1,0:T(8,128)}, u32[]{:S(2)}) copy-start(f32[128,128]{1,0:T(8,128)} %constant.10.clone.table_ref) | copy-start | bytes 196612
  3.1 17.7 %all-to-all-start = ((bf16[8,80,1024]{2,1,0:T(8,128)(2,1)}), bf16[8,80,1024]{2,1,0:T(8,128)(2,1)S(1)}, u32[]{:S(2)}, u32[]{:S(2)}) async-start(bf16[8,80,1024]{2,1,0:T(8,128)(2,1)} %pack_rest.1), calls=%async_computation | async-start | bytes 2621440 | tf_op jit(solution)/shard_map/cond/branch_0_fun/all_to_all | solution.py:432
  99.4 5.9 %collective-permute-start = (bf16[8,4,32,128]{3,2,1,0:T(8,128)(2,1)S(1)}, bf16[8,4,32,128]{3,2,1,0:T(8,128)(2,1)S(1)}, u32[]{:S(2)}, u32[]{:S(2)}) collective-permute-start(bf16[8,4,32,128]{3,2,1,0:T(8,128)(2,1)S(1)} %bitcast.11), channel_id=1, source_target_pairs={{0,32},{32,0},{1,33},{33,1},{2,34},{34,2},{3,35},{35,3},{4,36},{36... | collective-permute-start | bytes 786440 | tf_op jit(solution)/shard_map/ppermute | solution.py:466
  105.3 14.3 %copy-start.1 = (f32[1,8,8192]{2,1,0:T(8,128)S(1)}, f32[1,8,8192]{2,1,0:T(8,128)}, u32[]{:S(2)}) copy-start(f32[1,8,8192]{2,1,0:T(8,128)} %param.11) | copy-start | bytes 786436

commit v8 on v7

--- a/solution.py
+++ b/solution.py
@@ -13,7 +13,7 @@
 DEV = ("yh", "yl", "x")
 MIB = 1024 * 1024
 ACROSS = (((1,), (1,)), ((), ()))
-LEAD = 32
+LEAD = 48
 SIDE = 16
 
 

time: 121 us -> 121 us (level)
  blocking collectives: 88.9 us -> 86.1 us
  waiting for transfers between devices: 11.4 us -> 14.2 us
    all_to_all x1, waiting for transfers between devices: 10.3 us -> 13.1 us  [exchange(): return lax.all_to_all(value, axes, 0, 0, tiled=True)]
    all_to_all x5, blocking collectives: 88.9 us -> 86.1 us  [exchange(): return lax.all_to_all(value, axes, 0, 0, tiled=True)]
where the time goes in v8:
time: 121 us
  blocking collectives  86.1 us (71%)
  waiting for transfers between devices  14.2 us (12%)
  starting transfers between devices  10.8 us (9%)
  Pallas kernels  8.82 us (7%)
    all_to_all x5, blocking collectives, exchange(): return lax.all_to_all(value, axes, 0, 0, tiled=True)  86.1 us
    all_to_all x1, waiting for transfers between devices, exchange(): return lax.all_to_all(value, axes, 0, 0, tiled=True)  13.1 us
    all_to_all x1, starting transfers between devices, exchange(): return lax.all_to_all(value, axes, 0, 0, tiled=True)  5.87 us
    ppermute x1, starting transfers between devices, shards(): other = lax.ppermute(mine, 'core', [(0, 1), (1, 0)])  4.97 us
    pallas_call x1, Pallas kernels, pack_rest(): pl.pallas_call(body, in_specs=[anywhere] * 5, out_specs=pl.BlockSpec(memo...  2.59 us
  transfers between devices with their start and end apart: 2, of which 2 were waited for; matrix products, arithmetic and copies ran while one was open for 0% of the time, Pallas kernels for 1%

profile of v8, /device:TPU:1, one launch (start us, length us, event | category | flops | bytes accessed | tf_op | source)
XLA Modules:
  0.0 120.7 jit_solution(7684088497796739986)
XLA Ops:
  0.6 0.0 copy-start
  0.6 62.2 %conditional.1 = (bf16[8,128,1024]{2,1,0:T(8,128)(2,1)}, bf16[4,64,1024]{2,1,0:T(8,128)(2,1)S(1)}, bf16[8,16,1024]{2,1,0:T(8,128)(2,1)S(1)}) conditional(s32[]{:T(128)} %convert_element_type.3, (bf16[128,8192]{1,0:T(8,128)(2,1)}, bf16[128,256]{1,0:T(8,128)(2,1)}, f32[8,8192]{1,0:T(8,128)}, bf16[8,8192]{1,0:T(8,128)(2,1)}, ...), branch_computations={%region_0.0_spmd, %region_1.0_spmd} | conditional | bytes 8388664 | solution.py:459
  0.7 2.6 %pack_rest.1 = bf16[8,96,1024]{2,1,0:T(8,128)(2,1)} custom-call(bf16[128,8192]{1,0:T(8,128)(2,1)} %get-tuple-element.20.tok_ref, bf16[128,256]{1,0:T(8,128)(2,1)} %get-tuple-element.21.cot_ref, f32[8,8192]{1,0:T(8,128)} %get-tuple-element.22.mom_ref, bf16[8,8192]{1,0:T(8,128)(2,1)} %get-tuple-element.23.weight_ref, s32[16,128,128]{2,1,0:T(8,128)} %get-tuple-element.24.kept_ref), custom_call_target="tpu_custom_call" | custom-call | tf_op jit(solution)/shard_map/cond/branch_0_fun/pack_rest/pallas_call | solution.py:185
  3.3 5.9 %all-to-all-start = ((bf16[8,96,1024]{2,1,0:T(8,128)(2,1)}), bf16[8,96,1024]{2,1,0:T(8,128)(2,1)S(1)}, u32[]{:S(2)}, u32[]{:S(2)}) async-start(bf16[8,96,1024]{2,1,0:T(8,128)(2,1)} %pack_rest.1), calls=%async_computation | async-start | bytes 3145728 | tf_op jit(solution)/shard_map/cond/branch_0_fun/all_to_all | solution.py:432
  9.1 1.5 %split_tokens.1.value_ref = bf16[8,80,1024]{2,1,0:T(8,128)(2,1)S(1)} custom-call(bf16[128,8192]{1,0:T(8,128)(2,1)} %get-tuple-element.20.tok_ref), custom_call_target="tpu_custom_call" | custom-call | tf_op jit(solution)/shard_map/cond/branch_0_fun/split_tokens/pallas_call | solution.py:133
  10.6 13.1 %all-to-all-done.before_ref.refs_1_ = bf16[8,96,1024]{2,1,0:T(8,128)(2,1)S(1)} async-done(((bf16[8,96,1024]{2,1,0:T(8,128)(2,1)}), bf16[8,96,1024]{2,1,0:T(8,128)(2,1)S(1)}, u32[]{:S(2)}, u32[]{:S(2)}) %all-to-all-start) | async-done | bytes 1572896 | tf_op jit(solution)/shard_map/cond/branch_0_fun/all_to_all | solution.py:432
  23.7 21.2 %all_to_all.35.refs_0_ = bf16[8,80,1024]{2,1,0:T(8,128)(2,1)S(1)} all-to-all(bf16[8,80,1024]{2,1,0:T(8,128)(2,1)S(1)} %follow.1), channel_id=1, replica_groups=mesh['z'=8,'core'=2,'yh'=4,'yl'=2,'x'=4] {'yl','x'}, dimensions={0} | all-to-all | bytes 2621440 | tf_op jit(solution)/shard_map/cond/branch_0_fun/all_to_all | solution.py:432
  44.8 1.4 %gradient.2 = (bf16[256,1024]{1,0:T(8,128)(2,1)S(1)}, bf16[8,128,1024]{2,1,0:T(8,128)(2,1)}, bf16[8,16,1024]{2,1,0:T(8,128)(2,1)S(1)}) custom-call(bf16[8,80,1024]{2,1,0:T(8,128)(2,1)S(1)} %all_to_all.35.refs_0_, bf16[8,96,1024]{2,1,0:T(8,128)(2,1)S(1)} %all-to-all-done.before_ref.refs_1_), custom_call_target="tpu_custom_call" | custom-call | tf_op jit(solution)/shard_map/cond/branch_0_fun/gradient/pallas_call | solution.py:257
  46.2 16.7 %all_to_all.36 = bf16[4,64,1024]{2,1,0:T(8,128)(2,1)S(1)} all-to-all(bf16[4,64,1024]{2,1,0:T(8,128)(2,1)S(1)} %bitcast.13), channel_id=1, replica_groups=mesh['z'=8,'core'=2,'yh'=4,'yl'=2,'x'=4] {'yh'}, dimensions={0} | all-to-all | bytes 1048576 | tf_op jit(solution)/shard_map/cond/branch_0_fun/all_to_all | solution.py:432
  62.9 0.0 copy-done
  62.9 1.7 %raise_and_pick.1 = (bf16[16,32,128]{2,1,0:T(8,128)(2,1)S(1)}, bf16[8,32,256]{2,1,0:T(8,128)(2,1)S(1)}, f32[32,128]{1,0:T(8,128)S(1)}, bf16[8,128,1024]{2,1,0:T(8,128)(2,1)S(1)}) custom-call(bf16[4,64,1024]{2,1,0:T(8,128)(2,1)S(1)} %get-tuple-element.47.terms_hbm, bf16[8,16,1024]{2,1,0:T(8,128)(2,1)S(1)} %get-tuple-element.48.side_hbm, ...), custom_call_target="tpu_custom_call" | custom-call | tf_op jit(solution)/shard_map/raise_and_pick/pallas_call | solution.py:333
  64.6 19.4 %all_to_all.39.sent_ref = bf16[16,32,128]{2,1,0:T(8,128)(2,1)S(1)} all-to-all(bf16[16,32,128]{2,1,0:T(8,128)(2,1)S(1)} %get-tuple-element.51), channel_id=1, replica_groups=mesh['z'=8,'core'=2,'yh'=4,'yl'=2,'x'=4] {'z','core'}, dimensions={0} | all-to-all | bytes 262144 | tf_op jit(solution)/shard_map/all_to_all | solution.py:432
  84.0 0.2 update.1
  84.2 15.4 %all_to_all.40 = bf16[32,32,128]{2,1,0:T(8,128)(2,1)S(1)} all-to-all(bf16[32,32,128]{2,1,0:T(8,128)(2,1)S(1)} %update.1), channel_id=1, replica_groups=mesh['z'=8,'core'=2,'yh'=4,'yl'=2,'x'=4] {'z','yh'}, dimensions={0} | all-to-all | bytes 524288 | tf_op jit(solution)/shard_map/all_to_all | solution.py:432
  99.5 5.0 %collective-permute-start = (bf16[8,4,32,128]{3,2,1,0:T(8,128)(2,1)S(1)}, bf16[8,4,32,128]{3,2,1,0:T(8,128)(2,1)S(1)}, u32[]{:S(2)}, u32[]{:S(2)}) collective-permute-start(bf16[8,4,32,128]{3,2,1,0:T(8,128)(2,1)S(1)} %bitcast.11), channel_id=1, source_target_pairs={{0,32},{32,0},{1,33},{33,1},{2,34},{34,2},{3,35},{35,3},{4,36},{36... | collective-permute-start | bytes 786440 | tf_op jit(solution)/shard_map/ppermute | solution.py:466
  104.5 1.1 collective-permute-done.other_ref
  105.6 0.0 copy-start.1
  105.6 0.8 project.1
  106.4 13.5 %all_to_all.41.parts_ref = bf16[8,160,256]{2,1,0:T(8,128)(2,1)S(1)} all-to-all(bf16[8,160,256]{2,1,0:T(8,128)(2,1)S(1)} %project.1), channel_id=1, replica_groups=mesh['z'=8,'core'=2,'yh'=4,'yl'=2,'x'=4] {'yl','x'}, dimensions={0} | all-to-all | bytes 1310720 | tf_op jit(solution)/shard_map/all_to_all | solution.py:432
  119.9 0.0 copy-done.1
  119.9 0.8 finish.1
  (1 shorter events, 0.0 us)
Async XLA Ops:
  0.6 62.2 %copy-start = (f32[128,128]{1,0:T(8,128)S(1)}, f32[128,128]{1,0:T(8,128)}, u32[]{:S(2)}) copy-start(f32[128,128]{1,0:T(8,128)} %constant.10.clone.table_ref) | copy-start | bytes 196612
  3.3 20.4 %all-to-all-start = ((bf16[8,96,1024]{2,1,0:T(8,128)(2,1)}), bf16[8,96,1024]{2,1,0:T(8,128)(2,1)S(1)}, u32[]{:S(2)}, u32[]{:S(2)}) async-start(bf16[8,96,1024]{2,1,0:T(8,128)(2,1)} %pack_rest.1), calls=%async_computation | async-start | bytes 3145728 | tf_op jit(solution)/shard_map/cond/branch_0_fun/all_to_all | solution.py:432
  99.5 6.1 %collective-permute-start = (bf16[8,4,32,128]{3,2,1,0:T(8,128)(2,1)S(1)}, bf16[8,4,32,128]{3,2,1,0:T(8,128)(2,1)S(1)}, u32[]{:S(2)}, u32[]{:S(2)}) collective-permute-start(bf16[8,4,32,128]{3,2,1,0:T(8,128)(2,1)S(1)} %bitcast.11), channel_id=1, source_target_pairs={{0,32},{32,0},{1,33},{33,1},{2,34},{34,2},{3,35},{35,3},{4,36},{36... | collective-permute-start | bytes 786440 | tf_op jit(solution)/shard_map/ppermute | solution.py:466
  105.6 14.3 %copy-start.1 = (f32[1,8,8192]{2,1,0:T(8,128)S(1)}, f32[1,8,8192]{2,1,0:T(8,128)}, u32[]{:S(2)}) copy-start(f32[1,8,8192]{2,1,0:T(8,128)} %param.11) | copy-start | bytes 786436

commit v9 on v8

--- a/solution.py
+++ b/solution.py
@@ -13,7 +13,7 @@
 DEV = ("yh", "yl", "x")
 MIB = 1024 * 1024
 ACROSS = (((1,), (1,)), ((), ()))
-LEAD = 48
+LEAD = 16
 SIDE = 16
 
 

time: 121 us -> 121 us (level)
  blocking collectives: 86.1 us -> 91.5 us
  waiting for transfers between devices: 14.2 us -> 8.95 us
    all_to_all x5, blocking collectives: 86.1 us -> 91.5 us  [exchange(): return lax.all_to_all(value, axes, 0, 0, tiled=True)]
    all_to_all x1, waiting for transfers between devices: 13.1 us -> 7.81 us  [exchange(): return lax.all_to_all(value, axes, 0, 0, tiled=True)]
where the time goes in v9:
time: 121 us; the launch traced here: 120 us
  blocking collectives  91.5 us (76%)
  starting transfers between devices  10.5 us (9%)
  waiting for transfers between devices  8.95 us (7%)
  Pallas kernels  8.68 us (7%)
    all_to_all x5, blocking collectives, exchange(): return lax.all_to_all(value, axes, 0, 0, tiled=True)  91.5 us
    all_to_all x1, waiting for transfers between devices, exchange(): return lax.all_to_all(value, axes, 0, 0, tiled=True)  7.81 us
    all_to_all x1, starting transfers between devices, exchange(): return lax.all_to_all(value, axes, 0, 0, tiled=True)  5.87 us
    ppermute x1, starting transfers between devices, shards(): other = lax.ppermute(mine, 'core', [(0, 1), (1, 0)])  4.64 us
  transfers between devices with their start and end apart: 2, of which 2 were waited for; matrix products, arithmetic and copies ran while one was open for 0% of the time, Pallas kernels for 1%

profile of v9, /device:TPU:1, one launch (start us, length us, event | category | flops | bytes accessed | tf_op | source)
XLA Modules:
  0.0 120.4 jit_solution(4592370416322564012)
XLA Ops:
  0.6 0.0 copy-start
  0.6 64.8 %conditional.1 = (bf16[8,128,1024]{2,1,0:T(8,128)(2,1)}, bf16[4,64,1024]{2,1,0:T(8,128)(2,1)S(1)}, bf16[8,16,1024]{2,1,0:T(8,128)(2,1)S(1)}) conditional(s32[]{:T(128)} %convert_element_type.3, (bf16[128,8192]{1,0:T(8,128)(2,1)}, bf16[128,256]{1,0:T(8,128)(2,1)}, f32[8,8192]{1,0:T(8,128)}, bf16[8,8192]{1,0:T(8,128)(2,1)}, ...), branch_computations={%region_0.0_spmd, %region_1.0_spmd} | conditional | bytes 7864376 | solution.py:459
  0.7 2.3 %pack_rest.1 = bf16[8,64,1024]{2,1,0:T(8,128)(2,1)} custom-call(bf16[128,8192]{1,0:T(8,128)(2,1)} %get-tuple-element.20.tok_ref, bf16[128,256]{1,0:T(8,128)(2,1)} %get-tuple-element.21.cot_ref, f32[8,8192]{1,0:T(8,128)} %get-tuple-element.22.mom_ref, bf16[8,8192]{1,0:T(8,128)(2,1)} %get-tuple-element.23.weight_ref, s32[16,128,128]{2,1,0:T(8,128)} %get-tuple-element.24.kept_ref), custom_call_target="tpu_custom_call" | custom-call | tf_op jit(solution)/shard_map/cond/branch_0_fun/pack_rest/pallas_call | solution.py:185
  3.0 5.9 %all-to-all-start = ((bf16[8,64,1024]{2,1,0:T(8,128)(2,1)}), bf16[8,64,1024]{2,1,0:T(8,128)(2,1)S(1)}, u32[]{:S(2)}, u32[]{:S(2)}) async-start(bf16[8,64,1024]{2,1,0:T(8,128)(2,1)} %pack_rest.1), calls=%async_computation | async-start | bytes 2097152 | tf_op jit(solution)/shard_map/cond/branch_0_fun/all_to_all | solution.py:432
  8.8 1.6 %split_tokens.1.value_ref = bf16[8,112,1024]{2,1,0:T(8,128)(2,1)S(1)} custom-call(bf16[128,8192]{1,0:T(8,128)(2,1)} %get-tuple-element.20.tok_ref), custom_call_target="tpu_custom_call" | custom-call | tf_op jit(solution)/shard_map/cond/branch_0_fun/split_tokens/pallas_call | solution.py:133
  10.5 7.8 %all-to-all-done.before_ref.refs_1_ = bf16[8,64,1024]{2,1,0:T(8,128)(2,1)S(1)} async-done(((bf16[8,64,1024]{2,1,0:T(8,128)(2,1)}), bf16[8,64,1024]{2,1,0:T(8,128)(2,1)S(1)}, u32[]{:S(2)}, u32[]{:S(2)}) %all-to-all-start) | async-done | bytes 1048608 | tf_op jit(solution)/shard_map/cond/branch_0_fun/all_to_all | solution.py:432
  18.3 27.0 %all_to_all.35.refs_0_ = bf16[8,112,1024]{2,1,0:T(8,128)(2,1)S(1)} all-to-all(bf16[8,112,1024]{2,1,0:T(8,128)(2,1)S(1)} %follow.1), channel_id=1, replica_groups=mesh['z'=8,'core'=2,'yh'=4,'yl'=2,'x'=4] {'yl','x'}, dimensions={0} | all-to-all | bytes 3670016 | tf_op jit(solution)/shard_map/cond/branch_0_fun/all_to_all | solution.py:432
  45.2 1.3 %gradient.2 = (bf16[256,1024]{1,0:T(8,128)(2,1)S(1)}, bf16[8,128,1024]{2,1,0:T(8,128)(2,1)}, bf16[8,16,1024]{2,1,0:T(8,128)(2,1)S(1)}) custom-call(bf16[8,112,1024]{2,1,0:T(8,128)(2,1)S(1)} %all_to_all.35.refs_0_, bf16[8,64,1024]{2,1,0:T(8,128)(2,1)S(1)} %all-to-all-done.before_ref.refs_1_), custom_call_target="tpu_custom_call" | custom-call | tf_op jit(solution)/shard_map/cond/branch_0_fun/gradient/pallas_call | solution.py:257
  46.6 18.8 %all_to_all.36 = bf16[4,64,1024]{2,1,0:T(8,128)(2,1)S(1)} all-to-all(bf16[4,64,1024]{2,1,0:T(8,128)(2,1)S(1)} %bitcast.13), channel_id=1, replica_groups=mesh['z'=8,'core'=2,'yh'=4,'yl'=2,'x'=4] {'yh'}, dimensions={0} | all-to-all | bytes 1048576 | tf_op jit(solution)/shard_map/cond/branch_0_fun/all_to_all | solution.py:432
  65.4 0.0 copy-done
  65.4 1.7 %raise_and_pick.1 = (bf16[16,32,128]{2,1,0:T(8,128)(2,1)S(1)}, bf16[8,32,256]{2,1,0:T(8,128)(2,1)S(1)}, f32[32,128]{1,0:T(8,128)S(1)}, bf16[8,128,1024]{2,1,0:T(8,128)(2,1)S(1)}) custom-call(bf16[4,64,1024]{2,1,0:T(8,128)(2,1)S(1)} %get-tuple-element.47.terms_hbm, bf16[8,16,1024]{2,1,0:T(8,128)(2,1)S(1)} %get-tuple-element.48.side_hbm, ...), custom_call_target="tpu_custom_call" | custom-call | tf_op jit(solution)/shard_map/raise_and_pick/pallas_call | solution.py:333
  67.1 16.9 %all_to_all.39.sent_ref = bf16[16,32,128]{2,1,0:T(8,128)(2,1)S(1)} all-to-all(bf16[16,32,128]{2,1,0:T(8,128)(2,1)S(1)} %get-tuple-element.51), channel_id=1, replica_groups=mesh['z'=8,'core'=2,'yh'=4,'yl'=2,'x'=4] {'z','core'}, dimensions={0} | all-to-all | bytes 262144 | tf_op jit(solution)/shard_map/all_to_all | solution.py:432
  84.0 0.2 update.1
  84.2 15.2 %all_to_all.40 = bf16[32,32,128]{2,1,0:T(8,128)(2,1)S(1)} all-to-all(bf16[32,32,128]{2,1,0:T(8,128)(2,1)S(1)} %update.1), channel_id=1, replica_groups=mesh['z'=8,'core'=2,'yh'=4,'yl'=2,'x'=4] {'z','yh'}, dimensions={0} | all-to-all | bytes 524288 | tf_op jit(solution)/shard_map/all_to_all | solution.py:432
  99.4 4.6 %collective-permute-start = (bf16[8,4,32,128]{3,2,1,0:T(8,128)(2,1)S(1)}, bf16[8,4,32,128]{3,2,1,0:T(8,128)(2,1)S(1)}, u32[]{:S(2)}, u32[]{:S(2)}) collective-permute-start(bf16[8,4,32,128]{3,2,1,0:T(8,128)(2,1)S(1)} %bitcast.11), channel_id=1, source_target_pairs={{0,32},{32,0},{1,33},{33,1},{2,34},{34,2},{3,35},{35,3},{4,36},{36... | collective-permute-start | bytes 786440 | tf_op jit(solution)/shard_map/ppermute | solution.py:466
  104.0 1.1 collective-permute-done.other_ref
  105.2 0.0 copy-start.1
  105.2 0.8 project.1
  105.9 13.7 %all_to_all.41.parts_ref = bf16[8,160,256]{2,1,0:T(8,128)(2,1)S(1)} all-to-all(bf16[8,160,256]{2,1,0:T(8,128)(2,1)S(1)} %project.1), channel_id=1, replica_groups=mesh['z'=8,'core'=2,'yh'=4,'yl'=2,'x'=4] {'yl','x'}, dimensions={0} | all-to-all | bytes 1310720 | tf_op jit(solution)/shard_map/all_to_all | solution.py:432
  119.6 0.0 copy-done.1
  119.6 0.8 finish.1
  (1 shorter events, 0.0 us)
Async XLA Ops:
  0.6 64.8 %copy-start = (f32[128,128]{1,0:T(8,128)S(1)}, f32[128,128]{1,0:T(8,128)}, u32[]{:S(2)}) copy-start(f32[128,128]{1,0:T(8,128)} %constant.10.clone.table_ref) | copy-start | bytes 196612
  3.0 15.3 %all-to-all-start = ((bf16[8,64,1024]{2,1,0:T(8,128)(2,1)}), bf16[8,64,1024]{2,1,0:T(8,128)(2,1)S(1)}, u32[]{:S(2)}, u32[]{:S(2)}) async-start(bf16[8,64,1024]{2,1,0:T(8,128)(2,1)} %pack_rest.1), calls=%async_computation | async-start | bytes 2097152 | tf_op jit(solution)/shard_map/cond/branch_0_fun/all_to_all | solution.py:432
  99.4 5.8 %collective-permute-start = (bf16[8,4,32,128]{3,2,1,0:T(8,128)(2,1)S(1)}, bf16[8,4,32,128]{3,2,1,0:T(8,128)(2,1)S(1)}, u32[]{:S(2)}, u32[]{:S(2)}) collective-permute-start(bf16[8,4,32,128]{3,2,1,0:T(8,128)(2,1)S(1)} %bitcast.11), channel_id=1, source_target_pairs={{0,32},{32,0},{1,33},{33,1},{2,34},{34,2},{3,35},{35,3},{4,36},{36... | collective-permute-start | bytes 786440 | tf_op jit(solution)/shard_map/ppermute | solution.py:466
  105.2 14.5 %copy-start.1 = (f32[1,8,8192]{2,1,0:T(8,128)S(1)}, f32[1,8,8192]{2,1,0:T(8,128)}, u32[]{:S(2)}) copy-start(f32[1,8,8192]{2,1,0:T(8,128)} %param.11) | copy-start | bytes 786436

commit v10 on v7

--- a/solution.py
+++ b/solution.py
@@ -368,7 +368,9 @@
 
 def project(tokens, mine, other, change):
     groups, tok, part = tokens.shape
-    tiles, nyh, share, _ = mine.shape
+    _, share, _ = mine.shape
+    tiles = part // 128
+    nyh = mine.shape[0] // tiles
     rows_all = 2 * nyh * share
     extra = change.shape[1]
 
@@ -378,8 +380,11 @@
         for t in range(tiles):
             bands = []
             for y in range(nyh):
-                a, b = mine_ref[t, y], other_ref[t, y]
-                bands += [jnp.where(first, a, b), jnp.where(first, b, a)]
+                at, other_at = t * nyh + y, y * tiles + t
+                bands += [
+                    jnp.where(first, mine_ref[at], other_ref[at]),
+                    jnp.where(first, other_ref[other_at], mine_ref[other_at]),
+                ]
             weight.append(jnp.concatenate(bands, axis=0))
         weight = jnp.concatenate(weight, axis=1)
         weight = weight.T
@@ -462,7 +467,12 @@
     sent, change, held, held_tokens = raise_and_pick(terms, side, held_tokens, table, sites, rows_all, nx)
 
     fresh = update(exchange(sent, SITE), held, table, nz * nyh)
-    mine = exchange(fresh, ("z", "yh")).reshape(nz, nyh, band // ncore, 128)
+    mine = lax.cond(
+        lax.axis_index("core") == 0,
+        lambda value: exchange(value, ("z", "yh")),
+        lambda value: exchange(value, ("yh", "z")),
+        fresh,
+    )
     other = lax.ppermute(mine, "core", [(0, 1), (1, 0)])
     scores, moment_new = finish(exchange(project(held_tokens, mine, other, change), GROUP), momentum[0], tok)
     return (scores[None], moment_new[None])

time: 121 us -> 121 us (level)
  no operation moved by 1% of the time
where the time goes in v10:
time: 121 us; the launch traced here: 120 us
  blocking collectives  89.1 us (74%)
  waiting for transfers between devices  11.4 us (9%)
  starting transfers between devices  10.4 us (9%)
  Pallas kernels  8.73 us (7%)
    all_to_all x5, blocking collectives, exchange(): return lax.all_to_all(value, axes, 0, 0, tiled=True)  89.1 us
    all_to_all x1, waiting for transfers between devices, exchange(): return lax.all_to_all(value, axes, 0, 0, tiled=True)  10.3 us
    all_to_all x1, starting transfers between devices, exchange(): return lax.all_to_all(value, axes, 0, 0, tiled=True)  5.87 us
    ppermute x1, starting transfers between devices, shards(): other = lax.ppermute(mine, 'core', [(0, 1), (1, 0)])  4.51 us
  transfers between devices with their start and end apart: 2, of which 2 were waited for; matrix products, arithmetic and copies ran while one was open for 0% of the time, Pallas kernels for 1%

profile of v10, /device:TPU:1, one launch (start us, length us, event | category | flops | bytes accessed | tf_op | source)
XLA Modules:
  0.0 120.3 jit_solution(5238941753123932349)
XLA Ops:
  0.6 0.0 copy-start
  0.6 63.0 %conditional.2 = (bf16[8,128,1024]{2,1,0:T(8,128)(2,1)}, bf16[4,64,1024]{2,1,0:T(8,128)(2,1)S(1)}, bf16[8,16,1024]{2,1,0:T(8,128)(2,1)S(1)}) conditional(s32[]{:T(128)} %convert_element_type.4, (bf16[128,8192]{1,0:T(8,128)(2,1)}, bf16[128,256]{1,0:T(8,128)(2,1)}, f32[8,8192]{1,0:T(8,128)}, bf16[8,8192]{1,0:T(8,128)(2,1)}, ...), branch_computations={%region_0.0_spmd, %region_1.0_spmd} | conditional | bytes 8126520 | solution.py:464
  0.7 2.4 %pack_rest.1 = bf16[8,80,1024]{2,1,0:T(8,128)(2,1)} custom-call(bf16[128,8192]{1,0:T(8,128)(2,1)} %get-tuple-element.25.tok_ref, bf16[128,256]{1,0:T(8,128)(2,1)} %get-tuple-element.26.cot_ref, f32[8,8192]{1,0:T(8,128)} %get-tuple-element.27.mom_ref, bf16[8,8192]{1,0:T(8,128)(2,1)} %get-tuple-element.28.weight_ref, s32[16,128,128]{2,1,0:T(8,128)} %get-tuple-element.29.kept_ref), custom_call_target="tpu_custom_call" | custom-call | tf_op jit(solution)/shard_map/cond/branch_0_fun/pack_rest/pallas_call | solution.py:185
  3.1 5.9 %all-to-all-start = ((bf16[8,80,1024]{2,1,0:T(8,128)(2,1)}), bf16[8,80,1024]{2,1,0:T(8,128)(2,1)S(1)}, u32[]{:S(2)}, u32[]{:S(2)}) async-start(bf16[8,80,1024]{2,1,0:T(8,128)(2,1)} %pack_rest.1), calls=%async_computation | async-start | bytes 2621440 | tf_op jit(solution)/shard_map/cond/branch_0_fun/all_to_all | solution.py:437
  8.9 1.5 %split_tokens.1.value_ref = bf16[8,96,1024]{2,1,0:T(8,128)(2,1)S(1)} custom-call(bf16[128,8192]{1,0:T(8,128)(2,1)} %get-tuple-element.25.tok_ref), custom_call_target="tpu_custom_call" | custom-call | tf_op jit(solution)/shard_map/cond/branch_0_fun/split_tokens/pallas_call | solution.py:133
  10.5 10.3 %all-to-all-done.before_ref.refs_1_ = bf16[8,80,1024]{2,1,0:T(8,128)(2,1)S(1)} async-done(((bf16[8,80,1024]{2,1,0:T(8,128)(2,1)}), bf16[8,80,1024]{2,1,0:T(8,128)(2,1)S(1)}, u32[]{:S(2)}, u32[]{:S(2)}) %all-to-all-start) | async-done | bytes 1310752 | tf_op jit(solution)/shard_map/cond/branch_0_fun/all_to_all | solution.py:437
  20.7 24.1 %all_to_all.38.refs_0_ = bf16[8,96,1024]{2,1,0:T(8,128)(2,1)S(1)} all-to-all(bf16[8,96,1024]{2,1,0:T(8,128)(2,1)S(1)} %follow.1), channel_id=1, replica_groups=mesh['z'=8,'core'=2,'yh'=4,'yl'=2,'x'=4] {'yl','x'}, dimensions={0} | all-to-all | bytes 3145728 | tf_op jit(solution)/shard_map/cond/branch_0_fun/all_to_all | solution.py:437
  44.8 1.4 %gradient.2 = (bf16[256,1024]{1,0:T(8,128)(2,1)S(1)}, bf16[8,128,1024]{2,1,0:T(8,128)(2,1)}, bf16[8,16,1024]{2,1,0:T(8,128)(2,1)S(1)}) custom-call(bf16[8,96,1024]{2,1,0:T(8,128)(2,1)S(1)} %all_to_all.38.refs_0_, bf16[8,80,1024]{2,1,0:T(8,128)(2,1)S(1)} %all-to-all-done.before_ref.refs_1_), custom_call_target="tpu_custom_call" | custom-call | tf_op jit(solution)/shard_map/cond/branch_0_fun/gradient/pallas_call | solution.py:257
  46.2 17.4 %all_to_all.39 = bf16[4,64,1024]{2,1,0:T(8,128)(2,1)S(1)} all-to-all(bf16[4,64,1024]{2,1,0:T(8,128)(2,1)S(1)} %bitcast.10), channel_id=1, replica_groups=mesh['z'=8,'core'=2,'yh'=4,'yl'=2,'x'=4] {'yh'}, dimensions={0} | all-to-all | bytes 1048576 | tf_op jit(solution)/shard_map/cond/branch_0_fun/all_to_all | solution.py:437
  63.7 0.0 copy-done
  63.7 1.7 %raise_and_pick.1 = (bf16[16,32,128]{2,1,0:T(8,128)(2,1)S(1)}, bf16[8,32,256]{2,1,0:T(8,128)(2,1)S(1)}, f32[32,128]{1,0:T(8,128)S(1)}, bf16[8,128,1024]{2,1,0:T(8,128)(2,1)S(1)}) custom-call(bf16[4,64,1024]{2,1,0:T(8,128)(2,1)S(1)} %get-tuple-element.52.terms_hbm, bf16[8,16,1024]{2,1,0:T(8,128)(2,1)S(1)} %get-tuple-element.53.side_hbm, ...), custom_call_target="tpu_custom_call" | custom-call | tf_op jit(solution)/shard_map/raise_and_pick/pallas_call | solution.py:333
  65.3 18.4 %all_to_all.44.sent_ref = bf16[16,32,128]{2,1,0:T(8,128)(2,1)S(1)} all-to-all(bf16[16,32,128]{2,1,0:T(8,128)(2,1)S(1)} %get-tuple-element.56), channel_id=1, replica_groups=mesh['z'=8,'core'=2,'yh'=4,'yl'=2,'x'=4] {'z','core'}, dimensions={0} | all-to-all | bytes 262144 | tf_op jit(solution)/shard_map/all_to_all | solution.py:437
  83.7 0.2 update.1
  83.9 15.7 %conditional.3 = (bf16[32,32,128]{2,1,0:T(8,128)(2,1)S(1)}) conditional(s32[]{:T(128)} %convert_element_type.4, bf16[32,32,128]{2,1,0:T(8,128)(2,1)S(1)} %update.1, bf16[32,32,128]{2,1,0:T(8,128)(2,1)S(1)} %update.1), branch_computations={%region_2.0_spmd, %region_3.0_spmd} | conditional | bytes 524296 | solution.py:470
  83.9 15.7 %all_to_all.42 = bf16[32,32,128]{2,1,0:T(8,128)(2,1)S(1)} all-to-all(bf16[32,32,128]{2,1,0:T(8,128)(2,1)S(1)} %param.2), channel_id=1, replica_groups=mesh['z'=8,'core'=2,'yh'=4,'yl'=2,'x'=4] {'yh','z'}, dimensions={0} | all-to-all | bytes 524288 | tf_op jit(solution)/shard_map/cond/branch_0_fun/all_to_all | solution.py:437
  99.6 4.5 %collective-permute-start = (bf16[32,32,128]{2,1,0:T(8,128)(2,1)S(1)}, bf16[32,32,128]{2,1,0:T(8,128)(2,1)S(1)}, u32[]{:S(2)}, u32[]{:S(2)}) collective-permute-start(bf16[32,32,128]{2,1,0:T(8,128)(2,1)S(1)} %get-tuple-element.67.mine_ref), channel_id=1, source_target_pairs={{0,32},{32,0},{1,33},{33,1},{2,34},{34,2},{3,35},{35,3},{4,36},{36... | collective-permute-start | bytes 786440 | tf_op jit(solution)/shard_map/ppermute | solution.py:476
  104.1 1.1 collective-permute-done.other_ref
  105.3 0.0 copy-start.1
  105.3 0.8 project.1
  106.0 13.5 %all_to_all.45.parts_ref = bf16[8,160,256]{2,1,0:T(8,128)(2,1)S(1)} all-to-all(bf16[8,160,256]{2,1,0:T(8,128)(2,1)S(1)} %project.1), channel_id=1, replica_groups=mesh['z'=8,'core'=2,'yh'=4,'yl'=2,'x'=4] {'yl','x'}, dimensions={0} | all-to-all | bytes 1310720 | tf_op jit(solution)/shard_map/all_to_all | solution.py:437
  119.5 0.0 copy-done.1
  119.5 0.8 finish.1
  (1 shorter events, 0.0 us)
Async XLA Ops:
  0.6 63.0 %copy-start = (f32[128,128]{1,0:T(8,128)S(1)}, f32[128,128]{1,0:T(8,128)}, u32[]{:S(2)}) copy-start(f32[128,128]{1,0:T(8,128)} %constant.10.clone.table_ref) | copy-start | bytes 196612
  3.1 17.7 %all-to-all-start = ((bf16[8,80,1024]{2,1,0:T(8,128)(2,1)}), bf16[8,80,1024]{2,1,0:T(8,128)(2,1)S(1)}, u32[]{:S(2)}, u32[]{:S(2)}) async-start(bf16[8,80,1024]{2,1,0:T(8,128)(2,1)} %pack_rest.1), calls=%async_computation | async-start | bytes 2621440 | tf_op jit(solution)/shard_map/cond/branch_0_fun/all_to_all | solution.py:437
  99.6 5.7 %collective-permute-start = (bf16[32,32,128]{2,1,0:T(8,128)(2,1)S(1)}, bf16[32,32,128]{2,1,0:T(8,128)(2,1)S(1)}, u32[]{:S(2)}, u32[]{:S(2)}) collective-permute-start(bf16[32,32,128]{2,1,0:T(8,128)(2,1)S(1)} %get-tuple-element.67.mine_ref), channel_id=1, source_target_pairs={{0,32},{32,0},{1,33},{33,1},{2,34},{34,2},{3,35},{35,3},{4,36},{36... | collective-permute-start | bytes 786440 | tf_op jit(solution)/shard_map/ppermute | solution.py:476
  105.3 14.3 %copy-start.1 = (f32[1,8,8192]{2,1,0:T(8,128)S(1)}, f32[1,8,8192]{2,1,0:T(8,128)}, u32[]{:S(2)}) copy-start(f32[1,8,8192]{2,1,0:T(8,128)} %param.13) | copy-start | bytes 786436
